TPU v7x, 256 devices: a whole 4x4x8 slice. The times are simulated.
256 devices in a mesh: ctx: 32 (over y, x, z_lo), ch: 8 (over z_hi, core).
Axes of the slice: x: 4, y: 4, z: 8 (z_hi: 4, z_lo: 2; z = z_hi * 2 + z_lo), core: 2. Of those that a mesh axis runs over, the one named last changes fastest.
Arguments:
- tokens: bfloat16 [65536, 1024], P('ctx', 'ch'), may hold values from -6 to 6
- w_in: bfloat16 [1024, 1024], P(None, 'ch'), may hold values from -0.1875 to 0.1875
- filters: float32 [65536, 24], P('ctx'), may hold values from -0.0234375 to 0.0234375
- w_filter: float32 [24, 1024], P(None, 'ch'), may hold values from -1.25 to 1.25
- w_out: bfloat16 [1024, 1024], P('ch'), may hold values from -0.1875 to 0.1875
Outputs:
- output: bfloat16 [65536, 1024], P('ctx', 'ch')
All inputs are finite; a program needn't handle non-finite values.
Results may differ from a plain program's by a relative error of at most 0.0049.
Values may be sent and summed in bfloat16 or wider, within the bound.
No kernel may reach another device: no remote copies, remote signals or barrier semaphores. Data moves between devices by JAX's collectives and lax.ppermute only.
A program may use at most 64 MiB of HBM per device.

v0:
```python
import math

import jax
import jax.numpy as jnp
from jax import lax
from jax.sharding import PartitionSpec as P

COLS = 256


highest_mode = lax.Precision.HIGHEST


def cos_sin_table(left_index, right_index, period):
    phases = left_index[:, None] * right_index[None, :] % period
    angles = 2.0 * math.pi / period * phases.astype(jnp.float32)
    return (jnp.cos(angles), jnp.sin(angles))


def local(tokens, w_in, filters, w_filter, w_out):
    row_count, chan_count = tokens.shape
    ctx_count = lax.axis_size("ctx")
    ctx_place = lax.axis_index("ctx")
    inner_len = COLS
    outer_dev = row_count // inner_len
    outer_len = outer_dev * ctx_count
    padded_len = 2 * outer_len
    total_len = padded_len * inner_len
    inner_dev = inner_len // ctx_count
    projected = jnp.dot(
        lax.all_gather(tokens, "ch", axis=1, tiled=True), w_in, preferred_element_type=jnp.float32
    )
    shaped = jnp.dot(filters, w_filter, precision=highest_mode)
    signal = jnp.concatenate([projected, shaped], axis=1)
    signal = signal.reshape(outer_dev, inner_len, signal.shape[1])
    outer_index = jnp.arange(outer_len, dtype=jnp.int32)
    padded_index = jnp.arange(padded_len, dtype=jnp.int32)
    inner_index = jnp.arange(inner_len, dtype=jnp.int32)
    local_inner = ctx_place * inner_dev + jnp.arange(inner_dev, dtype=jnp.int32)
    outer_cos, outer_sin = cos_sin_table(padded_index, outer_index, padded_len)
    twiddle_cos, twiddle_sin = cos_sin_table(padded_index, local_inner, total_len)
    twiddle_cos = twiddle_cos[:, :, None]
    twiddle_sin = twiddle_sin[:, :, None]
    inner_cos, inner_sin = cos_sin_table(inner_index, inner_index, inner_len)
    block_part = lax.all_to_all(signal, "ctx", split_axis=1, concat_axis=0, tiled=True)
    real_part = jnp.einsum("kn,nbc->kbc", outer_cos, block_part, precision=highest_mode)
    imag_part = -jnp.einsum("kn,nbc->kbc", outer_sin, block_part, precision=highest_mode)
    first_spectra = jnp.stack(
        [
            real_part * twiddle_cos + imag_part * twiddle_sin,
            imag_part * twiddle_cos - real_part * twiddle_sin,
        ]
    )

    def inner_product(table, values):
        return jnp.einsum("kn,fnc->fkc", table, values, precision=highest_mode)

    block_part = lax.all_to_all(first_spectra, "ctx", split_axis=1, concat_axis=2, tiled=True)
    real_in = block_part[0]
    imag_in = block_part[1]
    real_out = inner_product(inner_cos, real_in) + inner_product(inner_sin, imag_in)
    imag_out = inner_product(inner_cos, imag_in) - inner_product(inner_sin, real_in)
    spectra = jnp.stack([real_out, imag_out])
    signal_re = spectra[0, :, :, :chan_count]
    signal_im = spectra[1, :, :, :chan_count]
    kernel = spectra[:, :, :, chan_count:]
    product_re = signal_re * kernel[0] - signal_im * kernel[1]
    product_im = signal_re * kernel[1] + signal_im * kernel[0]
    back_re = inner_product(inner_cos, product_re) - inner_product(inner_sin, product_im)
    back_im = inner_product(inner_cos, product_im) + inner_product(inner_sin, product_re)
    halfway = jnp.stack([back_re, back_im])
    block_part = lax.all_to_all(halfway, "ctx", split_axis=2, concat_axis=1, tiled=True)
    real_in = block_part[0]
    imag_in = block_part[1]
    turned_re = real_in * twiddle_cos - imag_in * twiddle_sin
    turned_im = imag_in * twiddle_cos + real_in * twiddle_sin
    summed = jnp.einsum("kn,kbc->nbc", outer_cos, turned_re, precision=highest_mode)
    summed = summed - jnp.einsum("kn,kbc->nbc", outer_sin, turned_im, precision=highest_mode)
    positions = summed * (1.0 / total_len)
    conv = (
        lax.all_to_all(
            positions.astype(jnp.bfloat16), "ctx", split_axis=0, concat_axis=1, tiled=True
        )
        .astype(positions.dtype)
        .reshape(row_count, chan_count)
    )
    mixed = conv.astype(jnp.bfloat16)
    partial_terms = jnp.dot(mixed, w_out, preferred_element_type=jnp.float32)
    result = lax.psum_scatter(partial_terms, "ch", scatter_dimension=1, tiled=True)
    return result.astype(jnp.bfloat16)


def solution(mesh):
    placed = (P("ctx", "ch"), P(None, "ch"), P("ctx", None), P(None, "ch"), P("ch", None))
    return jax.shard_map(
        local, mesh=mesh, in_specs=placed, out_specs=P("ctx", "ch"), check_vma=False
    )
```

profile of v0, /device:TPU:2, one launch (start us, length us, event | category | flops | bytes accessed | tf_op | source)
XLA Modules:
  0.0 495.2 jit_solution(14305966484975328182)
XLA Ops:
  7.3 1.9 fusion.152
  9.2 59.8 %all-gather.2.cloned.1.call-done = bf16[2048,1024]{1,0:T(8,128)(2,1)} async-done(((bf16[2048,128]{1,0:T(8,128)(2,1)}), bf16[2048,1024]{1,0:T(8,128)(2,1)}) %all-gather.2.cloned.1.call-update) | async-done | bytes 4194320 | tf_op jit(solution)/shard_map/all_gather | solution.py:31
  69.1 3.7 fusion.151
  72.9 0.9 copy.92
  73.8 2.1 copy.60
  75.9 7.8 %all-to-all-start = ((f32[8,256,256]{2,0,1:T(8,128)}), f32[8,256,256]{2,0,1:T(8,128)S(1)}, u32[]{:S(2)}, u32[]{:S(2)}) async-start(f32[8,256,256]{2,0,1:T(8,128)} %copy.60), calls=%async_computation | async-start | bytes 4194304 | tf_op jit(solution)/shard_map/all_to_all | solution.py:45
  83.9 29.0 %all-to-all-done = f32[8,256,256]{2,0,1:T(8,128)S(1)} async-done(((f32[8,256,256]{2,0,1:T(8,128)}), f32[8,256,256]{2,0,1:T(8,128)S(1)}, u32[]{:S(2)}, u32[]{:S(2)}) %all-to-all-start) | async-done | bytes 2097184 | tf_op jit(solution)/shard_map/all_to_all | solution.py:45
  112.8 5.8 %fusion.26 = f32[512,8,256]{2,0,1:T(8,128)S(1)} fusion(f32[32,8,8,256]{3,1,2,0:T(8,128)S(1)} %bitcast.127), kind=kOutput, calls=%fused_computation.34 | convolution fusion | flops 3223060480 | bytes 6291456 | tf_op jit(solution)/shard_map/kn,nbc->kbc/dot_general | solution.py:47
  118.6 20.1 %add_bitcast_fusion.1 = (f32[1,512,8,256]{3,1,2,0:T(8,128)S(1)}, f32[1,512,8,256]{3,1,2,0:T(8,128)S(1)}) fusion(f32[512,8,256]{2,0,1:T(8,128)S(1)} %fusion.26, f32[512,8]{0,1:T(8,128)S(1)} %get-tuple-element.16, f32[512,8]{0,1:T(8,128)S(1)} %get-tuple-element.15, f32[32,8,8,256]{3,1,2,0:T(8,128)S(1)} %bitcast.128), kind=kOutput, calls=%fused_computation.14 | convolution fusion | flops 3230400512 | bytes 14712832 | tf_op jit(solution)/shard_map/kn,nbc->kbc/dot_general | solution.py:46
  139.4 4.9 copy.65
  144.3 100.0 %all_to_all.66 = f32[2,512,8,256]{3,2,0,1:T(8,128)S(1)} all-to-all(f32[2,512,8,256]{3,2,0,1:T(8,128)S(1)} %copy.65), channel_id=1, replica_groups=mesh['ctx'=32,'ch'=8] {'ctx'}, dimensions={1} | all-to-all | bytes 16777216 | tf_op jit(solution)/shard_map/all_to_all | solution.py:58
  244.9 1.0 fusion.145
  245.9 7.9 %fusion.2 = f32[16,256,256]{2,1,0:T(8,128)S(1)} fusion(f32[1,16,32,8,256]{4,3,1,2,0:T(8,128)S(1)} %get-tuple-element.10), kind=kOutput, calls=%fused_computation.4 | convolution fusion | flops 3222142976 | bytes 8388608 | tf_op jit(solution)/shard_map/kn,fnc->fkc/dot_general | solution.py:56
  253.9 8.4 %fusion = f32[16,256,256]{2,1,0:T(8,128)S(1)} fusion(f32[1,16,32,8,256]{4,3,1,2,0:T(8,128)S(1)} %get-tuple-element.10), kind=kOutput, calls=%fused_computation.2 | convolution fusion | flops 3222142976 | bytes 8388608 | tf_op jit(solution)/shard_map/kn,fnc->fkc/dot_general | solution.py:56
  262.2 8.3 %add_bitcast_fusion = f32[1,16,256,256]{2,3,1,0:T(8,128)S(1)} fusion(f32[16,256,256]{2,1,0:T(8,128)S(1)} %fusion.2, f32[1,16,32,8,256]{4,3,1,2,0:T(8,128)S(1)} %get-tuple-element.9), kind=kOutput, calls=%fused_computation.12 | convolution fusion | flops 3223191552 | bytes 12582912 | tf_op jit(solution)/shard_map/kn,fnc->fkc/dot_general | solution.py:56
  270.6 8.3 %subtract_bitcast_fusion = f32[1,16,256,256]{2,3,1,0:T(8,128)S(1)} fusion(f32[16,256,256]{2,1,0:T(8,128)S(1)} %fusion, f32[1,16,32,8,256]{4,3,1,2,0:T(8,128)S(1)} %get-tuple-element.9), kind=kOutput, calls=%fused_computation.11 | convolution fusion | flops 3223191552 | bytes 12582912 | tf_op jit(solution)/shard_map/kn,fnc->fkc/dot_general | solution.py:56
  279.5 2.8 fusion.20
  282.4 3.0 fusion.18
  285.4 2.9 subtract_bitcast_fusion.2
  288.3 2.9 add_bitcast_fusion.2
  291.2 2.3 pad_maximum_fusion.1
  293.5 5.5 %copy.73 = f32[2,16,256,128]{3,1,0,2:T(8,128)} copy(f32[2,16,256,128]{2,3,1,0:T(8,128)} %pad_maximum_fusion.1) | data formatting | bytes 8388608 | tf_op jit(solution)/shard_map/stack | solution.py:71
  299.0 5.9 %all-to-all-start.2 = ((f32[2,16,256,128]{3,1,0,2:T(8,128)}), f32[2,16,256,128]{3,1,0,2:T(8,128)}, u32[]{:S(2)}, u32[]{:S(2)}) async-start(f32[2,16,256,128]{3,1,0,2:T(8,128)} %copy.73), calls=%async_computation.2 | async-start | bytes 8388608 | tf_op jit(solution)/shard_map/all_to_all | solution.py:72
  305.5 50.5 %all-to-all-done.2 = f32[2,16,256,128]{3,1,0,2:T(8,128)} async-done(((f32[2,16,256,128]{3,1,0,2:T(8,128)}), f32[2,16,256,128]{3,1,0,2:T(8,128)}, u32[]{:S(2)}, u32[]{:S(2)}) %all-to-all-start.2) | async-done | bytes 4194336 | tf_op jit(solution)/shard_map/all_to_all | solution.py:72
  356.0 4.6 copy.134
  361.5 1.6 fusion.16
  363.2 3.9 fusion.30
  367.1 4.0 fusion.46
  371.5 15.3 %all_to_all.67 = bf16[256,8,128]{2,1,0:T(8,128)(2,1)S(1)} all-to-all(bf16[256,8,128]{2,1,0:T(8,128)(2,1)S(1)} %copy.81), channel_id=1, replica_groups=mesh['ctx'=32,'ch'=8] {'ctx'}, dimensions={0} | all-to-all | bytes 1048576 | tf_op jit(solution)/shard_map/all_to_all | solution.py:81
  386.8 4.5 fusion.153
  391.3 94.5 %reduce-scatter.2.cloned.1.call-done = f32[2048,128]{1,0:T(8,128)} async-done(((f32[2048,1024]{1,0:T(8,128)}), f32[2048,128]{1,0:T(8,128)}) %reduce-scatter.2.cloned.1.call-update) | async-done | bytes 1048592 | tf_op jit(solution)/shard_map/reduce_scatter | solution.py:89
  485.8 2.1 convert_element_type.49
  (19 shorter events, 5.0 us)
Async XLA Ops:
  6.5 380.3 %copy-start = (bf16[128,1024]{1,0:T(8,128)(2,1)S(1)}, bf16[128,1024]{1,0:T(8,128)(2,1)}, u32[]{:S(2)}) copy-start(bf16[128,1024]{1,0:T(8,128)(2,1)} %param.9) | copy-start | bytes 786436
  6.5 62.5 %all-gather.2.cloned.1.call-start = ((), (), s32[]{:S(2)}) async-start(), calls=%async_computation.5 | async-start | bytes 4718592 | tf_op jit(solution)/shard_map/all_gather | solution.py:31
  75.9 36.9 %all-to-all-start = ((f32[8,256,256]{2,0,1:T(8,128)}), f32[8,256,256]{2,0,1:T(8,128)S(1)}, u32[]{:S(2)}, u32[]{:S(2)}) async-start(f32[8,256,256]{2,0,1:T(8,128)} %copy.60), calls=%async_computation | async-start | bytes 4194304 | tf_op jit(solution)/shard_map/all_to_all | solution.py:45
  299.0 57.0 %all-to-all-start.2 = ((f32[2,16,256,128]{3,1,0,2:T(8,128)}), f32[2,16,256,128]{3,1,0,2:T(8,128)}, u32[]{:S(2)}, u32[]{:S(2)}) async-start(f32[2,16,256,128]{3,1,0,2:T(8,128)} %copy.73), calls=%async_computation.2 | async-start | bytes 8388608 | tf_op jit(solution)/shard_map/all_to_all | solution.py:72
  304.9 180.9 %reduce-scatter.2.cloned.1.call-start = ((), (), s32[]{:S(2)}) async-start(), calls=%async_computation.6 | async-start | bytes 9437184 | tf_op jit(solution)/shard_map/reduce_scatter | solution.py:89
Sparse Core Ops, SparseCore 0:
  9.2 59.8 all-gather.1
  391.4 94.3 reduce-scatter.1
where the time goes:
time: 500 us; the launch traced here: 495 us
  waiting for transfers between devices  235 us (47%)
  blocking collectives  115 us (23%)
  matrix products  88.4 us (18%)
  local copies, waits for them, and re-layouts  21.2 us (4%)
  between operations  14.1 us (3%)
  starting transfers between devices  14 us (3%)
  other arithmetic  7.71 us (2%)
    all_to_all x1, blocking collectives, local(): lax.all_to_all(first_spectra, 'ctx', split_axis=1, concat_axis=2, tiled=T...  100 us
    reduce_scatter x1, waiting for transfers between devices, local(): lax.psum_scatter(partial_terms, 'ch', scatter_dimension=1, tiled=True)  94.5 us
    all_gather x1, waiting for transfers between devices, local(): lax.all_gather(tokens, 'ch', axis=1, tiled=True)  59.8 us
    all_to_all x1, waiting for transfers between devices, local(): lax.all_to_all(halfway, 'ctx', split_axis=2, concat_axis=1, tiled=True)  50.5 us
    dot_general x8, matrix products, inner_product(): return jnp.einsum('kn,fnc->fkc', table, values, precision=highest_mode)  44.5 us
    all_to_all x1, waiting for transfers between devices, local(): lax.all_to_all(signal, 'ctx', split_axis=1, concat_axis=0, tiled=True)  29 us
    dot_general x1, matrix products, local(): jnp.einsum('kn,nbc->kbc', outer_cos, block_part, precision=highest_mode)  20.1 us
    all_to_all x1, blocking collectives, local(): lax.all_to_all(positions.astype(jnp.bfloat16), 'ctx', split_axis=0, conca...  15.3 us
  transfers between devices with their start and end apart: 4, of which 4 were waited for; matrix products, arithmetic and copies ran while one was open for 0% of the time, Pallas kernels for 0%

commit v1 on v0

v1 whole, which is shorter than its diff:
```python
import math

import jax
import jax.numpy as jnp
import ml_dtypes
import numpy as np
from jax import lax
from jax.experimental import pallas as pl
from jax.experimental.pallas import tpu as pltpu
from jax.sharding import PartitionSpec as P


BF = jnp.bfloat16
F32 = jnp.float32
NB = 256
LANES = 128
VMEM_LIMIT = 56 * 1024 * 1024


def split_np(table):
    table = table.astype(np.float32)
    high = table.astype(ml_dtypes.bfloat16)
    low = (table - high.astype(np.float32)).astype(ml_dtypes.bfloat16)
    return high, low


def tables(ctx_count, ch_count):
    k = np.arange(NB, dtype=np.int64)
    arrive = (np.arange(ctx_count)[None, :] * ch_count + np.arange(ch_count)[:, None]).reshape(-1)
    angle = 2.0 * math.pi / (4 * NB) * (((1 + 4 * k)[:, None] * k[None, :]) % (4 * NB))
    outer = np.concatenate([np.cos(angle), np.sin(angle)], axis=0)
    outer_x = outer[:, arrive]
    back = outer_x.T / (NB * NB)
    angle = 2.0 * math.pi / (4 * NB * NB) * (((1 + 4 * k)[:, None] * k[None, :]) % (4 * NB * NB))
    turn = np.stack([np.cos(angle), np.sin(angle)]).astype(np.float32)
    angle = 2.0 * math.pi / NB * ((k[:, None] * k[None, :]) % NB)
    cos, sin = np.cos(angle), np.sin(angle)
    inner = np.block([[cos, sin], [-sin, cos]])
    inner_back = np.block([[cos, -sin], [sin, cos]])
    return (
        np.stack(split_np(outer)),
        np.stack(split_np(outer_x)),
        np.stack(split_np(inner)),
        np.stack(split_np(inner_back)),
        np.stack(split_np(back)),
        turn,
    )


def dot(a, b, dims=((1,), (0,))):
    return lax.dot_general(a, b, (dims, ((), ())), preferred_element_type=F32)


def split(x):
    high = x.astype(BF)
    return high, (x - high.astype(F32)).astype(BF)


def shape_kernel(filters_ref, w_ref, out_ref, wide_ref):
    fh, fl = split(filters_ref[...])
    wh, wl = split(w_ref[...])
    dims = ((0,), (1,))
    shaped = dot(wh, fh, dims) + (dot(wl, fh, dims) + dot(wh, fl, dims))
    rows = wide_ref.shape[0] // 32
    for block in range(shaped.shape[1] // LANES):
        m, half = divmod(block, 2)
        for c in range(4):
            wide_ref[pl.ds(m * 8 + c * 2 + half, 32, stride=rows), :] = shaped[
                32 * c : 32 * (c + 1), block * LANES : (block + 1) * LANES
            ]
    out_ref[...] = wide_ref[...].astype(out_ref.dtype)


def project_kernel(tokens_ref, w_ref, out_ref, wide_ref):
    count = tokens_ref.shape[0] // NB
    tokens = jnp.concatenate([tokens_ref[pl.ds(NB * j, NB), :] for j in range(count)], axis=1)
    for j in range(count):
        part = dot(w_ref[pl.ds(LANES * j, LANES), :], tokens, ((1,), (1,)))
        for c in range(4):
            for half in range(2):
                wide_ref[pl.ds(j * 256 + c * 2 + half, 32, stride=8), :] = part[
                    32 * c : 32 * (c + 1), half * LANES : (half + 1) * LANES
                ]
    out_ref[...] = wide_ref[...].astype(out_ref.dtype)


def forward(wide_ref, outer_ref, inner_ref, turn_ref, c):
    x = jnp.concatenate(
        [wide_ref[pl.ds(c * 2 + half, NB, stride=8), :] for half in range(2)], axis=1
    ).astype(BF)
    first = dot(outer_ref[0], x) + dot(outer_ref[1], x)
    re, im = first[:NB], first[NB:]
    cos, sin = turn_ref[0], turn_ref[1]
    turned = jnp.concatenate([re * cos - im * sin, re * sin + im * cos], axis=1)
    high, low = split(turned)
    return dot(high, inner_ref[0]) + (dot(low, inner_ref[0]) + dot(high, inner_ref[1]))


def filter_kernel(h_ref, outer_ref, inner_ref, turn_ref, out_ref, wide_ref):
    wide_ref[...] = h_ref[...].astype(F32)
    for c in range(4):
        out_ref[c] = forward(wide_ref, outer_ref, inner_ref, turn_ref, c)


def conv_kernel(
    x_ref, spec_ref, outer_ref, inner_ref, inner_back_ref, back_ref, turn_ref, out_ref, wide_ref
):
    wide_ref[...] = x_ref[...].astype(F32)
    cos, sin = turn_ref[0], turn_ref[1]
    for c in range(4):
        got = forward(wide_ref, outer_ref, inner_ref, turn_ref, c)
        re, im = got[:, :NB], got[:, NB:]
        hre, him = spec_ref[c, :, :NB], spec_ref[c, :, NB:]
        high, low = split(jnp.concatenate([re * hre - im * him, re * him + im * hre], axis=1))
        half = dot(high, inner_back_ref[0]) + (
            dot(low, inner_back_ref[0]) + dot(high, inner_back_ref[1])
        )
        re, im = half[:, :NB], half[:, NB:]
        high, low = split(jnp.concatenate([re * cos + im * sin, im * cos - re * sin], axis=0))
        y = dot(back_ref[0], high) + (dot(back_ref[0], low) + dot(back_ref[1], high))
        for part in range(2):
            wide_ref[pl.ds(c * 2 + part, NB, stride=8), :] = y[
                :, part * LANES : (part + 1) * LANES
            ]
    out_ref[...] = wide_ref[...].astype(out_ref.dtype)


def output_kernel(mixed_ref, w_ref, out_ref, wide_ref):
    wide_ref[...] = mixed_ref[...].astype(F32)
    count = out_ref.shape[0] // NB
    rows = []
    for j in range(count):
        for c in range(4):
            rows.append(
                jnp.concatenate(
                    [
                        wide_ref[pl.ds(j * 256 + c * 2 + half, 32, stride=8), :]
                        for half in range(2)
                    ],
                    axis=1,
                )
            )
    mixed = jnp.concatenate(rows, axis=0).astype(BF)
    result = dot(mixed, w_ref[...], ((0,), (0,))).astype(out_ref.dtype)
    for j in range(count):
        out_ref[pl.ds(NB * j, NB), :] = result[:, j * LANES : (j + 1) * LANES]


def call(kernel, shape, dtype, wide, flops, *args):
    size = sum(a.size * a.dtype.itemsize for a in args) + math.prod(shape) * 4
    return pl.pallas_call(
        kernel,
        out_shape=jax.ShapeDtypeStruct(shape, dtype),
        scratch_shapes=[pltpu.VMEM(wide, F32)],
        compiler_params=pltpu.CompilerParams(vmem_limit_bytes=VMEM_LIMIT),
        cost_estimate=pl.CostEstimate(flops=flops, bytes_accessed=size, transcendentals=0),
    )(*args)


def local(tokens, w_in, filters, w_filter, w_out):
    ctx_count, ch_count = lax.axis_size("ctx"), lax.axis_size("ch")
    every = ("ch", "ctx")
    outer, outer_x, inner, inner_back, back, turn = tables(ctx_count, ch_count)
    wide = tokens.shape
    w_in = lax.all_gather(w_in.T, "ch", axis=0, tiled=True)
    w_out = lax.all_gather(w_out, "ch", axis=0, tiled=True)
    tokens = lax.all_to_all(tokens, "ch", 0, 0, tiled=True)
    shaped = call(shape_kernel, wide, BF, wide, 2**25, filters, w_filter)
    shaped = lax.all_to_all(shaped, "ctx", 0, 0, tiled=True)
    spectrum = call(
        filter_kernel, (4, NB, 2 * NB), F32, wide, 2**31, shaped, outer, inner, turn
    )
    signal = call(project_kernel, wide, BF, wide, 2**29, tokens, w_in)
    signal = lax.all_to_all(signal, every, 0, 0, tiled=True)
    mixed = call(
        conv_kernel, wide, BF, wide, 2**32, signal, spectrum, outer_x, inner, inner_back, back, turn
    )
    mixed = lax.all_to_all(mixed, every, 0, 0, tiled=True)
    result = call(output_kernel, wide, BF, wide, 2**29, mixed, w_out)
    return lax.all_to_all(result, "ch", 0, 0, tiled=True)


def solution(mesh):
    placed = (P("ctx", "ch"), P(None, "ch"), P("ctx", None), P(None, "ch"), P("ch", None))
    return jax.shard_map(
        local, mesh=mesh, in_specs=placed, out_specs=P("ctx", "ch"), check_vma=False
    )
```

time: 500 us -> 173 us (0.35)
  waiting for transfers between devices: 235 us -> 68.2 us
  blocking collectives: 115 us -> 21.1 us
  matrix products: 88.4 us -> 0 us
  Pallas kernels: 0 us -> 27.6 us
  starting transfers between devices: 14 us -> 35.5 us
  local copies, waits for them, and re-layouts: 21.2 us -> 5.55 us
  other arithmetic: 7.71 us -> 0 us
    reduce_scatter x1 -> x0, waiting for transfers between devices: 94.5 us -> none  [local(): lax.psum_scatter(partial_terms, 'ch', scatter_dimension=1, tiled=True)]
    all_to_all x2 -> x1, blocking collectives: 115 us -> 21.1 us  [local(): return lax.all_to_all(result, 'ch', 0, 0, tiled=True)]
    dot_general x15 -> x0, matrix products: 88.4 us -> none  [the longest x8 44.5 us: inner_product(): return jnp.einsum('kn,fnc->fkc', table, values, precision=highest_mode)]
    all_gather x1 -> x2, waiting for transfers between devices: 59.8 us -> 7.97 us  [the longest x1 7.95 us: local(): w_in = lax.all_gather(w_in.T, 'ch', axis=0, tiled=True)]
    pallas_call x0 -> x5, Pallas kernels: none -> 27.6 us  [call(): pl.pallas_call(kernel, out_shape=jax.ShapeDtypeStruct(shape, dtype), scra...]
    all_to_all x2 -> x4, starting transfers between devices: 13.7 us -> 35.4 us  [the longest x1 10 us: local(): shaped = lax.all_to_all(shaped, 'ctx', 0, 0, tiled=True)]
    all_to_all x2 -> x4, waiting for transfers between devices: 79.5 us -> 59.6 us  [the longest x1 23.3 us: local(): signal = lax.all_to_all(signal, every, 0, 0, tiled=True)]
    another operation x2 -> x0, local copies, waits for them, and re-layouts: 10.3 us -> none  [the longest x1 5.48 us: local(): halfway = jnp.stack([back_re, back_im])]
  transfers between devices with their start and end apart: 4 -> 6, of which waited for: 4 -> 5; matrix products, arithmetic and copies ran while one was open for 0% -> 1% of each run, Pallas kernels for 0% -> 14%
where the time goes in v1:
time: 173 us; the launch traced here: 171 us
  waiting for transfers between devices  68.2 us (39%)
  starting transfers between devices  35.5 us (21%)
  Pallas kernels  27.6 us (16%)
  blocking collectives  21.1 us (12%)
  between operations  13.5 us (8%)
  local copies, waits for them, and re-layouts  5.55 us (3%)
    pallas_call x5, Pallas kernels, call(): pl.pallas_call(kernel, out_shape=jax.ShapeDtypeStruct(shape, dtype), scra...  27.6 us
    all_to_all x1, waiting for transfers between devices, local(): signal = lax.all_to_all(signal, every, 0, 0, tiled=True)  23.3 us
    all_to_all x1, blocking collectives, local(): return lax.all_to_all(result, 'ch', 0, 0, tiled=True)  21.1 us
    all_to_all x1, waiting for transfers between devices, local(): mixed = lax.all_to_all(mixed, every, 0, 0, tiled=True)  20.1 us
    all_to_all x1, waiting for transfers between devices, local(): tokens = lax.all_to_all(tokens, 'ch', 0, 0, tiled=True)  14.6 us
    all_to_all x1, starting transfers between devices, local(): shaped = lax.all_to_all(shaped, 'ctx', 0, 0, tiled=True)  10 us
    all_to_all x1, starting transfers between devices, local(): signal = lax.all_to_all(signal, every, 0, 0, tiled=True)  9.69 us
    all_to_all x1, starting transfers between devices, local(): tokens = lax.all_to_all(tokens, 'ch', 0, 0, tiled=True)  8.48 us
  transfers between devices with their start and end apart: 6, of which 5 were waited for; matrix products, arithmetic and copies ran while one was open for 1% of the time, Pallas kernels for 14%

profile of v1, /device:TPU:2, one launch (start us, length us, event | category | flops | bytes accessed | tf_op | source)
XLA Modules:
  0.0 171.5 jit_solution(9432245669245420563)
XLA Ops:
  6.5 0.0 copy-start.4
  6.5 0.0 all-gather.3.cloned.1.call-start
  6.5 1.8 %copy.12 = bf16[1024,128]{0,1:T(8,128)(2,1)} copy(bf16[1024,128]{1,0:T(8,128)(2,1)} %param.12) | data formatting | bytes 524288 | tf_op args[1]
  8.4 0.0 all-gather.3.cloned.1.call-update
  8.4 8.5 %all-to-all-start = ((bf16[8,256,128]{2,1,0:T(8,128)(2,1)}), bf16[8,256,128]{2,1,0:T(8,128)(2,1)S(1)}, u32[]{:S(2)}, u32[]{:S(2)}) async-start(bf16[8,256,128]{2,1,0:T(8,128)(2,1)} %bitcast.18), calls=%async_computation | async-start | bytes 1048576 | tf_op jit(solution)/shard_map/all_to_all | solution.py:167
  16.9 0.0 all-gather.5.cloned.1.call-start
  16.9 0.7 all-gather.5.cloned.1.call-update
  17.6 0.0 copy-done.4
  17.6 1.3 copy.13.filters_ref
  19.0 3.2 %shard_map.110 = bf16[2048,128]{1,0:T(8,128)(2,1)} custom-call(f32[2048,24]{1,0:T(8,128)} %copy.13.filters_ref, f32[24,128]{1,0:T(8,128)} %w_ref.1), custom_call_target="tpu_custom_call" | custom-call | flops 33554432 | bytes 1257472 | tf_op jit(solution)/shard_map/pallas_call | solution.py:151
  22.2 14.6 %all-to-all-done = bf16[8,256,128]{2,1,0:T(8,128)(2,1)S(1)} async-done(((bf16[8,256,128]{2,1,0:T(8,128)(2,1)}), bf16[8,256,128]{2,1,0:T(8,128)(2,1)S(1)}, u32[]{:S(2)}, u32[]{:S(2)}) %all-to-all-start) | async-done | bytes 524320 | tf_op jit(solution)/shard_map/all_to_all | solution.py:167
  36.8 0.0 copy-start
  36.8 10.0 %all-to-all-start.2 = ((bf16[32,64,128]{2,1,0:T(8,128)(2,1)}), bf16[32,64,128]{2,1,0:T(8,128)(2,1)S(1)}, u32[]{:S(2)}, u32[]{:S(2)}) async-start(bf16[32,64,128]{2,1,0:T(8,128)(2,1)} %bitcast.11), calls=%async_computation.2 | async-start | bytes 1048576 | tf_op jit(solution)/shard_map/all_to_all | solution.py:169
  46.8 7.9 %all-gather.3.cloned.1.call-done.w_ref = bf16[1024,1024]{1,0:T(8,128)(2,1)} async-done(((bf16[128,1024]{1,0:T(8,128)(2,1)}), bf16[1024,1024]{1,0:T(8,128)(2,1)}) %all-gather.3.cloned.1.call-update) | async-done | bytes 2097168 | tf_op jit(solution)/shard_map/all_gather | solution.py:165
  54.8 0.0 copy-done
  54.8 4.1 %shard_map.109 = bf16[2048,128]{1,0:T(8,128)(2,1)} custom-call(bf16[2048,128]{1,0:T(8,128)(2,1)} %bitcast.13, bf16[1024,1024]{1,0:T(8,128)(2,1)} %all-gather.3.cloned.1.call-done.w_ref), custom_call_target="tpu_custom_call" | custom-call | flops 536870912 | bytes 3670016 | tf_op jit(solution)/shard_map/pallas_call | solution.py:151
  58.9 1.5 all-to-all-done.2
  60.4 0.0 copy-start.2
  60.4 9.7 %all-to-all-start.1 = ((bf16[256,8,128]{2,1,0:T(8,128)(2,1)}), bf16[256,8,128]{2,1,0:T(8,128)(2,1)S(1)}, u32[]{:S(2)}, u32[]{:S(2)}) async-start(bf16[256,8,128]{2,1,0:T(8,128)(2,1)} %bitcast.14), calls=%async_computation.1 | async-start | bytes 1048576 | tf_op jit(solution)/shard_map/all_to_all | solution.py:174
  70.1 0.0 copy-done.2
  70.1 5.8 %shard_map.111.spec_ref = f32[4,256,512]{2,1,0:T(8,128)} custom-call(bf16[2048,128]{1,0:T(8,128)(2,1)} %bitcast.19, bf16[2,512,256]{2,1,0:T(8,128)(2,1)} %constant.12.clone.outer_ref, bf16[2,512,512]{2,1,0:T(8,128)(2,1)} %constant.13.clone.inner_ref, f32[2,256,256]{2,1,0:T(8,128)} %constant.14.clone.turn_ref), custom_call_target="tpu_custom_call" | custom-call | flops 2147483648 | bytes 4718592 | tf_op jit(solution)/shard_map/pallas_call | solution.py:151
  75.9 23.3 %all-to-all-done.1 = bf16[256,8,128]{2,1,0:T(8,128)(2,1)S(1)} async-done(((bf16[256,8,128]{2,1,0:T(8,128)(2,1)}), bf16[256,8,128]{2,1,0:T(8,128)(2,1)S(1)}, u32[]{:S(2)}, u32[]{:S(2)}) %all-to-all-start.1) | async-done | bytes 524320 | tf_op jit(solution)/shard_map/all_to_all | solution.py:174
  99.3 0.0 copy-start.3
  99.3 0.8 copy-done.3
  100.0 11.1 %shard_map.112 = bf16[2048,128]{1,0:T(8,128)(2,1)} custom-call(bf16[2048,128]{1,0:T(8,128)(2,1)} %bitcast.20, f32[4,256,512]{2,1,0:T(8,128)} %shard_map.111.spec_ref, bf16[2,512,256]{2,1,0:T(8,128)(2,1)} %constant.15.clone.outer_ref, bf16[2,512,512]{2,1,0:T(8,128)(2,1)} %constant.13.clone.inner_ref, bf16[2,512,512]{2,1,0:T(8,128)(2,1)} %constant.16.clone.inner_back_ref, ...), custom_call_target="tpu_custom_call" | custom-call | flops 4294967296 | bytes 7340032 | tf_op jit(solution)/shard_map/pallas_call | solution.py:151
  111.1 7.2 %all-to-all-start.3 = ((bf16[256,8,128]{2,1,0:T(8,128)(2,1)}), bf16[256,8,128]{2,1,0:T(8,128)(2,1)S(1)}, u32[]{:S(2)}, u32[]{:S(2)}) async-start(bf16[256,8,128]{2,1,0:T(8,128)(2,1)} %bitcast.21), calls=%async_computation.3 | async-start | bytes 1048576 | tf_op jit(solution)/shard_map/all_to_all | solution.py:178
  118.4 0.0 all-gather.5.cloned.1.call-done.w_ref
  118.4 20.1 %all-to-all-done.3 = bf16[256,8,128]{2,1,0:T(8,128)(2,1)S(1)} async-done(((bf16[256,8,128]{2,1,0:T(8,128)(2,1)}), bf16[256,8,128]{2,1,0:T(8,128)(2,1)S(1)}, u32[]{:S(2)}, u32[]{:S(2)}) %all-to-all-start.3) | async-done | bytes 524320 | tf_op jit(solution)/shard_map/all_to_all | solution.py:178
  138.5 0.8 copy-done.1
  139.3 3.4 %shard_map.113 = bf16[2048,128]{1,0:T(8,128)(2,1)} custom-call(bf16[2048,128]{1,0:T(8,128)(2,1)} %bitcast.15, bf16[1024,1024]{1,0:T(8,128)(2,1)} %all-gather.5.cloned.1.call-done.w_ref), custom_call_target="tpu_custom_call" | custom-call | flops 536870912 | bytes 3670016 | tf_op jit(solution)/shard_map/pallas_call | solution.py:151
  142.7 21.1 %all_to_all.56 = bf16[8,256,128]{2,1,0:T(8,128)(2,1)S(1)} all-to-all(bf16[8,256,128]{2,1,0:T(8,128)(2,1)} %bitcast.16), channel_id=1, replica_groups=mesh['ctx'=32,'ch'=8] {'ch'}, dimensions={0} | all-to-all | bytes 1048576 | tf_op jit(solution)/shard_map/all_to_all | solution.py:180
  163.9 0.8 copy.15
  (1 shorter events, 0.0 us)
Async XLA Ops:
  6.5 11.1 %copy-start.4 = (f32[2048,24]{0,1:T(8,128)S(1)}, f32[2048,24]{0,1:T(8,128)}, u32[]{:S(2)}) copy-start(f32[2048,24]{0,1:T(8,128)} %param.13) | copy-start | bytes 589828
  6.5 48.3 %all-gather.3.cloned.1.call-start = ((), (), s32[]{:S(2)}) async-start(), calls=%async_computation.5 | async-start | bytes 2359296 | tf_op jit(solution)/shard_map/all_gather | solution.py:165
  8.4 28.4 %all-to-all-start = ((bf16[8,256,128]{2,1,0:T(8,128)(2,1)}), bf16[8,256,128]{2,1,0:T(8,128)(2,1)S(1)}, u32[]{:S(2)}, u32[]{:S(2)}) async-start(bf16[8,256,128]{2,1,0:T(8,128)(2,1)} %bitcast.18), calls=%async_computation | async-start | bytes 1048576 | tf_op jit(solution)/shard_map/all_to_all | solution.py:167
  16.9 101.5 %all-gather.5.cloned.1.call-start = ((), (), s32[]{:S(2)}) async-start(), calls=%async_computation.6 | async-start | bytes 2359296 | tf_op jit(solution)/shard_map/all_gather | solution.py:166
  36.8 18.0 %copy-start = (bf16[8,256,128]{2,1,0:T(8,128)(2,1)}, bf16[8,256,128]{2,1,0:T(8,128)(2,1)S(1)}, u32[]{:S(2)}) copy-start(bf16[8,256,128]{2,1,0:T(8,128)(2,1)S(1)} %all-to-all-done) | copy-start | bytes 1572868
  36.8 23.6 %all-to-all-start.2 = ((bf16[32,64,128]{2,1,0:T(8,128)(2,1)}), bf16[32,64,128]{2,1,0:T(8,128)(2,1)S(1)}, u32[]{:S(2)}, u32[]{:S(2)}) async-start(bf16[32,64,128]{2,1,0:T(8,128)(2,1)} %bitcast.11), calls=%async_computation.2 | async-start | bytes 1048576 | tf_op jit(solution)/shard_map/all_to_all | solution.py:169
  60.4 9.7 %copy-start.2 = (bf16[32,64,128]{2,1,0:T(8,128)(2,1)}, bf16[32,64,128]{2,1,0:T(8,128)(2,1)S(1)}, u32[]{:S(2)}) copy-start(bf16[32,64,128]{2,1,0:T(8,128)(2,1)S(1)} %all-to-all-done.2) | copy-start | bytes 1572868
  60.4 38.9 %all-to-all-start.1 = ((bf16[256,8,128]{2,1,0:T(8,128)(2,1)}), bf16[256,8,128]{2,1,0:T(8,128)(2,1)S(1)}, u32[]{:S(2)}, u32[]{:S(2)}) async-start(bf16[256,8,128]{2,1,0:T(8,128)(2,1)} %bitcast.14), calls=%async_computation.1 | async-start | bytes 1048576 | tf_op jit(solution)/shard_map/all_to_all | solution.py:174
  99.3 0.8 copy-start.3
  111.1 27.4 %all-to-all-start.3 = ((bf16[256,8,128]{2,1,0:T(8,128)(2,1)}), bf16[256,8,128]{2,1,0:T(8,128)(2,1)S(1)}, u32[]{:S(2)}, u32[]{:S(2)}) async-start(bf16[256,8,128]{2,1,0:T(8,128)(2,1)} %bitcast.21), calls=%async_computation.3 | async-start | bytes 1048576 | tf_op jit(solution)/shard_map/all_to_all | solution.py:178
  138.5 0.8 copy-start.1
Sparse Core Ops, SparseCore 0:
  9.2 45.5 all-gather.2
  56.7 46.1 all-gather.4

commit v2 on v1

v2 whole, which is shorter than its diff:
```python
import math

import jax
import jax.numpy as jnp
import ml_dtypes
import numpy as np
from jax import lax
from jax.experimental import pallas as pl
from jax.experimental.pallas import tpu as pltpu
from jax.sharding import PartitionSpec as P


BF = jnp.bfloat16
F32 = jnp.float32
NB = 256
LANES = 128
VMEM_LIMIT = 24 * 1024 * 1024


def split_np(table):
    table = table.astype(np.float32)
    high = table.astype(ml_dtypes.bfloat16)
    low = (table - high.astype(np.float32)).astype(ml_dtypes.bfloat16)
    return high, low


def tables(ctx_count, ch_count):
    k = np.arange(NB, dtype=np.int64)
    arrive = (np.arange(ctx_count)[None, :] * ch_count + np.arange(ch_count)[:, None]).reshape(-1)
    angle = 2.0 * math.pi / (4 * NB) * (((1 + 4 * k)[:, None] * k[None, :]) % (4 * NB))
    outer = np.concatenate([np.cos(angle), np.sin(angle)], axis=0)
    outer_x = outer[:, arrive]
    back = (outer_x * np.repeat([1.0, -1.0], NB)[:, None]).T / (NB * NB)
    angle = 2.0 * math.pi / (4 * NB * NB) * (((1 + 4 * k)[:, None] * k[None, :]) % (4 * NB * NB))
    turn = np.stack([np.cos(angle), np.sin(angle)]).astype(np.float32)
    angle = 2.0 * math.pi / NB * ((k[:, None] * k[None, :]) % NB)
    cos, sin = np.cos(angle), np.sin(angle)
    inner = np.block([[cos, sin], [-sin, cos]])
    return (
        np.stack(split_np(outer)),
        np.stack(split_np(outer_x)),
        np.stack(split_np(inner)),
        np.stack(split_np(back)),
        turn,
    )


def dot(a, b, dims=((1,), (0,))):
    return lax.dot_general(a, b, (dims, ((), ())), preferred_element_type=F32)


def split(x):
    high = x.astype(BF)
    return high, (x - high.astype(F32)).astype(BF)


def weight_rows(place_ref, part_ref, z):
    z_back = (place_ref[1] - z + 4) % 4
    return jnp.concatenate(
        [
            part_ref[pl.ds(pl.multiple_of(((place_ref[2] - q + 4) % 4 * 4 + z_back) * 32, 32), 32), :]
            for q in range(4)
        ],
        axis=0,
    )


def shape_kernel(filters_ref, w_ref, out_ref, wide_ref):
    fh, fl = split(filters_ref[...])
    wh, wl = split(w_ref[...])
    dims = ((0,), (1,))
    shaped = dot(wh, fh, dims) + (dot(wl, fh, dims) + dot(wh, fl, dims))
    rows = wide_ref.shape[0] // 32
    for block in range(shaped.shape[1] // LANES):
        m, half = divmod(block, 2)
        for c in range(4):
            wide_ref[pl.ds(m * 8 + c * 2 + half, 32, stride=rows), :] = shaped[
                32 * c : 32 * (c + 1), block * LANES : (block + 1) * LANES
            ]
    out_ref[...] = wide_ref[...].astype(out_ref.dtype)


def project_kernel(place_ref, tokens_ref, own_ref, mate_ref, out_ref, wide_ref):
    count = tokens_ref.shape[0] // NB
    tokens = jnp.concatenate([tokens_ref[pl.ds(NB * j, NB), :] for j in range(count)], axis=1)
    for rel, part_ref in enumerate((own_ref, mate_ref)):
        for z in range(count // 2):
            j = 2 * z + (place_ref[0] + rel) % 2
            part = dot(weight_rows(place_ref, part_ref, z), tokens, ((1,), (1,)))
            for c in range(4):
                for half in range(2):
                    wide_ref[j, pl.ds(c * 2 + half, 32, stride=8), :] = part[
                        32 * c : 32 * (c + 1), half * LANES : (half + 1) * LANES
                    ]
    for j in range(count):
        out_ref[pl.ds(NB * j, NB), :] = wide_ref[j].astype(out_ref.dtype)


def spread(re, im, turn_ref, axis):
    cos, sin = turn_ref[0], turn_ref[1]
    return split(jnp.concatenate([re * cos - im * sin, re * sin + im * cos], axis=axis))


def inner_product(high, low, inner_ref):
    return dot(high, inner_ref[0]) + (dot(low, inner_ref[0]) + dot(high, inner_ref[1]))


def first_product(wide_ref, outer_ref, c):
    x = jnp.concatenate(
        [wide_ref[pl.ds(c * 2 + half, NB, stride=8), :] for half in range(2)], axis=1
    ).astype(BF)
    return dot(outer_ref[0], x) + dot(outer_ref[1], x)


def filter_kernel(h_ref, outer_ref, inner_ref, turn_ref, out_ref, wide_ref):
    wide_ref[...] = h_ref[...].astype(F32)
    for c in range(4):
        first = first_product(wide_ref, outer_ref, c)
        out_ref[c] = inner_product(*spread(first[:NB], first[NB:], turn_ref, 1), inner_ref)


def conv_kernel(*refs):
    sources, out_ref, wide_ref, held, sem = refs[:6], refs[6], refs[7], refs[8:14], refs[14]
    pairs = list(zip(sources, held))[:5] + [(sources[5].at[c], held[5].at[c]) for c in range(4)]
    copies = [pltpu.make_async_copy(*pair, sem.at[n]) for n, pair in enumerate(pairs)]
    for n in (0, 1, 2, 3, 5, 4):
        copies[n].start()
    x_ref, outer_ref, turn_ref, inner_ref, back_ref, spec_ref = held
    copies[0].wait()
    wide_ref[...] = x_ref[...].astype(F32)
    copies[1].wait()
    for n in (6, 7, 8):
        copies[n].start()
    for c in range(4):
        first = first_product(wide_ref, outer_ref, c)
        if c == 0:
            copies[2].wait()
        high, low = spread(first[:NB], first[NB:], turn_ref, 1)
        if c == 0:
            copies[3].wait()
        got = inner_product(high, low, inner_ref)
        copies[5 + c].wait()
        re, im = got[:, :NB], got[:, NB:]
        hre, him = spec_ref[c, :, :NB], spec_ref[c, :, NB:]
        high, low = split(jnp.concatenate([re * hre - im * him, -(re * him + im * hre)], axis=1))
        half = inner_product(high, low, inner_ref)
        high, low = spread(half[:, :NB], half[:, NB:], turn_ref, 0)
        if c == 0:
            copies[4].wait()
        y = dot(back_ref[0], high) + (dot(back_ref[0], low) + dot(back_ref[1], high))
        for part in range(2):
            wide_ref[pl.ds(c * 2 + part, NB, stride=8), :] = y[
                :, part * LANES : (part + 1) * LANES
            ]
    out_ref[...] = wide_ref[...].astype(out_ref.dtype)


def output_kernel(place_ref, mixed_ref, own_ref, mate_ref, out_ref, wide_ref):
    count = out_ref.shape[0] // NB
    for j in range(count):
        wide_ref[j] = mixed_ref[pl.ds(NB * j, NB), :].astype(F32)
    rows, weights = [], []
    for rel, part_ref in enumerate((own_ref, mate_ref)):
        for z in range(count // 2):
            j = 2 * z + (place_ref[0] + rel) % 2
            weights.append(weight_rows(place_ref, part_ref, z))
            for c in range(4):
                rows.append(
                    jnp.concatenate(
                        [wide_ref[j, pl.ds(c * 2 + half, 32, stride=8), :] for half in range(2)],
                        axis=1,
                    )
                )
    mixed = jnp.concatenate(rows, axis=0).astype(BF)
    result = dot(mixed, jnp.concatenate(weights, axis=0), ((0,), (0,))).astype(out_ref.dtype)
    for j in range(count):
        out_ref[pl.ds(NB * j, NB), :] = result[:, j * LANES : (j + 1) * LANES]


def call(kernel, shape, dtype, wide, flops, *args, scalars=False, fetched=None, limit=VMEM_LIMIT):
    size = sum(a.size * a.dtype.itemsize for a in args) + math.prod(shape) * 4
    space = pltpu.VMEM if fetched is None else pl.ANY
    specs = [pl.BlockSpec(memory_space=space)] * len(args)
    if scalars:
        specs[0] = pl.BlockSpec(memory_space=pltpu.SMEM)
    scratch = [pltpu.VMEM(wide, F32)]
    if fetched is not None:
        scratch = scratch + fetched
    return pl.pallas_call(
        kernel,
        out_shape=jax.ShapeDtypeStruct(shape, dtype),
        in_specs=specs,
        out_specs=pl.BlockSpec(memory_space=pltpu.VMEM),
        scratch_shapes=scratch,
        compiler_params=pltpu.CompilerParams(
            vmem_limit_bytes=limit
        ),
        cost_estimate=pl.CostEstimate(flops=flops, bytes_accessed=size, transcendentals=0),
    )(*args)


def over_z(x, step):
    return lax.ppermute(x, "ch", [(n, (n + 2 * step) % 8) for n in range(8)])


def over_core(x):
    return lax.ppermute(x, "ch", [(n, n ^ 1) for n in range(8)])


def over_plane(x, step_y, step_x):
    pairs = []
    for n in range(32):
        y, rest = divmod(n, 8)
        x_place, z_low = divmod(rest, 2)
        pairs.append((n, (y + step_y) % 4 * 8 + (x_place + step_x) % 4 * 2 + z_low))
    return lax.ppermute(x, "ctx", pairs)


def gather_rows(rows):
    rows = jnp.concatenate([rows, over_z(rows, 1), over_z(rows, 2), over_z(rows, -1)])
    rows = jnp.concatenate(
        [rows, over_plane(rows, 0, 1), over_plane(rows, 1, 0), over_plane(rows, 0, -1)]
    )
    return rows, over_core(rows)


def local(tokens, w_in, filters, w_filter, w_out):
    ctx_count, ch_count = lax.axis_size("ctx"), lax.axis_size("ch")
    ctx_place, ch_place = lax.axis_index("ctx"), lax.axis_index("ch")
    every = ("ch", "ctx")
    outer, outer_x, inner, back, turn = tables(ctx_count, ch_count)
    wide = tokens.shape
    blocks = (ch_count, wide[0] // ch_count, wide[1])
    quarter = (ctx_place // 2 % 4 + 2 * (ctx_place // 8)) % 4
    place = jnp.stack([ch_place % 2, ch_place // 2, quarter]).astype(jnp.int32)
    in_own, in_mate = gather_rows(lax.dynamic_slice_in_dim(w_in, 32 * quarter, 32, 1).T)
    tokens = lax.all_to_all(tokens, "ch", 0, 0, tiled=True)
    shaped = call(shape_kernel, wide, BF, wide, 2**25, filters, w_filter)
    shaped = lax.all_to_all(shaped, "ctx", 0, 0, tiled=True)
    spectrum = call(
        filter_kernel, (4, NB, 2 * NB), F32, wide, 2**31, shaped, outer, inner, turn
    )
    w_out, tokens = lax.optimization_barrier((w_out, tokens))
    out_own, out_mate = gather_rows(lax.dynamic_slice_in_dim(w_out, 32 * quarter, 32, 0))
    signal = call(
        project_kernel, wide, BF, blocks, 2**29, place, tokens, in_own, in_mate, scalars=True
    )
    signal = lax.all_to_all(signal, every, 0, 0, tiled=True)
    operands = [signal, outer_x, turn, inner, back, spectrum]
    fetched = [pltpu.VMEM(a.shape, a.dtype) for a in operands] + [pltpu.SemaphoreType.DMA((9,))]
    mixed = call(
        conv_kernel, wide, BF, wide, 2**32, *operands, fetched=fetched, limit=60 * 2**20
    )
    mixed = lax.all_to_all(mixed, every, 0, 0, tiled=True)
    result = call(
        output_kernel, wide, BF, blocks, 2**29, place, mixed, out_own, out_mate, scalars=True
    )
    return lax.all_to_all(result, "ch", 0, 0, tiled=True)


def solution(mesh):
    placed = (P("ctx", "ch"), P(None, "ch"), P("ctx", None), P(None, "ch"), P("ch", None))
    return jax.shard_map(
        local, mesh=mesh, in_specs=placed, out_specs=P("ctx", "ch"), check_vma=False
    )
```

time: 173 us -> 146 us (0.84)
  waiting for transfers between devices: 68.2 us -> 38.2 us
  starting transfers between devices: 35.5 us -> 53.4 us
  between operations: 13.5 us -> 0.25 us
  Pallas kernels: 27.6 us -> 20.2 us
  local copies, waits for them, and re-layouts: 5.55 us -> 12.2 us
    ppermute x0 -> x14, starting transfers between devices: none -> 25.3 us  [the longest x6 17.8 us: over_z(): return lax.ppermute(x, 'ch', [(n, (n + 2 * step) % 8) for n in range(8)])]
    all_to_all x1, waiting for transfers between devices: 23.3 us -> 3.23 us  [local(): signal = lax.all_to_all(signal, every, 0, 0, tiled=True)]
    all_to_all x1, waiting for transfers between devices: 14.6 us -> 2.4 us  [local(): tokens = lax.all_to_all(tokens, 'ch', 0, 0, tiled=True)]
    ppermute x0 -> x14, waiting for transfers between devices: none -> 8.98 us  [the longest x6 8.84 us: over_plane(): return lax.ppermute(x, 'ctx', pairs)]
    all_gather x2 -> x0, waiting for transfers between devices: 7.97 us -> none  [the longest x1 7.95 us: local(): w_in = lax.all_gather(w_in.T, 'ch', axis=0, tiled=True)]
    pallas_call x5, Pallas kernels: 27.6 us -> 20.2 us  [call(): pl.pallas_call(kernel, out_shape=jax.ShapeDtypeStruct(shape, dtype), in_s...]
    unnamed x13 -> x29, local copies, waits for them, and re-layouts: 5.55 us -> 11.3 us
    all_to_all x1, starting transfers between devices: 8.48 us -> 3.49 us  [local(): tokens = lax.all_to_all(tokens, 'ch', 0, 0, tiled=True)]
  transfers between devices with their start and end apart: 6 -> 18, of which waited for: 5 -> 9; matrix products, arithmetic and copies ran while one was open for 1% -> 6% of each run, Pallas kernels for 14% -> 13%
where the time goes in v2:
time: 146 us
  starting transfers between devices  53.4 us (37%)
  waiting for transfers between devices  38.2 us (26%)
  blocking collectives  20.4 us (14%)
  Pallas kernels  20.2 us (14%)
  local copies, waits for them, and re-layouts  12.2 us (8%)
    all_to_all x1, blocking collectives, local(): return lax.all_to_all(result, 'ch', 0, 0, tiled=True)  20.4 us
    pallas_call x5, Pallas kernels, call(): pl.pallas_call(kernel, out_shape=jax.ShapeDtypeStruct(shape, dtype), in_s...  20.2 us
    all_to_all x1, waiting for transfers between devices, local(): mixed = lax.all_to_all(mixed, every, 0, 0, tiled=True)  20.1 us
    ppermute x6, starting transfers between devices, over_z(): return lax.ppermute(x, 'ch', [(n, (n + 2 * step) % 8) for n in range(8)])  17.8 us
    unnamed x29, local copies, waits for them, and re-layouts  11.3 us
    ppermute x6, waiting for transfers between devices, over_plane(): return lax.ppermute(x, 'ctx', pairs)  8.84 us
    all_to_all x1, starting transfers between devices, local(): signal = lax.all_to_all(signal, every, 0, 0, tiled=True)  8.56 us
    all_to_all x1, starting transfers between devices, local(): mixed = lax.all_to_all(mixed, every, 0, 0, tiled=True)  8.07 us
  transfers between devices with their start and end apart: 18, of which 9 were waited for; matrix products, arithmetic and copies ran while one was open for 6% of the time, Pallas kernels for 13%

profile of v2, /device:TPU:2, one launch (start us, length us, event | category | flops | bytes accessed | tf_op | source)
XLA Modules:
  0.0 145.7 jit_solution(218497602963077294)
XLA Ops:
  0.0 0.9 copy-done
  1.2 3.3 %collective-permute-start = (bf16[32,1024]{1,0:T(8,128)(2,1)S(1)}, bf16[32,1024]{1,0:T(8,128)(2,1)S(1)}, u32[]{:S(2)}, u32[]{:S(2)}) collective-permute-start(bf16[32,1024]{1,0:T(8,128)(2,1)S(1)} %bitcast.20), channel_id=1, source_target_pairs={{0,2},{1,3},{2,4},{3,5},{4,6},{5,7},{6,0},{7,1},{8,10},{9,11},{10,... | collective-permute-start | bytes 196616 | tf_op jit(solution)/shard_map/ppermute | solution.py:203
  4.6 5.4 %collective-permute-start.1 = (bf16[32,1024]{1,0:T(8,128)(2,1)S(1)}, bf16[32,1024]{1,0:T(8,128)(2,1)S(1)}, u32[]{:S(2)}, u32[]{:S(2)}) collective-permute-start(bf16[32,1024]{1,0:T(8,128)(2,1)S(1)} %bitcast.21), channel_id=1, source_target_pairs={{0,4},{1,5},{2,6},{3,7},{4,0},{5,1},{6,2},{7,3},{8,12},{9,13},{10,... | collective-permute-start | bytes 196616 | tf_op jit(solution)/shard_map/ppermute | solution.py:203
  10.0 2.7 %collective-permute-start.2 = (bf16[32,1024]{1,0:T(8,128)(2,1)S(1)}, bf16[32,1024]{1,0:T(8,128)(2,1)S(1)}, u32[]{:S(2)}, u32[]{:S(2)}) collective-permute-start(bf16[32,1024]{1,0:T(8,128)(2,1)S(1)} %bitcast.22), channel_id=1, source_target_pairs={{0,6},{1,7},{2,0},{3,1},{4,2},{5,3},{6,4},{7,5},{8,14},{9,15},{10,... | collective-permute-start | bytes 196616 | tf_op jit(solution)/shard_map/ppermute | solution.py:203
  12.6 3.5 %all-to-all-start = ((bf16[8,256,128]{2,1,0:T(8,128)(2,1)}), bf16[8,256,128]{2,1,0:T(8,128)(2,1)S(1)}, u32[]{:S(2)}, u32[]{:S(2)}) async-start(bf16[8,256,128]{2,1,0:T(8,128)(2,1)} %bitcast.24), calls=%async_computation | async-start | bytes 1048576 | tf_op jit(solution)/shard_map/all_to_all | solution.py:237
  16.9 1.6 %collective-permute-start.3 = (bf16[128,1024]{1,0:T(8,128)(2,1)S(1)}, bf16[128,1024]{1,0:T(8,128)(2,1)S(1)}, u32[]{:S(2)}, u32[]{:S(2)}) collective-permute-start(bf16[128,1024]{1,0:T(8,128)(2,1)S(1)} %pad_maximum_fusion), channel_id=1, source_target_pairs={{0,16},{8,24},{16,32},{24,40},{32,48},{40,56},{48,0},{56,8},{64,80... | collective-permute-start | bytes 786440 | tf_op jit(solution)/shard_map/ppermute | solution.py:216
  18.5 1.6 %collective-permute-start.4 = (bf16[128,1024]{1,0:T(8,128)(2,1)S(1)}, bf16[128,1024]{1,0:T(8,128)(2,1)S(1)}, u32[]{:S(2)}, u32[]{:S(2)}) collective-permute-start(bf16[128,1024]{1,0:T(8,128)(2,1)S(1)} %pad_maximum_fusion), channel_id=1, source_target_pairs={{0,64},{8,72},{16,80},{24,88},{32,96},{40,104},{48,112},{56,120},{... | collective-permute-start | bytes 786440 | tf_op jit(solution)/shard_map/ppermute | solution.py:216
  22.5 3.0 %collective-permute-done.3 = bf16[128,1024]{1,0:T(8,128)(2,1)S(1)} collective-permute-done((bf16[128,1024]{1,0:T(8,128)(2,1)S(1)}, bf16[128,1024]{1,0:T(8,128)(2,1)S(1)}, u32[]{:S(2)}, u32[]{:S(2)}) %collective-permute-start.3) | collective-permute-done | bytes 262176 | tf_op jit(solution)/shard_map/ppermute | solution.py:216
  26.2 1.8 %collective-permute-done.4 = bf16[128,1024]{1,0:T(8,128)(2,1)S(1)} collective-permute-done((bf16[128,1024]{1,0:T(8,128)(2,1)S(1)}, bf16[128,1024]{1,0:T(8,128)(2,1)S(1)}, u32[]{:S(2)}, u32[]{:S(2)}) %collective-permute-start.4) | collective-permute-done | bytes 262176 | tf_op jit(solution)/shard_map/ppermute | solution.py:216
  29.8 2.0 %shard_map.101 = bf16[2048,128]{1,0:T(8,128)(2,1)} custom-call(f32[2048,24]{1,0:T(8,128)S(1)} %copy.12.filters_ref, f32[24,128]{1,0:T(8,128)S(1)} %copy-done.1), custom_call_target="tpu_custom_call" | custom-call | flops 33554432 | bytes 1257472 | tf_op jit(solution)/shard_map/pallas_call | solution.py:189
  31.8 2.4 %all-to-all-done = bf16[8,256,128]{2,1,0:T(8,128)(2,1)S(1)} async-done(((bf16[8,256,128]{2,1,0:T(8,128)(2,1)}), bf16[8,256,128]{2,1,0:T(8,128)(2,1)S(1)}, u32[]{:S(2)}, u32[]{:S(2)}) %all-to-all-start) | async-done | bytes 524320 | tf_op jit(solution)/shard_map/all_to_all | solution.py:237
  34.2 8.0 %all-to-all-start.2 = ((bf16[32,64,128]{2,1,0:T(8,128)(2,1)}), bf16[32,64,128]{2,1,0:T(8,128)(2,1)S(1)}, u32[]{:S(2)}, u32[]{:S(2)}) async-start(bf16[32,64,128]{2,1,0:T(8,128)(2,1)} %bitcast.8), calls=%async_computation.2 | async-start | bytes 1048576 | tf_op jit(solution)/shard_map/all_to_all | solution.py:239
  42.3 0.8 constant_dynamic-update-slice_fusion.13
  43.3 3.0 %collective-permute-start.8 = (bf16[32,1024]{1,0:T(8,128)(2,1)S(1)}, bf16[32,1024]{1,0:T(8,128)(2,1)}, u32[]{:S(2)}, u32[]{:S(2)}) collective-permute-start(bf16[32,1024]{1,0:T(8,128)(2,1)S(1)} %get-tuple-element.10), channel_id=1, source_target_pairs={{0,4},{1,5},{2,6},{3,7},{4,0},{5,1},{6,2},{7,3},{8,12},{9,13},{10,... | collective-permute-start | bytes 196616 | tf_op jit(solution)/shard_map/ppermute | solution.py:203
  46.3 3.3 %collective-permute-start.9 = (bf16[32,1024]{1,0:T(8,128)(2,1)S(1)}, bf16[32,1024]{1,0:T(8,128)(2,1)}, u32[]{:S(2)}, u32[]{:S(2)}) collective-permute-start(bf16[32,1024]{1,0:T(8,128)(2,1)S(1)} %get-tuple-element.10), channel_id=1, source_target_pairs={{0,6},{1,7},{2,0},{3,1},{4,2},{5,3},{6,4},{7,5},{8,14},{9,15},{10,... | collective-permute-start | bytes 196616 | tf_op jit(solution)/shard_map/ppermute | solution.py:203
  49.5 3.9 %shard_map.100 = bf16[2048,128]{1,0:T(8,128)(2,1)} custom-call(s32[3]{0:T(128)S(1)} %pad_add_fusion.place_ref, bf16[2048,128]{1,0:T(8,128)(2,1)S(1)} %bitcast.15, bf16[512,1024]{1,0:T(8,128)(2,1)} %constant_dynamic-update-slice_fusion.own_ref, bf16[512,1024]{1,0:T(8,128)(2,1)} %collective-permute-done.6.mate_ref), custom_call_target="tpu_custom_call" | custom-call | flops 536870912 | bytes 3670028 | tf_op jit(solution)/shard_map/pallas_call | solution.py:189
  53.4 3.5 %all-to-all-done.2 = bf16[32,64,128]{2,1,0:T(8,128)(2,1)S(1)} async-done(((bf16[32,64,128]{2,1,0:T(8,128)(2,1)}), bf16[32,64,128]{2,1,0:T(8,128)(2,1)S(1)}, u32[]{:S(2)}, u32[]{:S(2)}) %all-to-all-start.2) | async-done | bytes 524320 | tf_op jit(solution)/shard_map/all_to_all | solution.py:239
  56.9 8.6 %all-to-all-start.1 = ((bf16[256,8,128]{2,1,0:T(8,128)(2,1)}), bf16[256,8,128]{2,1,0:T(8,128)(2,1)}, u32[]{:S(2)}, u32[]{:S(2)}) async-start(bf16[256,8,128]{2,1,0:T(8,128)(2,1)} %bitcast.6), calls=%async_computation.1 | async-start | bytes 1048576 | tf_op jit(solution)/shard_map/all_to_all | solution.py:248
  65.5 0.9 pad_maximum_fusion.1
  66.4 1.7 %collective-permute-start.10 = (bf16[128,1024]{1,0:T(8,128)(2,1)S(1)}, bf16[128,1024]{1,0:T(8,128)(2,1)S(1)}, u32[]{:S(2)}, u32[]{:S(2)}) collective-permute-start(bf16[128,1024]{1,0:T(8,128)(2,1)S(1)} %pad_maximum_fusion.1), channel_id=1, source_target_pairs={{0,16},{8,24},{16,32},{24,40},{32,48},{40,56},{48,0},{56,8},{64,80... | collective-permute-start | bytes 786440 | tf_op jit(solution)/shard_map/ppermute | solution.py:216
  68.1 1.5 %collective-permute-start.11 = (bf16[128,1024]{1,0:T(8,128)(2,1)S(1)}, bf16[128,1024]{1,0:T(8,128)(2,1)S(1)}, u32[]{:S(2)}, u32[]{:S(2)}) collective-permute-start(bf16[128,1024]{1,0:T(8,128)(2,1)S(1)} %pad_maximum_fusion.1), channel_id=1, source_target_pairs={{0,64},{8,72},{16,80},{24,88},{32,96},{40,104},{48,112},{56,120},{... | collective-permute-start | bytes 786440 | tf_op jit(solution)/shard_map/ppermute | solution.py:216
  71.8 1.2 copy-done.2
  73.1 2.8 %shard_map.102.refs_5_ = f32[4,256,512]{2,1,0:T(8,128)S(1)} custom-call(bf16[2048,128]{1,0:T(8,128)(2,1)S(1)} %bitcast.18, bf16[2,512,256]{2,1,0:T(8,128)(2,1)S(1)} %copy-done.4, bf16[2,512,512]{2,1,0:T(8,128)(2,1)S(1)} %copy-done.2, f32[2,256,256]{2,1,0:T(8,128)S(1)} %copy-done.3), custom_call_target="tpu_custom_call" | custom-call | flops 2147483648 | bytes 4718592 | tf_op jit(solution)/shard_map/pallas_call | solution.py:189
  75.9 1.3 copy-done.5
  77.2 1.3 collective-permute-done.10
  78.6 2.7 %collective-permute-done.11 = bf16[128,1024]{1,0:T(8,128)(2,1)S(1)} collective-permute-done((bf16[128,1024]{1,0:T(8,128)(2,1)S(1)}, bf16[128,1024]{1,0:T(8,128)(2,1)S(1)}, u32[]{:S(2)}, u32[]{:S(2)}) %collective-permute-start.11) | collective-permute-done | bytes 262176 | tf_op jit(solution)/shard_map/ppermute | solution.py:216
  81.5 3.2 %all-to-all-done.1 = bf16[256,8,128]{2,1,0:T(8,128)(2,1)} async-done(((bf16[256,8,128]{2,1,0:T(8,128)(2,1)}), bf16[256,8,128]{2,1,0:T(8,128)(2,1)}, u32[]{:S(2)}, u32[]{:S(2)}) %all-to-all-start.1) | async-done | bytes 524320 | tf_op jit(solution)/shard_map/all_to_all | solution.py:248
  84.7 10.2 %shard_map.103 = bf16[2048,128]{1,0:T(8,128)(2,1)} custom-call(bf16[2048,128]{1,0:T(8,128)(2,1)} %bitcast.7.refs_0_, bf16[2,512,256]{2,1,0:T(8,128)(2,1)} %constant.82.clone.refs_1_, f32[2,256,256]{2,1,0:T(8,128)} %constant.81.clone.turn_ref.refs_2_, bf16[2,512,512]{2,1,0:T(8,128)(2,1)} %constant.80.clone.inner_ref.refs_3_, ...), custom_call_target="tpu_custom_call" | custom-call | flops 4294967296 | bytes 6291456 | tf_op jit(solution)/shard_map/pallas_call | solution.py:189
  94.9 8.1 %all-to-all-start.3 = ((bf16[256,8,128]{2,1,0:T(8,128)(2,1)}), bf16[256,8,128]{2,1,0:T(8,128)(2,1)S(1)}, u32[]{:S(2)}, u32[]{:S(2)}) async-start(bf16[256,8,128]{2,1,0:T(8,128)(2,1)} %bitcast.25), calls=%async_computation.3 | async-start | bytes 1048576 | tf_op jit(solution)/shard_map/all_to_all | solution.py:254
  102.9 20.1 %all-to-all-done.3 = bf16[256,8,128]{2,1,0:T(8,128)(2,1)S(1)} async-done(((bf16[256,8,128]{2,1,0:T(8,128)(2,1)}), bf16[256,8,128]{2,1,0:T(8,128)(2,1)S(1)}, u32[]{:S(2)}, u32[]{:S(2)}) %all-to-all-start.3) | async-done | bytes 524320 | tf_op jit(solution)/shard_map/all_to_all | solution.py:254
  123.1 1.4 shard_map.104
  124.5 20.4 %all_to_all.57 = bf16[8,256,128]{2,1,0:T(8,128)(2,1)S(1)} all-to-all(bf16[8,256,128]{2,1,0:T(8,128)(2,1)S(1)} %bitcast.17), channel_id=1, replica_groups=mesh['ctx'=32,'ch'=8] {'ch'}, dimensions={0} | all-to-all | bytes 1048576 | tf_op jit(solution)/shard_map/all_to_all | solution.py:258
  (45 shorter events, 9.4 us)
Async XLA Ops:
  0.0 1.0 copy-start
  1.1 28.3 %copy-start.6 = (f32[2048,24]{0,1:T(8,128)S(1)}, f32[2048,24]{0,1:T(8,128)}, u32[]{:S(2)}) copy-start(f32[2048,24]{0,1:T(8,128)} %param.12) | copy-start | bytes 589828
  1.2 15.5 %collective-permute-start = (bf16[32,1024]{1,0:T(8,128)(2,1)S(1)}, bf16[32,1024]{1,0:T(8,128)(2,1)S(1)}, u32[]{:S(2)}, u32[]{:S(2)}) collective-permute-start(bf16[32,1024]{1,0:T(8,128)(2,1)S(1)} %bitcast.20), channel_id=1, source_target_pairs={{0,2},{1,3},{2,4},{3,5},{4,6},{5,7},{6,0},{7,1},{8,10},{9,11},{10,... | collective-permute-start | bytes 196616 | tf_op jit(solution)/shard_map/ppermute | solution.py:203
  4.6 12.2 %collective-permute-start.1 = (bf16[32,1024]{1,0:T(8,128)(2,1)S(1)}, bf16[32,1024]{1,0:T(8,128)(2,1)S(1)}, u32[]{:S(2)}, u32[]{:S(2)}) collective-permute-start(bf16[32,1024]{1,0:T(8,128)(2,1)S(1)} %bitcast.21), channel_id=1, source_target_pairs={{0,4},{1,5},{2,6},{3,7},{4,0},{5,1},{6,2},{7,3},{8,12},{9,13},{10,... | collective-permute-start | bytes 196616 | tf_op jit(solution)/shard_map/ppermute | solution.py:203
  10.0 6.9 %collective-permute-start.2 = (bf16[32,1024]{1,0:T(8,128)(2,1)S(1)}, bf16[32,1024]{1,0:T(8,128)(2,1)S(1)}, u32[]{:S(2)}, u32[]{:S(2)}) collective-permute-start(bf16[32,1024]{1,0:T(8,128)(2,1)S(1)} %bitcast.22), channel_id=1, source_target_pairs={{0,6},{1,7},{2,0},{3,1},{4,2},{5,3},{6,4},{7,5},{8,14},{9,15},{10,... | collective-permute-start | bytes 196616 | tf_op jit(solution)/shard_map/ppermute | solution.py:203
  12.6 21.5 %all-to-all-start = ((bf16[8,256,128]{2,1,0:T(8,128)(2,1)}), bf16[8,256,128]{2,1,0:T(8,128)(2,1)S(1)}, u32[]{:S(2)}, u32[]{:S(2)}) async-start(bf16[8,256,128]{2,1,0:T(8,128)(2,1)} %bitcast.24), calls=%async_computation | async-start | bytes 1048576 | tf_op jit(solution)/shard_map/all_to_all | solution.py:237
  16.1 13.6 %copy-start.1 = (f32[24,128]{1,0:T(8,128)S(1)}, f32[24,128]{1,0:T(8,128)}, u32[]{:S(2)}) copy-start(f32[24,128]{1,0:T(8,128)} %w_ref.1) | copy-start | bytes 36868
  16.9 8.6 %collective-permute-start.3 = (bf16[128,1024]{1,0:T(8,128)(2,1)S(1)}, bf16[128,1024]{1,0:T(8,128)(2,1)S(1)}, u32[]{:S(2)}, u32[]{:S(2)}) collective-permute-start(bf16[128,1024]{1,0:T(8,128)(2,1)S(1)} %pad_maximum_fusion), channel_id=1, source_target_pairs={{0,16},{8,24},{16,32},{24,40},{32,48},{40,56},{48,0},{56,8},{64,80... | collective-permute-start | bytes 786440 | tf_op jit(solution)/shard_map/ppermute | solution.py:216
  18.5 9.5 %collective-permute-start.4 = (bf16[128,1024]{1,0:T(8,128)(2,1)S(1)}, bf16[128,1024]{1,0:T(8,128)(2,1)S(1)}, u32[]{:S(2)}, u32[]{:S(2)}) collective-permute-start(bf16[128,1024]{1,0:T(8,128)(2,1)S(1)} %pad_maximum_fusion), channel_id=1, source_target_pairs={{0,64},{8,72},{16,80},{24,88},{32,96},{40,104},{48,112},{56,120},{... | collective-permute-start | bytes 786440 | tf_op jit(solution)/shard_map/ppermute | solution.py:216
  20.1 8.7 %collective-permute-start.5 = (bf16[128,1024]{1,0:T(8,128)(2,1)S(1)}, bf16[128,1024]{1,0:T(8,128)(2,1)S(1)}, u32[]{:S(2)}, u32[]{:S(2)}) collective-permute-start(bf16[128,1024]{1,0:T(8,128)(2,1)S(1)} %pad_maximum_fusion), channel_id=1, source_target_pairs={{0,48},{8,56},{16,0},{24,8},{32,16},{40,24},{48,32},{56,40},{64,11... | collective-permute-start | bytes 786440 | tf_op jit(solution)/shard_map/ppermute | solution.py:216
  29.4 20.1 %collective-permute-start.6 = (bf16[512,1024]{1,0:T(8,128)(2,1)}, bf16[512,1024]{1,0:T(8,128)(2,1)}, u32[]{:S(2)}, u32[]{:S(2)}) collective-permute-start(bf16[512,1024]{1,0:T(8,128)(2,1)} %constant_dynamic-update-slice_fusion.own_ref), channel_id=1, source_target_pairs={{0,1},{1,0},{2,3},{3,2},{4,5},{5,4},{6,7},{7,6},{8,9},{9,8},{10,11... | collective-permute-start | bytes 3145736 | tf_op jit(solution)/shard_map/ppermute | solution.py:207
  34.2 22.7 %all-to-all-start.2 = ((bf16[32,64,128]{2,1,0:T(8,128)(2,1)}), bf16[32,64,128]{2,1,0:T(8,128)(2,1)S(1)}, u32[]{:S(2)}, u32[]{:S(2)}) async-start(bf16[32,64,128]{2,1,0:T(8,128)(2,1)} %bitcast.8), calls=%async_computation.2 | async-start | bytes 1048576 | tf_op jit(solution)/shard_map/all_to_all | solution.py:239
  43.1 28.7 %copy-start.3 = (f32[2,256,256]{2,1,0:T(8,128)S(1)}, f32[2,256,256]{2,1,0:T(8,128)}, u32[]{:S(2)}) copy-start(f32[2,256,256]{2,1,0:T(8,128)} %constant.81.clone.turn_ref.refs_2_) | copy-start | bytes 1572868
  43.1 28.7 %copy-start.4 = (bf16[2,512,256]{2,1,0:T(8,128)(2,1)S(1)}, bf16[2,512,256]{2,1,0:T(8,128)(2,1)}, u32[]{:S(2)}) copy-start(bf16[2,512,256]{2,1,0:T(8,128)(2,1)} %constant.79.clone.outer_ref) | copy-start | bytes 1572868
  43.2 22.3 %collective-permute-start.7 = (bf16[32,1024]{1,0:T(8,128)(2,1)S(1)}, bf16[32,1024]{1,0:T(8,128)(2,1)S(1)}, u32[]{:S(2)}, u32[]{:S(2)}) collective-permute-start(bf16[32,1024]{1,0:T(8,128)(2,1)S(1)} %get-tuple-element.10), channel_id=1, source_target_pairs={{0,2},{1,3},{2,4},{3,5},{4,6},{5,7},{6,0},{7,1},{8,10},{9,11},{10,... | collective-permute-start | bytes 196616 | tf_op jit(solution)/shard_map/ppermute | solution.py:203
  43.3 22.2 %collective-permute-start.8 = (bf16[32,1024]{1,0:T(8,128)(2,1)S(1)}, bf16[32,1024]{1,0:T(8,128)(2,1)}, u32[]{:S(2)}, u32[]{:S(2)}) collective-permute-start(bf16[32,1024]{1,0:T(8,128)(2,1)S(1)} %get-tuple-element.10), channel_id=1, source_target_pairs={{0,4},{1,5},{2,6},{3,7},{4,0},{5,1},{6,2},{7,3},{8,12},{9,13},{10,... | collective-permute-start | bytes 196616 | tf_op jit(solution)/shard_map/ppermute | solution.py:203
  46.3 19.2 %collective-permute-start.9 = (bf16[32,1024]{1,0:T(8,128)(2,1)S(1)}, bf16[32,1024]{1,0:T(8,128)(2,1)}, u32[]{:S(2)}, u32[]{:S(2)}) collective-permute-start(bf16[32,1024]{1,0:T(8,128)(2,1)S(1)} %get-tuple-element.10), channel_id=1, source_target_pairs={{0,6},{1,7},{2,0},{3,1},{4,2},{5,3},{6,4},{7,5},{8,14},{9,15},{10,... | collective-permute-start | bytes 196616 | tf_op jit(solution)/shard_map/ppermute | solution.py:203
  56.9 27.8 %all-to-all-start.1 = ((bf16[256,8,128]{2,1,0:T(8,128)(2,1)}), bf16[256,8,128]{2,1,0:T(8,128)(2,1)}, u32[]{:S(2)}, u32[]{:S(2)}) async-start(bf16[256,8,128]{2,1,0:T(8,128)(2,1)} %bitcast.6), calls=%async_computation.1 | async-start | bytes 1048576 | tf_op jit(solution)/shard_map/all_to_all | solution.py:248
  66.4 12.2 %collective-permute-start.10 = (bf16[128,1024]{1,0:T(8,128)(2,1)S(1)}, bf16[128,1024]{1,0:T(8,128)(2,1)S(1)}, u32[]{:S(2)}, u32[]{:S(2)}) collective-permute-start(bf16[128,1024]{1,0:T(8,128)(2,1)S(1)} %pad_maximum_fusion.1), channel_id=1, source_target_pairs={{0,16},{8,24},{16,32},{24,40},{32,48},{40,56},{48,0},{56,8},{64,80... | collective-permute-start | bytes 786440 | tf_op jit(solution)/shard_map/ppermute | solution.py:216
  68.1 13.2 %collective-permute-start.11 = (bf16[128,1024]{1,0:T(8,128)(2,1)S(1)}, bf16[128,1024]{1,0:T(8,128)(2,1)S(1)}, u32[]{:S(2)}, u32[]{:S(2)}) collective-permute-start(bf16[128,1024]{1,0:T(8,128)(2,1)S(1)} %pad_maximum_fusion.1), channel_id=1, source_target_pairs={{0,64},{8,72},{16,80},{24,88},{32,96},{40,104},{48,112},{56,120},{... | collective-permute-start | bytes 786440 | tf_op jit(solution)/shard_map/ppermute | solution.py:216
  69.6 11.8 %collective-permute-start.12 = (bf16[128,1024]{1,0:T(8,128)(2,1)S(1)}, bf16[128,1024]{1,0:T(8,128)(2,1)S(1)}, u32[]{:S(2)}, u32[]{:S(2)}) collective-permute-start(bf16[128,1024]{1,0:T(8,128)(2,1)S(1)} %pad_maximum_fusion.1), channel_id=1, source_target_pairs={{0,48},{8,56},{16,0},{24,8},{32,16},{40,24},{48,32},{56,40},{64,11... | collective-permute-start | bytes 786440 | tf_op jit(solution)/shard_map/ppermute | solution.py:216
  71.8 1.2 copy-start.2
  75.9 1.3 copy-start.5
  81.4 21.6 %collective-permute-start.13 = (bf16[512,1024]{1,0:T(8,128)(2,1)S(1)}, bf16[512,1024]{1,0:T(8,128)(2,1)S(1)}, u32[]{:S(2)}, u32[]{:S(2)}) collective-permute-start(bf16[512,1024]{1,0:T(8,128)(2,1)S(1)} %constant_dynamic-update-slice_fusion.7.own_ref), channel_id=1, source_target_pairs={{0,1},{1,0},{2,3},{3,2},{4,5},{5,4},{6,7},{7,6},{8,9},{9,8},{10,11... | collective-permute-start | bytes 3145736 | tf_op jit(solution)/shard_map/ppermute | solution.py:207
  94.9 28.2 %all-to-all-start.3 = ((bf16[256,8,128]{2,1,0:T(8,128)(2,1)}), bf16[256,8,128]{2,1,0:T(8,128)(2,1)S(1)}, u32[]{:S(2)}, u32[]{:S(2)}) async-start(bf16[256,8,128]{2,1,0:T(8,128)(2,1)} %bitcast.25), calls=%async_computation.3 | async-start | bytes 1048576 | tf_op jit(solution)/shard_map/all_to_all | solution.py:254

commit v3 on v2

--- a/solution.py
+++ b/solution.py
@@ -216,12 +216,11 @@
     return lax.ppermute(x, "ctx", pairs)
 
 
-def gather_rows(rows):
-    rows = jnp.concatenate([rows, over_z(rows, 1), over_z(rows, 2), over_z(rows, -1)])
+def gather_plane(rows):
     rows = jnp.concatenate(
         [rows, over_plane(rows, 0, 1), over_plane(rows, 1, 0), over_plane(rows, 0, -1)]
     )
-    return rows, over_core(rows)
+    return rows
 
 
 def local(tokens, w_in, filters, w_filter, w_out):
@@ -233,18 +232,32 @@
     blocks = (ch_count, wide[0] // ch_count, wide[1])
     quarter = (ctx_place // 2 % 4 + 2 * (ctx_place // 8)) % 4
     place = jnp.stack([ch_place % 2, ch_place // 2, quarter]).astype(jnp.int32)
-    in_own, in_mate = gather_rows(lax.dynamic_slice_in_dim(w_in, 32 * quarter, 32, 1).T)
+    shaped = call(shape_kernel, wide, BF, wide, 2**25, filters, w_filter)
+    w_in, w_out, shaped = lax.optimization_barrier((w_in, w_out, shaped))
+    rows = jnp.concatenate(
+        [
+            lax.dynamic_slice_in_dim(w_in, 32 * quarter, 32, 1).T,
+            lax.dynamic_slice_in_dim(w_out, 32 * quarter, 32, 0),
+        ]
+    )
+    shaped = lax.all_to_all(shaped, "ctx", 0, 0, tiled=True)
+    rows = jnp.stack([rows, over_z(rows, 1), over_z(rows, 2), over_z(rows, -1)])
+    tokens, shaped, rows = lax.optimization_barrier((tokens, shaped, rows))
+    in_rows = rows[:, :32].reshape(128, -1)
+    out_rows = rows[:, 32:].reshape(128, -1)
     tokens = lax.all_to_all(tokens, "ch", 0, 0, tiled=True)
-    shaped = call(shape_kernel, wide, BF, wide, 2**25, filters, w_filter)
-    shaped = lax.all_to_all(shaped, "ctx", 0, 0, tiled=True)
+    in_own = gather_plane(in_rows)
+    tokens, in_own = lax.optimization_barrier((tokens, in_own))
+    in_mate = over_core(in_own)
+    signal = call(
+        project_kernel, wide, BF, blocks, 2**29, place, tokens, in_own, in_mate, scalars=True
+    )
+    out_rows, signal, shaped = lax.optimization_barrier((out_rows, signal, shaped))
     spectrum = call(
         filter_kernel, (4, NB, 2 * NB), F32, wide, 2**31, shaped, outer, inner, turn
     )
-    w_out, tokens = lax.optimization_barrier((w_out, tokens))
-    out_own, out_mate = gather_rows(lax.dynamic_slice_in_dim(w_out, 32 * quarter, 32, 0))
-    signal = call(
-        project_kernel, wide, BF, blocks, 2**29, place, tokens, in_own, in_mate, scalars=True
-    )
+    out_own = gather_plane(out_rows)
+    out_mate = over_core(out_own)
     signal = lax.all_to_all(signal, every, 0, 0, tiled=True)
     operands = [signal, outer_x, turn, inner, back, spectrum]
     fetched = [pltpu.VMEM(a.shape, a.dtype) for a in operands] + [pltpu.SemaphoreType.DMA((9,))]

time: 146 us -> 152 us (1.041)
  waiting for transfers between devices: 38.2 us -> 57.5 us
  starting transfers between devices: 53.4 us -> 45.4 us
  local copies, waits for them, and re-layouts: 12.2 us -> 8.49 us
    ppermute x6 -> x3, waiting for transfers between devices: 0.14 us -> 12.9 us  [over_z(): return lax.ppermute(x, 'ch', [(n, (n + 2 * step) % 8) for n in range(8)])]
    ppermute x6 -> x3, starting transfers between devices: 17.8 us -> 9.29 us  [over_z(): return lax.ppermute(x, 'ch', [(n, (n + 2 * step) % 8) for n in range(8)])]
    all_to_all x1, waiting for transfers between devices: 2.4 us -> 6.39 us  [local(): tokens = lax.all_to_all(tokens, 'ch', 0, 0, tiled=True)]
    unnamed x29 -> x21, local copies, waits for them, and re-layouts: 11.3 us -> 7.52 us
    all_to_all x1, waiting for transfers between devices: 3.47 us -> 0.01 us  [local(): shaped = lax.all_to_all(shaped, 'ctx', 0, 0, tiled=True)]
    ppermute x6, waiting for transfers between devices: 8.84 us -> 11.4 us  [over_plane(): return lax.ppermute(x, 'ctx', pairs)]
    ppermute x2, waiting for transfers between devices: 0.01 us -> 2.58 us  [over_core(): return lax.ppermute(x, 'ch', [(n, n ^ 1) for n in range(8)])]
  transfers between devices with their start and end apart: 18 -> 15, of which waited for: 9 -> 11; matrix products, arithmetic and copies ran while one was open for 6% -> 1% of each run, Pallas kernels for 13% -> 9%
where the time goes in v3:
time: 152 us
  waiting for transfers between devices  57.5 us (38%)
  starting transfers between devices  45.4 us (30%)
  blocking collectives  20.4 us (13%)
  Pallas kernels  19.2 us (13%)
  local copies, waits for them, and re-layouts  8.49 us (6%)
    all_to_all x1, blocking collectives, local(): return lax.all_to_all(result, 'ch', 0, 0, tiled=True)  20.4 us
    all_to_all x1, waiting for transfers between devices, local(): mixed = lax.all_to_all(mixed, every, 0, 0, tiled=True)  20.1 us
    pallas_call x5, Pallas kernels, call(): pl.pallas_call(kernel, out_shape=jax.ShapeDtypeStruct(shape, dtype), in_s...  19.2 us
    ppermute x3, waiting for transfers between devices, over_z(): return lax.ppermute(x, 'ch', [(n, (n + 2 * step) % 8) for n in range(8)])  12.9 us
    ppermute x6, waiting for transfers between devices, over_plane(): return lax.ppermute(x, 'ctx', pairs)  11.4 us
    ppermute x3, starting transfers between devices, over_z(): return lax.ppermute(x, 'ch', [(n, (n + 2 * step) % 8) for n in range(8)])  9.29 us
    all_to_all x1, starting transfers between devices, local(): shaped = lax.all_to_all(shaped, 'ctx', 0, 0, tiled=True)  8.97 us
    all_to_all x1, starting transfers between devices, local(): signal = lax.all_to_all(signal, every, 0, 0, tiled=True)  8.94 us
  transfers between devices with their start and end apart: 15, of which 11 were waited for; matrix products, arithmetic and copies ran while one was open for 1% of the time, Pallas kernels for 9%

profile of v3, /device:TPU:2, one launch (start us, length us, event | category | flops | bytes accessed | tf_op | source)
XLA Modules:
  0.0 151.6 jit_solution(14213161406586309578)
XLA Ops:
  0.0 1.3 copy.11.filters_ref
  2.0 2.0 %shard_map.100 = bf16[2048,128]{1,0:T(8,128)(2,1)} custom-call(f32[2048,24]{1,0:T(8,128)S(1)} %copy.11.filters_ref, f32[24,128]{1,0:T(8,128)S(1)} %copy-done.1), custom_call_target="tpu_custom_call" | custom-call | flops 33554432 | bytes 1257472 | tf_op jit(solution)/shard_map/pallas_call | solution.py:189
  4.0 9.0 %all-to-all-start = ((bf16[32,64,128]{2,1,0:T(8,128)(2,1)}), bf16[32,64,128]{2,1,0:T(8,128)(2,1)S(1)}, u32[]{:S(2)}, u32[]{:S(2)}) async-start(bf16[32,64,128]{2,1,0:T(8,128)(2,1)} %bitcast.3), calls=%async_computation | async-start | bytes 1048576 | tf_op jit(solution)/shard_map/all_to_all | solution.py:243
  13.3 5.5 %collective-permute-start.2 = (bf16[64,1024]{1,0:T(8,128)(2,1)S(1)}, bf16[64,1024]{1,0:T(8,128)(2,1)S(1)}, u32[]{:S(2)}, u32[]{:S(2)}) collective-permute-start(bf16[64,1024]{1,0:T(8,128)(2,1)S(1)} %get-tuple-element.30), channel_id=1, source_target_pairs={{0,6},{1,7},{2,0},{3,1},{4,2},{5,3},{6,4},{7,5},{8,14},{9,15},{10,... | collective-permute-start | bytes 393224 | tf_op jit(solution)/shard_map/ppermute | solution.py:203
  18.8 1.4 collective-permute-start.1
  20.2 2.4 %collective-permute-start = (bf16[64,1024]{1,0:T(8,128)(2,1)S(1)}, bf16[64,1024]{1,0:T(8,128)(2,1)S(1)}, u32[]{:S(2)}, u32[]{:S(2)}) collective-permute-start(bf16[64,1024]{1,0:T(8,128)(2,1)S(1)} %get-tuple-element.30), channel_id=1, source_target_pairs={{0,2},{1,3},{2,4},{3,5},{4,6},{5,7},{6,0},{7,1},{8,10},{9,11},{10,... | collective-permute-start | bytes 393224 | tf_op jit(solution)/shard_map/ppermute | solution.py:203
  22.6 11.3 %collective-permute-done.1 = bf16[64,1024]{1,0:T(8,128)(2,1)S(1)} collective-permute-done((bf16[64,1024]{1,0:T(8,128)(2,1)S(1)}, bf16[64,1024]{1,0:T(8,128)(2,1)S(1)}, u32[]{:S(2)}, u32[]{:S(2)}) %collective-permute-start.1) | collective-permute-done | bytes 131104 | tf_op jit(solution)/shard_map/ppermute | solution.py:203
  33.9 1.6 %collective-permute-done = bf16[64,1024]{1,0:T(8,128)(2,1)S(1)} collective-permute-done((bf16[64,1024]{1,0:T(8,128)(2,1)S(1)}, bf16[64,1024]{1,0:T(8,128)(2,1)S(1)}, u32[]{:S(2)}, u32[]{:S(2)}) %collective-permute-start) | collective-permute-done | bytes 131104 | tf_op jit(solution)/shard_map/ppermute | solution.py:203
  35.5 3.5 %all-to-all-start.1 = ((bf16[8,256,128]{2,1,0:T(8,128)(2,1)}), bf16[8,256,128]{2,1,0:T(8,128)(2,1)S(1)}, u32[]{:S(2)}, u32[]{:S(2)}) async-start(bf16[8,256,128]{2,1,0:T(8,128)(2,1)} %bitcast.11), calls=%async_computation.1 | async-start | bytes 1048576 | tf_op jit(solution)/shard_map/all_to_all | solution.py:248
  40.2 1.6 %collective-permute-start.4 = (bf16[128,1024]{1,0:T(8,128)(2,1)S(1)}, bf16[128,1024]{1,0:T(8,128)(2,1)S(1)}, u32[]{:S(2)}, u32[]{:S(2)}) collective-permute-start(bf16[128,1024]{1,0:T(8,128)(2,1)S(1)} %bitcast.32), channel_id=1, source_target_pairs={{0,64},{8,72},{16,80},{24,88},{32,96},{40,104},{48,112},{56,120},{... | collective-permute-start | bytes 786440 | tf_op jit(solution)/shard_map/ppermute | solution.py:216
  41.9 1.5 collective-permute-start.3
  43.3 5.1 %collective-permute-done.5 = bf16[128,1024]{1,0:T(8,128)(2,1)S(1)} collective-permute-done((bf16[128,1024]{1,0:T(8,128)(2,1)S(1)}, bf16[128,1024]{1,0:T(8,128)(2,1)S(1)}, u32[]{:S(2)}, u32[]{:S(2)}) %collective-permute-start.5) | collective-permute-done | bytes 262176 | tf_op jit(solution)/shard_map/ppermute | solution.py:216
  48.5 1.3 collective-permute-done.4
  49.8 1.1 collective-permute-done.3
  50.9 6.4 %all-to-all-done.1 = bf16[8,256,128]{2,1,0:T(8,128)(2,1)S(1)} async-done(((bf16[8,256,128]{2,1,0:T(8,128)(2,1)}), bf16[8,256,128]{2,1,0:T(8,128)(2,1)S(1)}, u32[]{:S(2)}, u32[]{:S(2)}) %all-to-all-start.1) | async-done | bytes 524320 | tf_op jit(solution)/shard_map/all_to_all | solution.py:248
  57.4 2.6 %collective-permute-done.6.mate_ref = bf16[512,1024]{1,0:T(8,128)(2,1)S(1)} collective-permute-done((bf16[512,1024]{1,0:T(8,128)(2,1)S(1)}, bf16[512,1024]{1,0:T(8,128)(2,1)S(1)}, u32[]{:S(2)}, u32[]{:S(2)}) %collective-permute-start.6) | collective-permute-done | bytes 1048608 | tf_op jit(solution)/shard_map/ppermute | solution.py:207
  60.0 2.9 %shard_map.101 = bf16[2048,128]{1,0:T(8,128)(2,1)} custom-call(s32[3]{0:T(128)S(1)} %pad_add_fusion.place_ref, bf16[2048,128]{1,0:T(8,128)(2,1)S(1)} %bitcast.22, bf16[512,1024]{1,0:T(8,128)(2,1)S(1)} %pad_maximum_fusion.own_ref, bf16[512,1024]{1,0:T(8,128)(2,1)S(1)} %collective-permute-done.6.mate_ref), custom_call_target="tpu_custom_call" | custom-call | flops 536870912 | bytes 3670028 | tf_op jit(solution)/shard_map/pallas_call | solution.py:189
  62.9 8.9 %all-to-all-start.2 = ((bf16[256,8,128]{2,1,0:T(8,128)(2,1)}), bf16[256,8,128]{2,1,0:T(8,128)(2,1)}, u32[]{:S(2)}, u32[]{:S(2)}) async-start(bf16[256,8,128]{2,1,0:T(8,128)(2,1)} %bitcast.14), calls=%async_computation.2 | async-start | bytes 1048576 | tf_op jit(solution)/shard_map/all_to_all | solution.py:261
  71.8 1.5 %collective-permute-start.7 = (bf16[128,1024]{1,0:T(8,128)(2,1)}, bf16[128,1024]{1,0:T(8,128)(2,1)S(1)}, u32[]{:S(2)}, u32[]{:S(2)}) collective-permute-start(bf16[128,1024]{1,0:T(8,128)(2,1)} %bitcast.27), channel_id=1, source_target_pairs={{0,16},{8,24},{16,32},{24,40},{32,48},{40,56},{48,0},{56,8},{64,80... | collective-permute-start | bytes 786440 | tf_op jit(solution)/shard_map/ppermute | solution.py:216
  73.4 1.5 collective-permute-start.8
  75.4 1.2 copy-done.2
  77.7 1.0 copy-done.4
  78.7 2.8 %shard_map.102.refs_5_ = f32[4,256,512]{2,1,0:T(8,128)S(1)} custom-call(bf16[2048,128]{1,0:T(8,128)(2,1)S(1)} %bitcast.25, bf16[2,512,256]{2,1,0:T(8,128)(2,1)S(1)} %copy-done.4, bf16[2,512,512]{2,1,0:T(8,128)(2,1)S(1)} %copy-done.2, f32[2,256,256]{2,1,0:T(8,128)S(1)} %copy-done.3), custom_call_target="tpu_custom_call" | custom-call | flops 2147483648 | bytes 4718592 | tf_op jit(solution)/shard_map/pallas_call | solution.py:189
  81.5 1.3 copy-done.5
  82.9 1.6 %collective-permute-done.7 = bf16[128,1024]{1,0:T(8,128)(2,1)S(1)} collective-permute-done((bf16[128,1024]{1,0:T(8,128)(2,1)}, bf16[128,1024]{1,0:T(8,128)(2,1)S(1)}, u32[]{:S(2)}, u32[]{:S(2)}) %collective-permute-start.7) | collective-permute-done | bytes 262176 | tf_op jit(solution)/shard_map/ppermute | solution.py:216
  84.5 2.3 %collective-permute-done.8 = bf16[128,1024]{1,0:T(8,128)(2,1)S(1)} collective-permute-done((bf16[128,1024]{1,0:T(8,128)(2,1)}, bf16[128,1024]{1,0:T(8,128)(2,1)S(1)}, u32[]{:S(2)}, u32[]{:S(2)}) %collective-permute-start.8) | collective-permute-done | bytes 262176 | tf_op jit(solution)/shard_map/ppermute | solution.py:216
  86.9 4.1 %all-to-all-done.2 = bf16[256,8,128]{2,1,0:T(8,128)(2,1)} async-done(((bf16[256,8,128]{2,1,0:T(8,128)(2,1)}), bf16[256,8,128]{2,1,0:T(8,128)(2,1)}, u32[]{:S(2)}, u32[]{:S(2)}) %all-to-all-start.2) | async-done | bytes 524320 | tf_op jit(solution)/shard_map/all_to_all | solution.py:261
  91.1 10.2 %shard_map.103 = bf16[2048,128]{1,0:T(8,128)(2,1)} custom-call(bf16[2048,128]{1,0:T(8,128)(2,1)} %bitcast.15.refs_0_, bf16[2,512,256]{2,1,0:T(8,128)(2,1)} %constant.82.clone.refs_1_, f32[2,256,256]{2,1,0:T(8,128)} %constant.81.clone.turn_ref.refs_2_, bf16[2,512,512]{2,1,0:T(8,128)(2,1)} %constant.80.clone.inner_ref.refs_3_, ...), custom_call_target="tpu_custom_call" | custom-call | flops 4294967296 | bytes 6291456 | tf_op jit(solution)/shard_map/pallas_call | solution.py:189
  101.2 7.5 %all-to-all-start.3 = ((bf16[256,8,128]{2,1,0:T(8,128)(2,1)}), bf16[256,8,128]{2,1,0:T(8,128)(2,1)S(1)}, u32[]{:S(2)}, u32[]{:S(2)}) async-start(bf16[256,8,128]{2,1,0:T(8,128)(2,1)} %bitcast.35), calls=%async_computation.3 | async-start | bytes 1048576 | tf_op jit(solution)/shard_map/all_to_all | solution.py:267
  108.8 20.1 %all-to-all-done.3 = bf16[256,8,128]{2,1,0:T(8,128)(2,1)S(1)} async-done(((bf16[256,8,128]{2,1,0:T(8,128)(2,1)}), bf16[256,8,128]{2,1,0:T(8,128)(2,1)S(1)}, u32[]{:S(2)}, u32[]{:S(2)}) %all-to-all-start.3) | async-done | bytes 524320 | tf_op jit(solution)/shard_map/all_to_all | solution.py:267
  128.9 1.4 shard_map.104
  130.3 20.4 %all_to_all.58 = bf16[8,256,128]{2,1,0:T(8,128)(2,1)S(1)} all-to-all(bf16[8,256,128]{2,1,0:T(8,128)(2,1)S(1)} %bitcast.24), channel_id=1, replica_groups=mesh['ctx'=32,'ch'=8] {'ch'}, dimensions={0} | all-to-all | bytes 1048576 | tf_op jit(solution)/shard_map/all_to_all | solution.py:271
  (34 shorter events, 4.9 us)
Async XLA Ops:
  0.0 13.2 %copy-start = (bf16[128,1024]{1,0:T(8,128)(2,1)S(1)}, bf16[128,1024]{1,0:T(8,128)(2,1)}, u32[]{:S(2)}) copy-start(bf16[128,1024]{1,0:T(8,128)(2,1)} %param.14) | copy-start | bytes 786436
  0.0 13.0 %copy-start.7 = (bf16[1024,128]{1,0:T(8,128)(2,1)S(1)}, bf16[1024,128]{1,0:T(8,128)(2,1)}, u32[]{:S(2)}) copy-start(bf16[1024,128]{1,0:T(8,128)(2,1)} %param.11) | copy-start | bytes 786436
  1.3 0.7 copy-start.1
  4.0 31.5 %all-to-all-start = ((bf16[32,64,128]{2,1,0:T(8,128)(2,1)}), bf16[32,64,128]{2,1,0:T(8,128)(2,1)S(1)}, u32[]{:S(2)}, u32[]{:S(2)}) async-start(bf16[32,64,128]{2,1,0:T(8,128)(2,1)} %bitcast.3), calls=%async_computation | async-start | bytes 1048576 | tf_op jit(solution)/shard_map/all_to_all | solution.py:243
  13.3 9.3 %collective-permute-start.2 = (bf16[64,1024]{1,0:T(8,128)(2,1)S(1)}, bf16[64,1024]{1,0:T(8,128)(2,1)S(1)}, u32[]{:S(2)}, u32[]{:S(2)}) collective-permute-start(bf16[64,1024]{1,0:T(8,128)(2,1)S(1)} %get-tuple-element.30), channel_id=1, source_target_pairs={{0,6},{1,7},{2,0},{3,1},{4,2},{5,3},{6,4},{7,5},{8,14},{9,15},{10,... | collective-permute-start | bytes 393224 | tf_op jit(solution)/shard_map/ppermute | solution.py:203
  18.8 15.1 %collective-permute-start.1 = (bf16[64,1024]{1,0:T(8,128)(2,1)S(1)}, bf16[64,1024]{1,0:T(8,128)(2,1)S(1)}, u32[]{:S(2)}, u32[]{:S(2)}) collective-permute-start(bf16[64,1024]{1,0:T(8,128)(2,1)S(1)} %get-tuple-element.30), channel_id=1, source_target_pairs={{0,4},{1,5},{2,6},{3,7},{4,0},{5,1},{6,2},{7,3},{8,12},{9,13},{10,... | collective-permute-start | bytes 393224 | tf_op jit(solution)/shard_map/ppermute | solution.py:203
  20.2 15.2 %collective-permute-start = (bf16[64,1024]{1,0:T(8,128)(2,1)S(1)}, bf16[64,1024]{1,0:T(8,128)(2,1)S(1)}, u32[]{:S(2)}, u32[]{:S(2)}) collective-permute-start(bf16[64,1024]{1,0:T(8,128)(2,1)S(1)} %get-tuple-element.30), channel_id=1, source_target_pairs={{0,2},{1,3},{2,4},{3,5},{4,6},{5,7},{6,0},{7,1},{8,10},{9,11},{10,... | collective-permute-start | bytes 393224 | tf_op jit(solution)/shard_map/ppermute | solution.py:203
  35.5 21.8 %all-to-all-start.1 = ((bf16[8,256,128]{2,1,0:T(8,128)(2,1)}), bf16[8,256,128]{2,1,0:T(8,128)(2,1)S(1)}, u32[]{:S(2)}, u32[]{:S(2)}) async-start(bf16[8,256,128]{2,1,0:T(8,128)(2,1)} %bitcast.11), calls=%async_computation.1 | async-start | bytes 1048576 | tf_op jit(solution)/shard_map/all_to_all | solution.py:248
  39.8 8.6 %collective-permute-start.5 = (bf16[128,1024]{1,0:T(8,128)(2,1)S(1)}, bf16[128,1024]{1,0:T(8,128)(2,1)S(1)}, u32[]{:S(2)}, u32[]{:S(2)}) collective-permute-start(bf16[128,1024]{1,0:T(8,128)(2,1)S(1)} %bitcast.31), channel_id=1, source_target_pairs={{0,48},{8,56},{16,0},{24,8},{32,16},{40,24},{48,32},{56,40},{64,11... | collective-permute-start | bytes 786440 | tf_op jit(solution)/shard_map/ppermute | solution.py:216
  40.2 9.6 %collective-permute-start.4 = (bf16[128,1024]{1,0:T(8,128)(2,1)S(1)}, bf16[128,1024]{1,0:T(8,128)(2,1)S(1)}, u32[]{:S(2)}, u32[]{:S(2)}) collective-permute-start(bf16[128,1024]{1,0:T(8,128)(2,1)S(1)} %bitcast.32), channel_id=1, source_target_pairs={{0,64},{8,72},{16,80},{24,88},{32,96},{40,104},{48,112},{56,120},{... | collective-permute-start | bytes 786440 | tf_op jit(solution)/shard_map/ppermute | solution.py:216
  41.9 9.0 %collective-permute-start.3 = (bf16[128,1024]{1,0:T(8,128)(2,1)S(1)}, bf16[128,1024]{1,0:T(8,128)(2,1)S(1)}, u32[]{:S(2)}, u32[]{:S(2)}) collective-permute-start(bf16[128,1024]{1,0:T(8,128)(2,1)S(1)} %bitcast.33), channel_id=1, source_target_pairs={{0,16},{8,24},{16,32},{24,40},{32,48},{40,56},{48,0},{56,8},{64,80... | collective-permute-start | bytes 786440 | tf_op jit(solution)/shard_map/ppermute | solution.py:216
  57.3 2.7 %collective-permute-start.6 = (bf16[512,1024]{1,0:T(8,128)(2,1)S(1)}, bf16[512,1024]{1,0:T(8,128)(2,1)S(1)}, u32[]{:S(2)}, u32[]{:S(2)}) collective-permute-start(bf16[512,1024]{1,0:T(8,128)(2,1)S(1)} %pad_maximum_fusion.own_ref), channel_id=1, source_target_pairs={{0,1},{1,0},{2,3},{3,2},{4,5},{5,4},{6,7},{7,6},{8,9},{9,8},{10,11... | collective-permute-start | bytes 3145736 | tf_op jit(solution)/shard_map/ppermute | solution.py:207
  62.9 20.0 %copy-start.6 = (bf16[4,32,1024]{2,1,0:T(8,128)(2,1)S(1)}, bf16[4,32,1024]{2,1,0:T(8,128)(2,1)}, u32[]{:S(2)}) copy-start(bf16[4,32,1024]{2,1,0:T(8,128)(2,1)} %get-tuple-element.28) | copy-start | bytes 786436
  62.9 28.2 %all-to-all-start.2 = ((bf16[256,8,128]{2,1,0:T(8,128)(2,1)}), bf16[256,8,128]{2,1,0:T(8,128)(2,1)}, u32[]{:S(2)}, u32[]{:S(2)}) async-start(bf16[256,8,128]{2,1,0:T(8,128)(2,1)} %bitcast.14), calls=%async_computation.2 | async-start | bytes 1048576 | tf_op jit(solution)/shard_map/all_to_all | solution.py:261
  71.8 12.6 %collective-permute-start.7 = (bf16[128,1024]{1,0:T(8,128)(2,1)}, bf16[128,1024]{1,0:T(8,128)(2,1)S(1)}, u32[]{:S(2)}, u32[]{:S(2)}) collective-permute-start(bf16[128,1024]{1,0:T(8,128)(2,1)} %bitcast.27), channel_id=1, source_target_pairs={{0,16},{8,24},{16,32},{24,40},{32,48},{40,56},{48,0},{56,8},{64,80... | collective-permute-start | bytes 786440 | tf_op jit(solution)/shard_map/ppermute | solution.py:216
  73.4 13.4 %collective-permute-start.8 = (bf16[128,1024]{1,0:T(8,128)(2,1)}, bf16[128,1024]{1,0:T(8,128)(2,1)S(1)}, u32[]{:S(2)}, u32[]{:S(2)}) collective-permute-start(bf16[128,1024]{1,0:T(8,128)(2,1)} %bitcast.28), channel_id=1, source_target_pairs={{0,64},{8,72},{16,80},{24,88},{32,96},{40,104},{48,112},{56,120},{... | collective-permute-start | bytes 786440 | tf_op jit(solution)/shard_map/ppermute | solution.py:216
  74.8 12.0 %collective-permute-start.9 = (bf16[128,1024]{1,0:T(8,128)(2,1)}, bf16[128,1024]{1,0:T(8,128)(2,1)S(1)}, u32[]{:S(2)}, u32[]{:S(2)}) collective-permute-start(bf16[128,1024]{1,0:T(8,128)(2,1)} %bitcast.29), channel_id=1, source_target_pairs={{0,48},{8,56},{16,0},{24,8},{32,16},{40,24},{48,32},{56,40},{64,11... | collective-permute-start | bytes 786440 | tf_op jit(solution)/shard_map/ppermute | solution.py:216
  75.4 1.2 copy-start.2
  76.6 1.0 copy-start.3
  77.7 1.0 copy-start.4
  81.5 1.3 copy-start.5
  86.8 21.9 %collective-permute-start.10 = (bf16[512,1024]{1,0:T(8,128)(2,1)S(1)}, bf16[512,1024]{1,0:T(8,128)(2,1)S(1)}, u32[]{:S(2)}, u32[]{:S(2)}) collective-permute-start(bf16[512,1024]{1,0:T(8,128)(2,1)S(1)} %constant_dynamic-update-slice_fusion.own_ref), channel_id=1, source_target_pairs={{0,1},{1,0},{2,3},{3,2},{4,5},{5,4},{6,7},{7,6},{8,9},{9,8},{10,11... | collective-permute-start | bytes 3145736 | tf_op jit(solution)/shard_map/ppermute | solution.py:207
  101.2 27.7 %all-to-all-start.3 = ((bf16[256,8,128]{2,1,0:T(8,128)(2,1)}), bf16[256,8,128]{2,1,0:T(8,128)(2,1)S(1)}, u32[]{:S(2)}, u32[]{:S(2)}) async-start(bf16[256,8,128]{2,1,0:T(8,128)(2,1)} %bitcast.35), calls=%async_computation.3 | async-start | bytes 1048576 | tf_op jit(solution)/shard_map/all_to_all | solution.py:267

commit v4 on v2

--- a/solution.py
+++ b/solution.py
@@ -105,53 +105,60 @@
     return dot(high, inner_ref[0]) + (dot(low, inner_ref[0]) + dot(high, inner_ref[1]))
 
 
-def first_product(wide_ref, outer_ref, c):
-    x = jnp.concatenate(
-        [wide_ref[pl.ds(c * 2 + half, NB, stride=8), :] for half in range(2)], axis=1
-    ).astype(BF)
+def first_product(wide_ref, outer_ref):
+    x = jnp.concatenate([wide_ref[pl.ds(n, NB, stride=8), :] for n in range(8)], axis=1)
+    x = x.astype(BF)
     return dot(outer_ref[0], x) + dot(outer_ref[1], x)
+
+
+def channel(values, c):
+    return values[:, c * NB : (c + 1) * NB]
+
+
+def rows_of_channels(first, turn_ref):
+    pairs = [
+        spread(channel(first[:NB], c), channel(first[NB:], c), turn_ref, 1) for c in range(4)
+    ]
+    return [jnp.concatenate(part, axis=0) for part in zip(*pairs)]
 
 
 def filter_kernel(h_ref, outer_ref, inner_ref, turn_ref, out_ref, wide_ref):
     wide_ref[...] = h_ref[...].astype(F32)
-    for c in range(4):
-        first = first_product(wide_ref, outer_ref, c)
-        out_ref[c] = inner_product(*spread(first[:NB], first[NB:], turn_ref, 1), inner_ref)
+    high, low = rows_of_channels(first_product(wide_ref, outer_ref), turn_ref)
+    out_ref[...] = inner_product(high, low, inner_ref)
 
 
 def conv_kernel(*refs):
     sources, out_ref, wide_ref, held, sem = refs[:6], refs[6], refs[7], refs[8:14], refs[14]
-    pairs = list(zip(sources, held))[:5] + [(sources[5].at[c], held[5].at[c]) for c in range(4)]
-    copies = [pltpu.make_async_copy(*pair, sem.at[n]) for n, pair in enumerate(pairs)]
-    for n in (0, 1, 2, 3, 5, 4):
-        copies[n].start()
-    x_ref, outer_ref, turn_ref, inner_ref, back_ref, spec_ref = held
+    copies = [
+        pltpu.make_async_copy(source, into, sem.at[n])
+        for n, (source, into) in enumerate(zip(sources, held))
+    ]
+    for copy in copies:
+        copy.start()
+    x_ref, outer_ref, turn_ref, inner_ref, spec_ref, back_ref = held
     copies[0].wait()
     wide_ref[...] = x_ref[...].astype(F32)
     copies[1].wait()
-    for n in (6, 7, 8):
-        copies[n].start()
-    for c in range(4):
-        first = first_product(wide_ref, outer_ref, c)
-        if c == 0:
-            copies[2].wait()
-        high, low = spread(first[:NB], first[NB:], turn_ref, 1)
-        if c == 0:
-            copies[3].wait()
-        got = inner_product(high, low, inner_ref)
-        copies[5 + c].wait()
-        re, im = got[:, :NB], got[:, NB:]
-        hre, him = spec_ref[c, :, :NB], spec_ref[c, :, NB:]
-        high, low = split(jnp.concatenate([re * hre - im * him, -(re * him + im * hre)], axis=1))
-        half = inner_product(high, low, inner_ref)
-        high, low = spread(half[:, :NB], half[:, NB:], turn_ref, 0)
-        if c == 0:
-            copies[4].wait()
-        y = dot(back_ref[0], high) + (dot(back_ref[0], low) + dot(back_ref[1], high))
-        for part in range(2):
-            wide_ref[pl.ds(c * 2 + part, NB, stride=8), :] = y[
-                :, part * LANES : (part + 1) * LANES
-            ]
+    first = first_product(wide_ref, outer_ref)
+    copies[2].wait()
+    high, low = rows_of_channels(first, turn_ref)
+    copies[3].wait()
+    got = inner_product(high, low, inner_ref)
+    copies[4].wait()
+    re, im = got[:, :NB], got[:, NB:]
+    hre, him = spec_ref[:, :NB], spec_ref[:, NB:]
+    high, low = split(jnp.concatenate([re * hre - im * him, -(re * him + im * hre)], axis=1))
+    half = inner_product(high, low, inner_ref)
+    pairs = [
+        spread(half[c * NB : (c + 1) * NB, :NB], half[c * NB : (c + 1) * NB, NB:], turn_ref, 0)
+        for c in range(4)
+    ]
+    high, low = [jnp.concatenate(part, axis=1) for part in zip(*pairs)]
+    copies[5].wait()
+    y = dot(back_ref[0], high) + (dot(back_ref[0], low) + dot(back_ref[1], high))
+    for n in range(8):
+        wide_ref[pl.ds(n, NB, stride=8), :] = y[:, n * LANES : (n + 1) * LANES]
     out_ref[...] = wide_ref[...].astype(out_ref.dtype)
 
 
@@ -238,7 +245,7 @@
     shaped = call(shape_kernel, wide, BF, wide, 2**25, filters, w_filter)
     shaped = lax.all_to_all(shaped, "ctx", 0, 0, tiled=True)
     spectrum = call(
-        filter_kernel, (4, NB, 2 * NB), F32, wide, 2**31, shaped, outer, inner, turn
+        filter_kernel, (4 * NB, 2 * NB), F32, wide, 2**31, shaped, outer, inner, turn
     )
     w_out, tokens = lax.optimization_barrier((w_out, tokens))
     out_own, out_mate = gather_rows(lax.dynamic_slice_in_dim(w_out, 32 * quarter, 32, 0))
@@ -246,8 +253,8 @@
         project_kernel, wide, BF, blocks, 2**29, place, tokens, in_own, in_mate, scalars=True
     )
     signal = lax.all_to_all(signal, every, 0, 0, tiled=True)
-    operands = [signal, outer_x, turn, inner, back, spectrum]
-    fetched = [pltpu.VMEM(a.shape, a.dtype) for a in operands] + [pltpu.SemaphoreType.DMA((9,))]
+    operands = [signal, outer_x, turn, inner, spectrum, back]
+    fetched = [pltpu.VMEM(a.shape, a.dtype) for a in operands] + [pltpu.SemaphoreType.DMA((6,))]
     mixed = call(
         conv_kernel, wide, BF, wide, 2**32, *operands, fetched=fetched, limit=60 * 2**20
     )

time: 146 us -> 145 us (level)
  Pallas kernels: 20.2 us -> 18.3 us
    pallas_call x5, Pallas kernels: 20.2 us -> 18.3 us  [call(): pl.pallas_call(kernel, out_shape=jax.ShapeDtypeStruct(shape, dtype), in_s...]
  transfers between devices with their start and end apart: 18 -> 18, of which waited for: 9 -> 9; matrix products, arithmetic and copies ran while one was open for 6% -> 6% of each run, Pallas kernels for 13% -> 12%
where the time goes in v4:
time: 145 us; the launch traced here: 144 us
  starting transfers between devices  53.5 us (37%)
  waiting for transfers between devices  38.4 us (26%)
  blocking collectives  20.4 us (14%)
  Pallas kernels  18.3 us (13%)
  local copies, waits for them, and re-layouts  12.2 us (8%)
    all_to_all x1, blocking collectives, local(): return lax.all_to_all(result, 'ch', 0, 0, tiled=True)  20.4 us
    all_to_all x1, waiting for transfers between devices, local(): mixed = lax.all_to_all(mixed, every, 0, 0, tiled=True)  20.1 us
    pallas_call x5, Pallas kernels, call(): pl.pallas_call(kernel, out_shape=jax.ShapeDtypeStruct(shape, dtype), in_s...  18.3 us
    ppermute x6, starting transfers between devices, over_z(): return lax.ppermute(x, 'ch', [(n, (n + 2 * step) % 8) for n in range(8)])  17.8 us
    unnamed x29, local copies, waits for them, and re-layouts  11.3 us
    ppermute x6, waiting for transfers between devices, over_plane(): return lax.ppermute(x, 'ctx', pairs)  9.02 us
    all_to_all x1, starting transfers between devices, local(): signal = lax.all_to_all(signal, every, 0, 0, tiled=True)  8.56 us
    all_to_all x1, starting transfers between devices, local(): mixed = lax.all_to_all(mixed, every, 0, 0, tiled=True)  8.08 us
  transfers between devices with their start and end apart: 18, of which 9 were waited for; matrix products, arithmetic and copies ran while one was open for 6% of the time, Pallas kernels for 12%

profile of v4, /device:TPU:2, one launch (start us, length us, event | category | flops | bytes accessed | tf_op | source)
XLA Modules:
  0.0 144.0 jit_solution(8795877106600319635)
XLA Ops:
  0.0 0.9 copy-done
  1.2 3.3 %collective-permute-start = (bf16[32,1024]{1,0:T(8,128)(2,1)S(1)}, bf16[32,1024]{1,0:T(8,128)(2,1)S(1)}, u32[]{:S(2)}, u32[]{:S(2)}) collective-permute-start(bf16[32,1024]{1,0:T(8,128)(2,1)S(1)} %bitcast.20), channel_id=1, source_target_pairs={{0,2},{1,3},{2,4},{3,5},{4,6},{5,7},{6,0},{7,1},{8,10},{9,11},{10,... | collective-permute-start | bytes 196616 | tf_op jit(solution)/shard_map/ppermute | solution.py:210
  4.6 5.4 %collective-permute-start.1 = (bf16[32,1024]{1,0:T(8,128)(2,1)S(1)}, bf16[32,1024]{1,0:T(8,128)(2,1)S(1)}, u32[]{:S(2)}, u32[]{:S(2)}) collective-permute-start(bf16[32,1024]{1,0:T(8,128)(2,1)S(1)} %bitcast.21), channel_id=1, source_target_pairs={{0,4},{1,5},{2,6},{3,7},{4,0},{5,1},{6,2},{7,3},{8,12},{9,13},{10,... | collective-permute-start | bytes 196616 | tf_op jit(solution)/shard_map/ppermute | solution.py:210
  10.0 2.7 %collective-permute-start.2 = (bf16[32,1024]{1,0:T(8,128)(2,1)S(1)}, bf16[32,1024]{1,0:T(8,128)(2,1)S(1)}, u32[]{:S(2)}, u32[]{:S(2)}) collective-permute-start(bf16[32,1024]{1,0:T(8,128)(2,1)S(1)} %bitcast.22), channel_id=1, source_target_pairs={{0,6},{1,7},{2,0},{3,1},{4,2},{5,3},{6,4},{7,5},{8,14},{9,15},{10,... | collective-permute-start | bytes 196616 | tf_op jit(solution)/shard_map/ppermute | solution.py:210
  12.6 3.5 %all-to-all-start = ((bf16[8,256,128]{2,1,0:T(8,128)(2,1)}), bf16[8,256,128]{2,1,0:T(8,128)(2,1)S(1)}, u32[]{:S(2)}, u32[]{:S(2)}) async-start(bf16[8,256,128]{2,1,0:T(8,128)(2,1)} %bitcast.24), calls=%async_computation | async-start | bytes 1048576 | tf_op jit(solution)/shard_map/all_to_all | solution.py:244
  16.9 1.6 %collective-permute-start.3 = (bf16[128,1024]{1,0:T(8,128)(2,1)S(1)}, bf16[128,1024]{1,0:T(8,128)(2,1)S(1)}, u32[]{:S(2)}, u32[]{:S(2)}) collective-permute-start(bf16[128,1024]{1,0:T(8,128)(2,1)S(1)} %pad_maximum_fusion), channel_id=1, source_target_pairs={{0,16},{8,24},{16,32},{24,40},{32,48},{40,56},{48,0},{56,8},{64,80... | collective-permute-start | bytes 786440 | tf_op jit(solution)/shard_map/ppermute | solution.py:223
  18.5 1.6 %collective-permute-start.4 = (bf16[128,1024]{1,0:T(8,128)(2,1)S(1)}, bf16[128,1024]{1,0:T(8,128)(2,1)S(1)}, u32[]{:S(2)}, u32[]{:S(2)}) collective-permute-start(bf16[128,1024]{1,0:T(8,128)(2,1)S(1)} %pad_maximum_fusion), channel_id=1, source_target_pairs={{0,64},{8,72},{16,80},{24,88},{32,96},{40,104},{48,112},{56,120},{... | collective-permute-start | bytes 786440 | tf_op jit(solution)/shard_map/ppermute | solution.py:223
  22.5 3.0 %collective-permute-done.3 = bf16[128,1024]{1,0:T(8,128)(2,1)S(1)} collective-permute-done((bf16[128,1024]{1,0:T(8,128)(2,1)S(1)}, bf16[128,1024]{1,0:T(8,128)(2,1)S(1)}, u32[]{:S(2)}, u32[]{:S(2)}) %collective-permute-start.3) | collective-permute-done | bytes 262176 | tf_op jit(solution)/shard_map/ppermute | solution.py:223
  26.2 1.8 %collective-permute-done.4 = bf16[128,1024]{1,0:T(8,128)(2,1)S(1)} collective-permute-done((bf16[128,1024]{1,0:T(8,128)(2,1)S(1)}, bf16[128,1024]{1,0:T(8,128)(2,1)S(1)}, u32[]{:S(2)}, u32[]{:S(2)}) %collective-permute-start.4) | collective-permute-done | bytes 262176 | tf_op jit(solution)/shard_map/ppermute | solution.py:223
  29.8 2.0 %shard_map.101 = bf16[2048,128]{1,0:T(8,128)(2,1)} custom-call(f32[2048,24]{1,0:T(8,128)S(1)} %copy.12.filters_ref, f32[24,128]{1,0:T(8,128)S(1)} %copy-done.1), custom_call_target="tpu_custom_call" | custom-call | flops 33554432 | bytes 1257472 | tf_op jit(solution)/shard_map/pallas_call | solution.py:196
  31.8 2.4 %all-to-all-done = bf16[8,256,128]{2,1,0:T(8,128)(2,1)S(1)} async-done(((bf16[8,256,128]{2,1,0:T(8,128)(2,1)}), bf16[8,256,128]{2,1,0:T(8,128)(2,1)S(1)}, u32[]{:S(2)}, u32[]{:S(2)}) %all-to-all-start) | async-done | bytes 524320 | tf_op jit(solution)/shard_map/all_to_all | solution.py:244
  34.2 8.0 %all-to-all-start.2 = ((bf16[32,64,128]{2,1,0:T(8,128)(2,1)}), bf16[32,64,128]{2,1,0:T(8,128)(2,1)S(1)}, u32[]{:S(2)}, u32[]{:S(2)}) async-start(bf16[32,64,128]{2,1,0:T(8,128)(2,1)} %bitcast.8), calls=%async_computation.2 | async-start | bytes 1048576 | tf_op jit(solution)/shard_map/all_to_all | solution.py:246
  42.3 0.8 constant_dynamic-update-slice_fusion.13
  43.3 3.0 %collective-permute-start.8 = (bf16[32,1024]{1,0:T(8,128)(2,1)S(1)}, bf16[32,1024]{1,0:T(8,128)(2,1)}, u32[]{:S(2)}, u32[]{:S(2)}) collective-permute-start(bf16[32,1024]{1,0:T(8,128)(2,1)S(1)} %get-tuple-element.10), channel_id=1, source_target_pairs={{0,4},{1,5},{2,6},{3,7},{4,0},{5,1},{6,2},{7,3},{8,12},{9,13},{10,... | collective-permute-start | bytes 196616 | tf_op jit(solution)/shard_map/ppermute | solution.py:210
  46.3 3.3 %collective-permute-start.9 = (bf16[32,1024]{1,0:T(8,128)(2,1)S(1)}, bf16[32,1024]{1,0:T(8,128)(2,1)}, u32[]{:S(2)}, u32[]{:S(2)}) collective-permute-start(bf16[32,1024]{1,0:T(8,128)(2,1)S(1)} %get-tuple-element.10), channel_id=1, source_target_pairs={{0,6},{1,7},{2,0},{3,1},{4,2},{5,3},{6,4},{7,5},{8,14},{9,15},{10,... | collective-permute-start | bytes 196616 | tf_op jit(solution)/shard_map/ppermute | solution.py:210
  49.5 3.9 %shard_map.100 = bf16[2048,128]{1,0:T(8,128)(2,1)} custom-call(s32[3]{0:T(128)S(1)} %pad_add_fusion.place_ref, bf16[2048,128]{1,0:T(8,128)(2,1)S(1)} %bitcast.15, bf16[512,1024]{1,0:T(8,128)(2,1)} %constant_dynamic-update-slice_fusion.own_ref, bf16[512,1024]{1,0:T(8,128)(2,1)} %collective-permute-done.6.mate_ref), custom_call_target="tpu_custom_call" | custom-call | flops 536870912 | bytes 3670028 | tf_op jit(solution)/shard_map/pallas_call | solution.py:196
  53.4 3.5 %all-to-all-done.2 = bf16[32,64,128]{2,1,0:T(8,128)(2,1)S(1)} async-done(((bf16[32,64,128]{2,1,0:T(8,128)(2,1)}), bf16[32,64,128]{2,1,0:T(8,128)(2,1)S(1)}, u32[]{:S(2)}, u32[]{:S(2)}) %all-to-all-start.2) | async-done | bytes 524320 | tf_op jit(solution)/shard_map/all_to_all | solution.py:246
  56.9 8.6 %all-to-all-start.1 = ((bf16[256,8,128]{2,1,0:T(8,128)(2,1)}), bf16[256,8,128]{2,1,0:T(8,128)(2,1)}, u32[]{:S(2)}, u32[]{:S(2)}) async-start(bf16[256,8,128]{2,1,0:T(8,128)(2,1)} %bitcast.6), calls=%async_computation.1 | async-start | bytes 1048576 | tf_op jit(solution)/shard_map/all_to_all | solution.py:255
  65.5 0.9 pad_maximum_fusion.1
  66.4 1.7 %collective-permute-start.10 = (bf16[128,1024]{1,0:T(8,128)(2,1)S(1)}, bf16[128,1024]{1,0:T(8,128)(2,1)S(1)}, u32[]{:S(2)}, u32[]{:S(2)}) collective-permute-start(bf16[128,1024]{1,0:T(8,128)(2,1)S(1)} %pad_maximum_fusion.1), channel_id=1, source_target_pairs={{0,16},{8,24},{16,32},{24,40},{32,48},{40,56},{48,0},{56,8},{64,80... | collective-permute-start | bytes 786440 | tf_op jit(solution)/shard_map/ppermute | solution.py:223
  68.1 1.5 %collective-permute-start.11 = (bf16[128,1024]{1,0:T(8,128)(2,1)S(1)}, bf16[128,1024]{1,0:T(8,128)(2,1)S(1)}, u32[]{:S(2)}, u32[]{:S(2)}) collective-permute-start(bf16[128,1024]{1,0:T(8,128)(2,1)S(1)} %pad_maximum_fusion.1), channel_id=1, source_target_pairs={{0,64},{8,72},{16,80},{24,88},{32,96},{40,104},{48,112},{56,120},{... | collective-permute-start | bytes 786440 | tf_op jit(solution)/shard_map/ppermute | solution.py:223
  71.8 1.2 copy-done.2
  73.1 2.7 %shard_map.102.refs_4_ = f32[1024,512]{1,0:T(8,128)S(1)} custom-call(bf16[2048,128]{1,0:T(8,128)(2,1)S(1)} %bitcast.18, bf16[2,512,256]{2,1,0:T(8,128)(2,1)S(1)} %copy-done.4, bf16[2,512,512]{2,1,0:T(8,128)(2,1)S(1)} %copy-done.2, f32[2,256,256]{2,1,0:T(8,128)S(1)} %copy-done.3), custom_call_target="tpu_custom_call" | custom-call | flops 2147483648 | bytes 4718592 | tf_op jit(solution)/shard_map/pallas_call | solution.py:196
  75.7 1.3 copy-done.5
  77.1 1.5 %collective-permute-done.10 = bf16[128,1024]{1,0:T(8,128)(2,1)S(1)} collective-permute-done((bf16[128,1024]{1,0:T(8,128)(2,1)S(1)}, bf16[128,1024]{1,0:T(8,128)(2,1)S(1)}, u32[]{:S(2)}, u32[]{:S(2)}) %collective-permute-start.10) | collective-permute-done | bytes 262176 | tf_op jit(solution)/shard_map/ppermute | solution.py:223
  78.6 2.7 %collective-permute-done.11 = bf16[128,1024]{1,0:T(8,128)(2,1)S(1)} collective-permute-done((bf16[128,1024]{1,0:T(8,128)(2,1)S(1)}, bf16[128,1024]{1,0:T(8,128)(2,1)S(1)}, u32[]{:S(2)}, u32[]{:S(2)}) %collective-permute-start.11) | collective-permute-done | bytes 262176 | tf_op jit(solution)/shard_map/ppermute | solution.py:223
  81.5 3.2 %all-to-all-done.1 = bf16[256,8,128]{2,1,0:T(8,128)(2,1)} async-done(((bf16[256,8,128]{2,1,0:T(8,128)(2,1)}), bf16[256,8,128]{2,1,0:T(8,128)(2,1)}, u32[]{:S(2)}, u32[]{:S(2)}) %all-to-all-start.1) | async-done | bytes 524320 | tf_op jit(solution)/shard_map/all_to_all | solution.py:255
  84.7 8.4 %shard_map.103 = bf16[2048,128]{1,0:T(8,128)(2,1)} custom-call(bf16[2048,128]{1,0:T(8,128)(2,1)} %bitcast.7.refs_0_, bf16[2,512,256]{2,1,0:T(8,128)(2,1)} %constant.82.clone.refs_1_, f32[2,256,256]{2,1,0:T(8,128)} %constant.81.clone.turn_ref.refs_2_, bf16[2,512,512]{2,1,0:T(8,128)(2,1)} %constant.80.clone.inner_ref.refs_3_, f32[1024,512]{1,0:T(8,128)} %copy-done.5, ...), custom_call_target="tpu_custom_call" | custom-call | flops 4294967296 | bytes 6291456 | tf_op jit(solution)/shard_map/pallas_call | solution.py:196
  93.1 8.1 %all-to-all-start.3 = ((bf16[256,8,128]{2,1,0:T(8,128)(2,1)}), bf16[256,8,128]{2,1,0:T(8,128)(2,1)S(1)}, u32[]{:S(2)}, u32[]{:S(2)}) async-start(bf16[256,8,128]{2,1,0:T(8,128)(2,1)} %bitcast.25), calls=%async_computation.3 | async-start | bytes 1048576 | tf_op jit(solution)/shard_map/all_to_all | solution.py:261
  101.2 20.1 %all-to-all-done.3 = bf16[256,8,128]{2,1,0:T(8,128)(2,1)S(1)} async-done(((bf16[256,8,128]{2,1,0:T(8,128)(2,1)}), bf16[256,8,128]{2,1,0:T(8,128)(2,1)S(1)}, u32[]{:S(2)}, u32[]{:S(2)}) %all-to-all-start.3) | async-done | bytes 524320 | tf_op jit(solution)/shard_map/all_to_all | solution.py:261
  121.4 1.4 shard_map.104
  122.8 20.4 %all_to_all.57 = bf16[8,256,128]{2,1,0:T(8,128)(2,1)S(1)} all-to-all(bf16[8,256,128]{2,1,0:T(8,128)(2,1)S(1)} %bitcast.17), channel_id=1, replica_groups=mesh['ctx'=32,'ch'=8] {'ch'}, dimensions={0} | all-to-all | bytes 1048576 | tf_op jit(solution)/shard_map/all_to_all | solution.py:265
  (45 shorter events, 9.4 us)
Async XLA Ops:
  0.0 1.0 copy-start
  1.1 28.3 %copy-start.6 = (f32[2048,24]{0,1:T(8,128)S(1)}, f32[2048,24]{0,1:T(8,128)}, u32[]{:S(2)}) copy-start(f32[2048,24]{0,1:T(8,128)} %param.12) | copy-start | bytes 589828
  1.2 15.5 %collective-permute-start = (bf16[32,1024]{1,0:T(8,128)(2,1)S(1)}, bf16[32,1024]{1,0:T(8,128)(2,1)S(1)}, u32[]{:S(2)}, u32[]{:S(2)}) collective-permute-start(bf16[32,1024]{1,0:T(8,128)(2,1)S(1)} %bitcast.20), channel_id=1, source_target_pairs={{0,2},{1,3},{2,4},{3,5},{4,6},{5,7},{6,0},{7,1},{8,10},{9,11},{10,... | collective-permute-start | bytes 196616 | tf_op jit(solution)/shard_map/ppermute | solution.py:210
  4.6 12.2 %collective-permute-start.1 = (bf16[32,1024]{1,0:T(8,128)(2,1)S(1)}, bf16[32,1024]{1,0:T(8,128)(2,1)S(1)}, u32[]{:S(2)}, u32[]{:S(2)}) collective-permute-start(bf16[32,1024]{1,0:T(8,128)(2,1)S(1)} %bitcast.21), channel_id=1, source_target_pairs={{0,4},{1,5},{2,6},{3,7},{4,0},{5,1},{6,2},{7,3},{8,12},{9,13},{10,... | collective-permute-start | bytes 196616 | tf_op jit(solution)/shard_map/ppermute | solution.py:210
  10.0 6.9 %collective-permute-start.2 = (bf16[32,1024]{1,0:T(8,128)(2,1)S(1)}, bf16[32,1024]{1,0:T(8,128)(2,1)S(1)}, u32[]{:S(2)}, u32[]{:S(2)}) collective-permute-start(bf16[32,1024]{1,0:T(8,128)(2,1)S(1)} %bitcast.22), channel_id=1, source_target_pairs={{0,6},{1,7},{2,0},{3,1},{4,2},{5,3},{6,4},{7,5},{8,14},{9,15},{10,... | collective-permute-start | bytes 196616 | tf_op jit(solution)/shard_map/ppermute | solution.py:210
  12.6 21.5 %all-to-all-start = ((bf16[8,256,128]{2,1,0:T(8,128)(2,1)}), bf16[8,256,128]{2,1,0:T(8,128)(2,1)S(1)}, u32[]{:S(2)}, u32[]{:S(2)}) async-start(bf16[8,256,128]{2,1,0:T(8,128)(2,1)} %bitcast.24), calls=%async_computation | async-start | bytes 1048576 | tf_op jit(solution)/shard_map/all_to_all | solution.py:244
  16.1 13.6 %copy-start.1 = (f32[24,128]{1,0:T(8,128)S(1)}, f32[24,128]{1,0:T(8,128)}, u32[]{:S(2)}) copy-start(f32[24,128]{1,0:T(8,128)} %w_ref.1) | copy-start | bytes 36868
  16.9 8.6 %collective-permute-start.3 = (bf16[128,1024]{1,0:T(8,128)(2,1)S(1)}, bf16[128,1024]{1,0:T(8,128)(2,1)S(1)}, u32[]{:S(2)}, u32[]{:S(2)}) collective-permute-start(bf16[128,1024]{1,0:T(8,128)(2,1)S(1)} %pad_maximum_fusion), channel_id=1, source_target_pairs={{0,16},{8,24},{16,32},{24,40},{32,48},{40,56},{48,0},{56,8},{64,80... | collective-permute-start | bytes 786440 | tf_op jit(solution)/shard_map/ppermute | solution.py:223
  18.5 9.5 %collective-permute-start.4 = (bf16[128,1024]{1,0:T(8,128)(2,1)S(1)}, bf16[128,1024]{1,0:T(8,128)(2,1)S(1)}, u32[]{:S(2)}, u32[]{:S(2)}) collective-permute-start(bf16[128,1024]{1,0:T(8,128)(2,1)S(1)} %pad_maximum_fusion), channel_id=1, source_target_pairs={{0,64},{8,72},{16,80},{24,88},{32,96},{40,104},{48,112},{56,120},{... | collective-permute-start | bytes 786440 | tf_op jit(solution)/shard_map/ppermute | solution.py:223
  20.1 8.7 %collective-permute-start.5 = (bf16[128,1024]{1,0:T(8,128)(2,1)S(1)}, bf16[128,1024]{1,0:T(8,128)(2,1)S(1)}, u32[]{:S(2)}, u32[]{:S(2)}) collective-permute-start(bf16[128,1024]{1,0:T(8,128)(2,1)S(1)} %pad_maximum_fusion), channel_id=1, source_target_pairs={{0,48},{8,56},{16,0},{24,8},{32,16},{40,24},{48,32},{56,40},{64,11... | collective-permute-start | bytes 786440 | tf_op jit(solution)/shard_map/ppermute | solution.py:223
  29.4 20.1 %collective-permute-start.6 = (bf16[512,1024]{1,0:T(8,128)(2,1)}, bf16[512,1024]{1,0:T(8,128)(2,1)}, u32[]{:S(2)}, u32[]{:S(2)}) collective-permute-start(bf16[512,1024]{1,0:T(8,128)(2,1)} %constant_dynamic-update-slice_fusion.own_ref), channel_id=1, source_target_pairs={{0,1},{1,0},{2,3},{3,2},{4,5},{5,4},{6,7},{7,6},{8,9},{9,8},{10,11... | collective-permute-start | bytes 3145736 | tf_op jit(solution)/shard_map/ppermute | solution.py:214
  34.2 22.7 %all-to-all-start.2 = ((bf16[32,64,128]{2,1,0:T(8,128)(2,1)}), bf16[32,64,128]{2,1,0:T(8,128)(2,1)S(1)}, u32[]{:S(2)}, u32[]{:S(2)}) async-start(bf16[32,64,128]{2,1,0:T(8,128)(2,1)} %bitcast.8), calls=%async_computation.2 | async-start | bytes 1048576 | tf_op jit(solution)/shard_map/all_to_all | solution.py:246
  43.1 28.7 %copy-start.3 = (f32[2,256,256]{2,1,0:T(8,128)S(1)}, f32[2,256,256]{2,1,0:T(8,128)}, u32[]{:S(2)}) copy-start(f32[2,256,256]{2,1,0:T(8,128)} %constant.81.clone.turn_ref.refs_2_) | copy-start | bytes 1572868
  43.1 28.7 %copy-start.4 = (bf16[2,512,256]{2,1,0:T(8,128)(2,1)S(1)}, bf16[2,512,256]{2,1,0:T(8,128)(2,1)}, u32[]{:S(2)}) copy-start(bf16[2,512,256]{2,1,0:T(8,128)(2,1)} %constant.79.clone.outer_ref) | copy-start | bytes 1572868
  43.2 22.3 %collective-permute-start.7 = (bf16[32,1024]{1,0:T(8,128)(2,1)S(1)}, bf16[32,1024]{1,0:T(8,128)(2,1)S(1)}, u32[]{:S(2)}, u32[]{:S(2)}) collective-permute-start(bf16[32,1024]{1,0:T(8,128)(2,1)S(1)} %get-tuple-element.10), channel_id=1, source_target_pairs={{0,2},{1,3},{2,4},{3,5},{4,6},{5,7},{6,0},{7,1},{8,10},{9,11},{10,... | collective-permute-start | bytes 196616 | tf_op jit(solution)/shard_map/ppermute | solution.py:210
  43.3 22.2 %collective-permute-start.8 = (bf16[32,1024]{1,0:T(8,128)(2,1)S(1)}, bf16[32,1024]{1,0:T(8,128)(2,1)}, u32[]{:S(2)}, u32[]{:S(2)}) collective-permute-start(bf16[32,1024]{1,0:T(8,128)(2,1)S(1)} %get-tuple-element.10), channel_id=1, source_target_pairs={{0,4},{1,5},{2,6},{3,7},{4,0},{5,1},{6,2},{7,3},{8,12},{9,13},{10,... | collective-permute-start | bytes 196616 | tf_op jit(solution)/shard_map/ppermute | solution.py:210
  46.3 19.2 %collective-permute-start.9 = (bf16[32,1024]{1,0:T(8,128)(2,1)S(1)}, bf16[32,1024]{1,0:T(8,128)(2,1)}, u32[]{:S(2)}, u32[]{:S(2)}) collective-permute-start(bf16[32,1024]{1,0:T(8,128)(2,1)S(1)} %get-tuple-element.10), channel_id=1, source_target_pairs={{0,6},{1,7},{2,0},{3,1},{4,2},{5,3},{6,4},{7,5},{8,14},{9,15},{10,... | collective-permute-start | bytes 196616 | tf_op jit(solution)/shard_map/ppermute | solution.py:210
  56.9 27.8 %all-to-all-start.1 = ((bf16[256,8,128]{2,1,0:T(8,128)(2,1)}), bf16[256,8,128]{2,1,0:T(8,128)(2,1)}, u32[]{:S(2)}, u32[]{:S(2)}) async-start(bf16[256,8,128]{2,1,0:T(8,128)(2,1)} %bitcast.6), calls=%async_computation.1 | async-start | bytes 1048576 | tf_op jit(solution)/shard_map/all_to_all | solution.py:255
  66.4 12.2 %collective-permute-start.10 = (bf16[128,1024]{1,0:T(8,128)(2,1)S(1)}, bf16[128,1024]{1,0:T(8,128)(2,1)S(1)}, u32[]{:S(2)}, u32[]{:S(2)}) collective-permute-start(bf16[128,1024]{1,0:T(8,128)(2,1)S(1)} %pad_maximum_fusion.1), channel_id=1, source_target_pairs={{0,16},{8,24},{16,32},{24,40},{32,48},{40,56},{48,0},{56,8},{64,80... | collective-permute-start | bytes 786440 | tf_op jit(solution)/shard_map/ppermute | solution.py:223
  68.1 13.2 %collective-permute-start.11 = (bf16[128,1024]{1,0:T(8,128)(2,1)S(1)}, bf16[128,1024]{1,0:T(8,128)(2,1)S(1)}, u32[]{:S(2)}, u32[]{:S(2)}) collective-permute-start(bf16[128,1024]{1,0:T(8,128)(2,1)S(1)} %pad_maximum_fusion.1), channel_id=1, source_target_pairs={{0,64},{8,72},{16,80},{24,88},{32,96},{40,104},{48,112},{56,120},{... | collective-permute-start | bytes 786440 | tf_op jit(solution)/shard_map/ppermute | solution.py:223
  69.6 11.8 %collective-permute-start.12 = (bf16[128,1024]{1,0:T(8,128)(2,1)S(1)}, bf16[128,1024]{1,0:T(8,128)(2,1)S(1)}, u32[]{:S(2)}, u32[]{:S(2)}) collective-permute-start(bf16[128,1024]{1,0:T(8,128)(2,1)S(1)} %pad_maximum_fusion.1), channel_id=1, source_target_pairs={{0,48},{8,56},{16,0},{24,8},{32,16},{40,24},{48,32},{56,40},{64,11... | collective-permute-start | bytes 786440 | tf_op jit(solution)/shard_map/ppermute | solution.py:223
  71.8 1.2 copy-start.2
  75.7 1.3 copy-start.5
  81.4 19.8 %collective-permute-start.13 = (bf16[512,1024]{1,0:T(8,128)(2,1)S(1)}, bf16[512,1024]{1,0:T(8,128)(2,1)S(1)}, u32[]{:S(2)}, u32[]{:S(2)}) collective-permute-start(bf16[512,1024]{1,0:T(8,128)(2,1)S(1)} %constant_dynamic-update-slice_fusion.7.own_ref), channel_id=1, source_target_pairs={{0,1},{1,0},{2,3},{3,2},{4,5},{5,4},{6,7},{7,6},{8,9},{9,8},{10,11... | collective-permute-start | bytes 3145736 | tf_op jit(solution)/shard_map/ppermute | solution.py:214
  93.1 28.2 %all-to-all-start.3 = ((bf16[256,8,128]{2,1,0:T(8,128)(2,1)}), bf16[256,8,128]{2,1,0:T(8,128)(2,1)S(1)}, u32[]{:S(2)}, u32[]{:S(2)}) async-start(bf16[256,8,128]{2,1,0:T(8,128)(2,1)} %bitcast.25), calls=%async_computation.3 | async-start | bytes 1048576 | tf_op jit(solution)/shard_map/all_to_all | solution.py:261

commit v5 on v4

--- a/solution.py
+++ b/solution.py
@@ -223,8 +223,10 @@
     return lax.ppermute(x, "ctx", pairs)
 
 
-def gather_rows(rows):
-    rows = jnp.concatenate([rows, over_z(rows, 1), over_z(rows, 2), over_z(rows, -1)])
+def gather_rows(rows, relay):
+    below, above = over_z(rows, 1), over_z(rows, -1)
+    across = over_z(below, 1) if relay else over_z(rows, 2)
+    rows = jnp.concatenate([rows, below, across, above])
     rows = jnp.concatenate(
         [rows, over_plane(rows, 0, 1), over_plane(rows, 1, 0), over_plane(rows, 0, -1)]
     )
@@ -240,7 +242,7 @@
     blocks = (ch_count, wide[0] // ch_count, wide[1])
     quarter = (ctx_place // 2 % 4 + 2 * (ctx_place // 8)) % 4
     place = jnp.stack([ch_place % 2, ch_place // 2, quarter]).astype(jnp.int32)
-    in_own, in_mate = gather_rows(lax.dynamic_slice_in_dim(w_in, 32 * quarter, 32, 1).T)
+    in_own, in_mate = gather_rows(lax.dynamic_slice_in_dim(w_in, 32 * quarter, 32, 1).T, True)
     tokens = lax.all_to_all(tokens, "ch", 0, 0, tiled=True)
     shaped = call(shape_kernel, wide, BF, wide, 2**25, filters, w_filter)
     shaped = lax.all_to_all(shaped, "ctx", 0, 0, tiled=True)
@@ -248,7 +250,7 @@
         filter_kernel, (4 * NB, 2 * NB), F32, wide, 2**31, shaped, outer, inner, turn
     )
     w_out, tokens = lax.optimization_barrier((w_out, tokens))
-    out_own, out_mate = gather_rows(lax.dynamic_slice_in_dim(w_out, 32 * quarter, 32, 0))
+    out_own, out_mate = gather_rows(lax.dynamic_slice_in_dim(w_out, 32 * quarter, 32, 0), False)
     signal = call(
         project_kernel, wide, BF, blocks, 2**29, place, tokens, in_own, in_mate, scalars=True
     )

time: 145 us -> 158 us (1.090)
  waiting for transfers between devices: 38.4 us -> 48.2 us
  starting transfers between devices: 53.5 us -> 56.6 us
    ppermute x6, waiting for transfers between devices: 0.14 us -> 14.2 us  [over_z(): return lax.ppermute(x, 'ch', [(n, (n + 2 * step) % 8) for n in range(8)])]
    all_to_all x1, starting transfers between devices: 3.49 us -> 6.21 us  [local(): tokens = lax.all_to_all(tokens, 'ch', 0, 0, tiled=True)]
    all_to_all x1, waiting for transfers between devices: 2.4 us -> 0.01 us  [local(): tokens = lax.all_to_all(tokens, 'ch', 0, 0, tiled=True)]
    ppermute x6, starting transfers between devices: 17.8 us -> 15.9 us  [over_z(): return lax.ppermute(x, 'ch', [(n, (n + 2 * step) % 8) for n in range(8)])]
  transfers between devices with their start and end apart: 18 -> 18, of which waited for: 9 -> 8; matrix products, arithmetic and copies ran while one was open for 6% -> 5% of each run, Pallas kernels for 12% -> 11%
where the time goes in v5:
time: 158 us; the launch traced here: 157 us
  starting transfers between devices  56.6 us (36%)
  waiting for transfers between devices  48.2 us (31%)
  blocking collectives  20.4 us (13%)
  Pallas kernels  18.3 us (12%)
  local copies, waits for them, and re-layouts  12.2 us (8%)
    all_to_all x1, blocking collectives, local(): return lax.all_to_all(result, 'ch', 0, 0, tiled=True)  20.4 us
    all_to_all x1, waiting for transfers between devices, local(): mixed = lax.all_to_all(mixed, every, 0, 0, tiled=True)  20.1 us
    pallas_call x5, Pallas kernels, call(): pl.pallas_call(kernel, out_shape=jax.ShapeDtypeStruct(shape, dtype), in_s...  18.3 us
    ppermute x6, starting transfers between devices, over_z(): return lax.ppermute(x, 'ch', [(n, (n + 2 * step) % 8) for n in range(8)])  15.9 us
    ppermute x6, waiting for transfers between devices, over_z(): return lax.ppermute(x, 'ch', [(n, (n + 2 * step) % 8) for n in range(8)])  14.2 us
    unnamed x29, local copies, waits for them, and re-layouts  11.3 us
    all_to_all x1, starting transfers between devices, local(): signal = lax.all_to_all(signal, every, 0, 0, tiled=True)  9.47 us
    all_to_all x1, starting transfers between devices, local(): shaped = lax.all_to_all(shaped, 'ctx', 0, 0, tiled=True)  9.4 us
  transfers between devices with their start and end apart: 18, of which 8 were waited for; matrix products, arithmetic and copies ran while one was open for 5% of the time, Pallas kernels for 11%

profile of v5, /device:TPU:2, one launch (start us, length us, event | category | flops | bytes accessed | tf_op | source)
XLA Modules:
  0.0 157.0 jit_solution(8852467816737853677)
XLA Ops:
  0.0 0.9 copy-done
  1.2 3.3 %collective-permute-start = (bf16[32,1024]{1,0:T(8,128)(2,1)S(1)}, bf16[32,1024]{1,0:T(8,128)(2,1)S(1)}, u32[]{:S(2)}, u32[]{:S(2)}) collective-permute-start(bf16[32,1024]{1,0:T(8,128)(2,1)S(1)} %bitcast.20), channel_id=1, source_target_pairs={{0,2},{1,3},{2,4},{3,5},{4,6},{5,7},{6,0},{7,1},{8,10},{9,11},{10,... | collective-permute-start | bytes 196616 | tf_op jit(solution)/shard_map/ppermute | solution.py:210
  4.6 3.1 %collective-permute-start.2 = (bf16[32,1024]{1,0:T(8,128)(2,1)S(1)}, bf16[32,1024]{1,0:T(8,128)(2,1)S(1)}, u32[]{:S(2)}, u32[]{:S(2)}) collective-permute-start(bf16[32,1024]{1,0:T(8,128)(2,1)S(1)} %bitcast.21), channel_id=1, source_target_pairs={{0,6},{1,7},{2,0},{3,1},{4,2},{5,3},{6,4},{7,5},{8,14},{9,15},{10,... | collective-permute-start | bytes 196616 | tf_op jit(solution)/shard_map/ppermute | solution.py:210
  7.7 6.2 %all-to-all-start = ((bf16[8,256,128]{2,1,0:T(8,128)(2,1)}), bf16[8,256,128]{2,1,0:T(8,128)(2,1)S(1)}, u32[]{:S(2)}, u32[]{:S(2)}) async-start(bf16[8,256,128]{2,1,0:T(8,128)(2,1)} %bitcast.23), calls=%async_computation | async-start | bytes 1048576 | tf_op jit(solution)/shard_map/all_to_all | solution.py:246
  13.9 3.0 %collective-permute-start.1 = (bf16[32,1024]{1,0:T(8,128)(2,1)S(1)}, bf16[32,1024]{1,0:T(8,128)(2,1)S(1)}, u32[]{:S(2)}, u32[]{:S(2)}) collective-permute-start(bf16[32,1024]{1,0:T(8,128)(2,1)S(1)} %collective-permute-done), channel_id=1, source_target_pairs={{0,2},{1,3},{2,4},{3,5},{4,6},{5,7},{6,0},{7,1},{8,10},{9,11},{10,... | collective-permute-start | bytes 196616 | tf_op jit(solution)/shard_map/ppermute | solution.py:210
  17.5 14.2 %collective-permute-done.1 = bf16[32,1024]{1,0:T(8,128)(2,1)S(1)} collective-permute-done((bf16[32,1024]{1,0:T(8,128)(2,1)S(1)}, bf16[32,1024]{1,0:T(8,128)(2,1)S(1)}, u32[]{:S(2)}, u32[]{:S(2)}) %collective-permute-start.1) | collective-permute-done | bytes 65568 | tf_op jit(solution)/shard_map/ppermute | solution.py:210
  31.7 1.6 collective-permute-start.3
  33.9 1.6 %collective-permute-start.4 = (bf16[128,1024]{1,0:T(8,128)(2,1)S(1)}, bf16[128,1024]{1,0:T(8,128)(2,1)S(1)}, u32[]{:S(2)}, u32[]{:S(2)}) collective-permute-start(bf16[128,1024]{1,0:T(8,128)(2,1)S(1)} %pad_maximum_fusion), channel_id=1, source_target_pairs={{0,64},{8,72},{16,80},{24,88},{32,96},{40,104},{48,112},{56,120},{... | collective-permute-start | bytes 786440 | tf_op jit(solution)/shard_map/ppermute | solution.py:223
  37.3 1.6 collective-permute-done.3
  39.6 2.4 %collective-permute-done.4 = bf16[128,1024]{1,0:T(8,128)(2,1)S(1)} collective-permute-done((bf16[128,1024]{1,0:T(8,128)(2,1)S(1)}, bf16[128,1024]{1,0:T(8,128)(2,1)S(1)}, u32[]{:S(2)}, u32[]{:S(2)}) %collective-permute-start.4) | collective-permute-done | bytes 262176 | tf_op jit(solution)/shard_map/ppermute | solution.py:223
  43.7 2.0 %shard_map.101 = bf16[2048,128]{1,0:T(8,128)(2,1)} custom-call(f32[2048,24]{1,0:T(8,128)S(1)} %copy.12.filters_ref, f32[24,128]{1,0:T(8,128)S(1)} %copy-done.1), custom_call_target="tpu_custom_call" | custom-call | flops 33554432 | bytes 1257472 | tf_op jit(solution)/shard_map/pallas_call | solution.py:196
  45.7 9.4 %all-to-all-start.2 = ((bf16[32,64,128]{2,1,0:T(8,128)(2,1)}), bf16[32,64,128]{2,1,0:T(8,128)(2,1)S(1)}, u32[]{:S(2)}, u32[]{:S(2)}) async-start(bf16[32,64,128]{2,1,0:T(8,128)(2,1)} %bitcast.8), calls=%async_computation.2 | async-start | bytes 1048576 | tf_op jit(solution)/shard_map/all_to_all | solution.py:248
  55.2 0.8 constant_dynamic-update-slice_fusion.13
  56.2 4.1 %collective-permute-start.8 = (bf16[32,1024]{1,0:T(8,128)(2,1)S(1)}, bf16[32,1024]{1,0:T(8,128)(2,1)}, u32[]{:S(2)}, u32[]{:S(2)}) collective-permute-start(bf16[32,1024]{1,0:T(8,128)(2,1)S(1)} %get-tuple-element.10), channel_id=1, source_target_pairs={{0,4},{1,5},{2,6},{3,7},{4,0},{5,1},{6,2},{7,3},{8,12},{9,13},{10,... | collective-permute-start | bytes 196616 | tf_op jit(solution)/shard_map/ppermute | solution.py:210
  60.3 2.3 %collective-permute-start.9 = (bf16[32,1024]{1,0:T(8,128)(2,1)S(1)}, bf16[32,1024]{1,0:T(8,128)(2,1)}, u32[]{:S(2)}, u32[]{:S(2)}) collective-permute-start(bf16[32,1024]{1,0:T(8,128)(2,1)S(1)} %get-tuple-element.10), channel_id=1, source_target_pairs={{0,6},{1,7},{2,0},{3,1},{4,2},{5,3},{6,4},{7,5},{8,14},{9,15},{10,... | collective-permute-start | bytes 196616 | tf_op jit(solution)/shard_map/ppermute | solution.py:210
  62.6 3.9 %shard_map.100 = bf16[2048,128]{1,0:T(8,128)(2,1)} custom-call(s32[3]{0:T(128)S(1)} %pad_add_fusion.place_ref, bf16[2048,128]{1,0:T(8,128)(2,1)S(1)} %bitcast.15, bf16[512,1024]{1,0:T(8,128)(2,1)} %constant_dynamic-update-slice_fusion.own_ref, bf16[512,1024]{1,0:T(8,128)(2,1)} %collective-permute-done.6.mate_ref), custom_call_target="tpu_custom_call" | custom-call | flops 536870912 | bytes 3670028 | tf_op jit(solution)/shard_map/pallas_call | solution.py:196
  66.5 2.5 %all-to-all-done.2 = bf16[32,64,128]{2,1,0:T(8,128)(2,1)S(1)} async-done(((bf16[32,64,128]{2,1,0:T(8,128)(2,1)}), bf16[32,64,128]{2,1,0:T(8,128)(2,1)S(1)}, u32[]{:S(2)}, u32[]{:S(2)}) %all-to-all-start.2) | async-done | bytes 524320 | tf_op jit(solution)/shard_map/all_to_all | solution.py:248
  68.9 9.5 %all-to-all-start.1 = ((bf16[256,8,128]{2,1,0:T(8,128)(2,1)}), bf16[256,8,128]{2,1,0:T(8,128)(2,1)}, u32[]{:S(2)}, u32[]{:S(2)}) async-start(bf16[256,8,128]{2,1,0:T(8,128)(2,1)} %bitcast.6), calls=%async_computation.1 | async-start | bytes 1048576 | tf_op jit(solution)/shard_map/all_to_all | solution.py:257
  78.4 0.9 pad_maximum_fusion.1
  79.3 1.7 %collective-permute-start.10 = (bf16[128,1024]{1,0:T(8,128)(2,1)S(1)}, bf16[128,1024]{1,0:T(8,128)(2,1)S(1)}, u32[]{:S(2)}, u32[]{:S(2)}) collective-permute-start(bf16[128,1024]{1,0:T(8,128)(2,1)S(1)} %pad_maximum_fusion.1), channel_id=1, source_target_pairs={{0,16},{8,24},{16,32},{24,40},{32,48},{40,56},{48,0},{56,8},{64,80... | collective-permute-start | bytes 786440 | tf_op jit(solution)/shard_map/ppermute | solution.py:223
  81.1 1.5 collective-permute-start.11
  84.8 1.2 copy-done.2
  86.0 2.7 %shard_map.102.refs_4_ = f32[1024,512]{1,0:T(8,128)S(1)} custom-call(bf16[2048,128]{1,0:T(8,128)(2,1)S(1)} %bitcast.18, bf16[2,512,256]{2,1,0:T(8,128)(2,1)S(1)} %copy-done.4, bf16[2,512,512]{2,1,0:T(8,128)(2,1)S(1)} %copy-done.2, f32[2,256,256]{2,1,0:T(8,128)S(1)} %copy-done.3), custom_call_target="tpu_custom_call" | custom-call | flops 2147483648 | bytes 4718592 | tf_op jit(solution)/shard_map/pallas_call | solution.py:196
  88.7 1.3 copy-done.5
  90.0 1.5 collective-permute-done.10
  91.5 2.7 %collective-permute-done.11 = bf16[128,1024]{1,0:T(8,128)(2,1)S(1)} collective-permute-done((bf16[128,1024]{1,0:T(8,128)(2,1)S(1)}, bf16[128,1024]{1,0:T(8,128)(2,1)S(1)}, u32[]{:S(2)}, u32[]{:S(2)}) %collective-permute-start.11) | collective-permute-done | bytes 262176 | tf_op jit(solution)/shard_map/ppermute | solution.py:223
  94.4 3.2 %all-to-all-done.1 = bf16[256,8,128]{2,1,0:T(8,128)(2,1)} async-done(((bf16[256,8,128]{2,1,0:T(8,128)(2,1)}), bf16[256,8,128]{2,1,0:T(8,128)(2,1)}, u32[]{:S(2)}, u32[]{:S(2)}) %all-to-all-start.1) | async-done | bytes 524320 | tf_op jit(solution)/shard_map/all_to_all | solution.py:257
  97.7 8.4 %shard_map.103 = bf16[2048,128]{1,0:T(8,128)(2,1)} custom-call(bf16[2048,128]{1,0:T(8,128)(2,1)} %bitcast.7.refs_0_, bf16[2,512,256]{2,1,0:T(8,128)(2,1)} %constant.82.clone.refs_1_, f32[2,256,256]{2,1,0:T(8,128)} %constant.81.clone.turn_ref.refs_2_, bf16[2,512,512]{2,1,0:T(8,128)(2,1)} %constant.80.clone.inner_ref.refs_3_, f32[1024,512]{1,0:T(8,128)} %copy-done.5, ...), custom_call_target="tpu_custom_call" | custom-call | flops 4294967296 | bytes 6291456 | tf_op jit(solution)/shard_map/pallas_call | solution.py:196
  106.1 8.1 %all-to-all-start.3 = ((bf16[256,8,128]{2,1,0:T(8,128)(2,1)}), bf16[256,8,128]{2,1,0:T(8,128)(2,1)S(1)}, u32[]{:S(2)}, u32[]{:S(2)}) async-start(bf16[256,8,128]{2,1,0:T(8,128)(2,1)} %bitcast.24), calls=%async_computation.3 | async-start | bytes 1048576 | tf_op jit(solution)/shard_map/all_to_all | solution.py:263
  114.2 20.1 %all-to-all-done.3 = bf16[256,8,128]{2,1,0:T(8,128)(2,1)S(1)} async-done(((bf16[256,8,128]{2,1,0:T(8,128)(2,1)}), bf16[256,8,128]{2,1,0:T(8,128)(2,1)S(1)}, u32[]{:S(2)}, u32[]{:S(2)}) %all-to-all-start.3) | async-done | bytes 524320 | tf_op jit(solution)/shard_map/all_to_all | solution.py:263
  134.3 1.4 shard_map.104
  135.7 20.4 %all_to_all.57 = bf16[8,256,128]{2,1,0:T(8,128)(2,1)S(1)} all-to-all(bf16[8,256,128]{2,1,0:T(8,128)(2,1)S(1)} %bitcast.17), channel_id=1, replica_groups=mesh['ctx'=32,'ch'=8] {'ch'}, dimensions={0} | all-to-all | bytes 1048576 | tf_op jit(solution)/shard_map/all_to_all | solution.py:267
  (45 shorter events, 9.2 us)
Async XLA Ops:
  0.0 1.0 copy-start
  1.1 42.3 %copy-start.6 = (f32[2048,24]{0,1:T(8,128)S(1)}, f32[2048,24]{0,1:T(8,128)}, u32[]{:S(2)}) copy-start(f32[2048,24]{0,1:T(8,128)} %param.12) | copy-start | bytes 589828
  1.2 12.7 %collective-permute-start = (bf16[32,1024]{1,0:T(8,128)(2,1)S(1)}, bf16[32,1024]{1,0:T(8,128)(2,1)S(1)}, u32[]{:S(2)}, u32[]{:S(2)}) collective-permute-start(bf16[32,1024]{1,0:T(8,128)(2,1)S(1)} %bitcast.20), channel_id=1, source_target_pairs={{0,2},{1,3},{2,4},{3,5},{4,6},{5,7},{6,0},{7,1},{8,10},{9,11},{10,... | collective-permute-start | bytes 196616 | tf_op jit(solution)/shard_map/ppermute | solution.py:210
  4.6 13.0 %collective-permute-start.2 = (bf16[32,1024]{1,0:T(8,128)(2,1)S(1)}, bf16[32,1024]{1,0:T(8,128)(2,1)S(1)}, u32[]{:S(2)}, u32[]{:S(2)}) collective-permute-start(bf16[32,1024]{1,0:T(8,128)(2,1)S(1)} %bitcast.21), channel_id=1, source_target_pairs={{0,6},{1,7},{2,0},{3,1},{4,2},{5,3},{6,4},{7,5},{8,14},{9,15},{10,... | collective-permute-start | bytes 196616 | tf_op jit(solution)/shard_map/ppermute | solution.py:210
  7.7 38.0 %all-to-all-start = ((bf16[8,256,128]{2,1,0:T(8,128)(2,1)}), bf16[8,256,128]{2,1,0:T(8,128)(2,1)S(1)}, u32[]{:S(2)}, u32[]{:S(2)}) async-start(bf16[8,256,128]{2,1,0:T(8,128)(2,1)} %bitcast.23), calls=%async_computation | async-start | bytes 1048576 | tf_op jit(solution)/shard_map/all_to_all | solution.py:246
  13.9 29.8 %copy-start.1 = (f32[24,128]{1,0:T(8,128)S(1)}, f32[24,128]{1,0:T(8,128)}, u32[]{:S(2)}) copy-start(f32[24,128]{1,0:T(8,128)} %w_ref.1) | copy-start | bytes 36868
  13.9 17.8 %collective-permute-start.1 = (bf16[32,1024]{1,0:T(8,128)(2,1)S(1)}, bf16[32,1024]{1,0:T(8,128)(2,1)S(1)}, u32[]{:S(2)}, u32[]{:S(2)}) collective-permute-start(bf16[32,1024]{1,0:T(8,128)(2,1)S(1)} %collective-permute-done), channel_id=1, source_target_pairs={{0,2},{1,3},{2,4},{3,5},{4,6},{5,7},{6,0},{7,1},{8,10},{9,11},{10,... | collective-permute-start | bytes 196616 | tf_op jit(solution)/shard_map/ppermute | solution.py:210
  31.7 7.1 %collective-permute-start.3 = (bf16[128,1024]{1,0:T(8,128)(2,1)S(1)}, bf16[128,1024]{1,0:T(8,128)(2,1)S(1)}, u32[]{:S(2)}, u32[]{:S(2)}) collective-permute-start(bf16[128,1024]{1,0:T(8,128)(2,1)S(1)} %pad_maximum_fusion), channel_id=1, source_target_pairs={{0,16},{8,24},{16,32},{24,40},{32,48},{40,56},{48,0},{56,8},{64,80... | collective-permute-start | bytes 786440 | tf_op jit(solution)/shard_map/ppermute | solution.py:223
  33.9 8.0 %collective-permute-start.4 = (bf16[128,1024]{1,0:T(8,128)(2,1)S(1)}, bf16[128,1024]{1,0:T(8,128)(2,1)S(1)}, u32[]{:S(2)}, u32[]{:S(2)}) collective-permute-start(bf16[128,1024]{1,0:T(8,128)(2,1)S(1)} %pad_maximum_fusion), channel_id=1, source_target_pairs={{0,64},{8,72},{16,80},{24,88},{32,96},{40,104},{48,112},{56,120},{... | collective-permute-start | bytes 786440 | tf_op jit(solution)/shard_map/ppermute | solution.py:223
  35.5 7.2 %collective-permute-start.5 = (bf16[128,1024]{1,0:T(8,128)(2,1)S(1)}, bf16[128,1024]{1,0:T(8,128)(2,1)S(1)}, u32[]{:S(2)}, u32[]{:S(2)}) collective-permute-start(bf16[128,1024]{1,0:T(8,128)(2,1)S(1)} %pad_maximum_fusion), channel_id=1, source_target_pairs={{0,48},{8,56},{16,0},{24,8},{32,16},{40,24},{48,32},{56,40},{64,11... | collective-permute-start | bytes 786440 | tf_op jit(solution)/shard_map/ppermute | solution.py:223
  43.4 19.2 %collective-permute-start.6 = (bf16[512,1024]{1,0:T(8,128)(2,1)}, bf16[512,1024]{1,0:T(8,128)(2,1)}, u32[]{:S(2)}, u32[]{:S(2)}) collective-permute-start(bf16[512,1024]{1,0:T(8,128)(2,1)} %constant_dynamic-update-slice_fusion.own_ref), channel_id=1, source_target_pairs={{0,1},{1,0},{2,3},{3,2},{4,5},{5,4},{6,7},{7,6},{8,9},{9,8},{10,11... | collective-permute-start | bytes 3145736 | tf_op jit(solution)/shard_map/ppermute | solution.py:214
  45.7 23.2 %all-to-all-start.2 = ((bf16[32,64,128]{2,1,0:T(8,128)(2,1)}), bf16[32,64,128]{2,1,0:T(8,128)(2,1)S(1)}, u32[]{:S(2)}, u32[]{:S(2)}) async-start(bf16[32,64,128]{2,1,0:T(8,128)(2,1)} %bitcast.8), calls=%async_computation.2 | async-start | bytes 1048576 | tf_op jit(solution)/shard_map/all_to_all | solution.py:248
  56.1 28.7 %copy-start.3 = (f32[2,256,256]{2,1,0:T(8,128)S(1)}, f32[2,256,256]{2,1,0:T(8,128)}, u32[]{:S(2)}) copy-start(f32[2,256,256]{2,1,0:T(8,128)} %constant.81.clone.turn_ref.refs_2_) | copy-start | bytes 1572868
  56.1 28.7 %copy-start.4 = (bf16[2,512,256]{2,1,0:T(8,128)(2,1)S(1)}, bf16[2,512,256]{2,1,0:T(8,128)(2,1)}, u32[]{:S(2)}) copy-start(bf16[2,512,256]{2,1,0:T(8,128)(2,1)} %constant.79.clone.outer_ref) | copy-start | bytes 1572868
  56.1 22.3 %collective-permute-start.7 = (bf16[32,1024]{1,0:T(8,128)(2,1)S(1)}, bf16[32,1024]{1,0:T(8,128)(2,1)S(1)}, u32[]{:S(2)}, u32[]{:S(2)}) collective-permute-start(bf16[32,1024]{1,0:T(8,128)(2,1)S(1)} %get-tuple-element.10), channel_id=1, source_target_pairs={{0,2},{1,3},{2,4},{3,5},{4,6},{5,7},{6,0},{7,1},{8,10},{9,11},{10,... | collective-permute-start | bytes 196616 | tf_op jit(solution)/shard_map/ppermute | solution.py:210
  56.2 22.2 %collective-permute-start.8 = (bf16[32,1024]{1,0:T(8,128)(2,1)S(1)}, bf16[32,1024]{1,0:T(8,128)(2,1)}, u32[]{:S(2)}, u32[]{:S(2)}) collective-permute-start(bf16[32,1024]{1,0:T(8,128)(2,1)S(1)} %get-tuple-element.10), channel_id=1, source_target_pairs={{0,4},{1,5},{2,6},{3,7},{4,0},{5,1},{6,2},{7,3},{8,12},{9,13},{10,... | collective-permute-start | bytes 196616 | tf_op jit(solution)/shard_map/ppermute | solution.py:210
  60.3 18.1 %collective-permute-start.9 = (bf16[32,1024]{1,0:T(8,128)(2,1)S(1)}, bf16[32,1024]{1,0:T(8,128)(2,1)}, u32[]{:S(2)}, u32[]{:S(2)}) collective-permute-start(bf16[32,1024]{1,0:T(8,128)(2,1)S(1)} %get-tuple-element.10), channel_id=1, source_target_pairs={{0,6},{1,7},{2,0},{3,1},{4,2},{5,3},{6,4},{7,5},{8,14},{9,15},{10,... | collective-permute-start | bytes 196616 | tf_op jit(solution)/shard_map/ppermute | solution.py:210
  68.9 28.7 %all-to-all-start.1 = ((bf16[256,8,128]{2,1,0:T(8,128)(2,1)}), bf16[256,8,128]{2,1,0:T(8,128)(2,1)}, u32[]{:S(2)}, u32[]{:S(2)}) async-start(bf16[256,8,128]{2,1,0:T(8,128)(2,1)} %bitcast.6), calls=%async_computation.1 | async-start | bytes 1048576 | tf_op jit(solution)/shard_map/all_to_all | solution.py:257
  79.3 12.2 %collective-permute-start.10 = (bf16[128,1024]{1,0:T(8,128)(2,1)S(1)}, bf16[128,1024]{1,0:T(8,128)(2,1)S(1)}, u32[]{:S(2)}, u32[]{:S(2)}) collective-permute-start(bf16[128,1024]{1,0:T(8,128)(2,1)S(1)} %pad_maximum_fusion.1), channel_id=1, source_target_pairs={{0,16},{8,24},{16,32},{24,40},{32,48},{40,56},{48,0},{56,8},{64,80... | collective-permute-start | bytes 786440 | tf_op jit(solution)/shard_map/ppermute | solution.py:223
  81.1 13.2 %collective-permute-start.11 = (bf16[128,1024]{1,0:T(8,128)(2,1)S(1)}, bf16[128,1024]{1,0:T(8,128)(2,1)S(1)}, u32[]{:S(2)}, u32[]{:S(2)}) collective-permute-start(bf16[128,1024]{1,0:T(8,128)(2,1)S(1)} %pad_maximum_fusion.1), channel_id=1, source_target_pairs={{0,64},{8,72},{16,80},{24,88},{32,96},{40,104},{48,112},{56,120},{... | collective-permute-start | bytes 786440 | tf_op jit(solution)/shard_map/ppermute | solution.py:223
  82.5 11.8 %collective-permute-start.12 = (bf16[128,1024]{1,0:T(8,128)(2,1)S(1)}, bf16[128,1024]{1,0:T(8,128)(2,1)S(1)}, u32[]{:S(2)}, u32[]{:S(2)}) collective-permute-start(bf16[128,1024]{1,0:T(8,128)(2,1)S(1)} %pad_maximum_fusion.1), channel_id=1, source_target_pairs={{0,48},{8,56},{16,0},{24,8},{32,16},{40,24},{48,32},{56,40},{64,11... | collective-permute-start | bytes 786440 | tf_op jit(solution)/shard_map/ppermute | solution.py:223
  84.8 1.2 copy-start.2
  88.7 1.3 copy-start.5
  94.3 19.8 %collective-permute-start.13 = (bf16[512,1024]{1,0:T(8,128)(2,1)S(1)}, bf16[512,1024]{1,0:T(8,128)(2,1)S(1)}, u32[]{:S(2)}, u32[]{:S(2)}) collective-permute-start(bf16[512,1024]{1,0:T(8,128)(2,1)S(1)} %constant_dynamic-update-slice_fusion.7.own_ref), channel_id=1, source_target_pairs={{0,1},{1,0},{2,3},{3,2},{4,5},{5,4},{6,7},{7,6},{8,9},{9,8},{10,11... | collective-permute-start | bytes 3145736 | tf_op jit(solution)/shard_map/ppermute | solution.py:214
  106.1 28.2 %all-to-all-start.3 = ((bf16[256,8,128]{2,1,0:T(8,128)(2,1)}), bf16[256,8,128]{2,1,0:T(8,128)(2,1)S(1)}, u32[]{:S(2)}, u32[]{:S(2)}) async-start(bf16[256,8,128]{2,1,0:T(8,128)(2,1)} %bitcast.24), calls=%async_computation.3 | async-start | bytes 1048576 | tf_op jit(solution)/shard_map/all_to_all | solution.py:263

commit v6 on v4

--- a/solution.py
+++ b/solution.py
@@ -83,15 +83,18 @@
 def project_kernel(place_ref, tokens_ref, own_ref, mate_ref, out_ref, wide_ref):
     count = tokens_ref.shape[0] // NB
     tokens = jnp.concatenate([tokens_ref[pl.ds(NB * j, NB), :] for j in range(count)], axis=1)
-    for rel, part_ref in enumerate((own_ref, mate_ref)):
-        for z in range(count // 2):
-            j = 2 * z + (place_ref[0] + rel) % 2
-            part = dot(weight_rows(place_ref, part_ref, z), tokens, ((1,), (1,)))
-            for c in range(4):
-                for half in range(2):
-                    wide_ref[j, pl.ds(c * 2 + half, 32, stride=8), :] = part[
-                        32 * c : 32 * (c + 1), half * LANES : (half + 1) * LANES
-                    ]
+    places = [(rel, z) for rel in range(2) for z in range(count // 2)]
+    parts = (own_ref, mate_ref)
+    weight = jnp.concatenate([weight_rows(place_ref, parts[rel], z) for rel, z in places], axis=0)
+    result = dot(weight, tokens, ((1,), (1,)))
+    for n, (rel, z) in enumerate(places):
+        j = 2 * z + (place_ref[0] + rel) % 2
+        for c in range(4):
+            row = n * LANES + 32 * c
+            for half in range(2):
+                wide_ref[j, pl.ds(c * 2 + half, 32, stride=8), :] = result[
+                    row : row + 32, half * LANES : (half + 1) * LANES
+                ]
     for j in range(count):
         out_ref[pl.ds(NB * j, NB), :] = wide_ref[j].astype(out_ref.dtype)
 

time: 145 us -> 144 us (level)
  transfers between devices with their start and end apart: 18 -> 18, of which waited for: 9 -> 9; matrix products, arithmetic and copies ran while one was open for 6% -> 6% of each run, Pallas kernels for 12% -> 11%
where the time goes in v6:
time: 144 us
  starting transfers between devices  52.8 us (37%)
  waiting for transfers between devices  39.4 us (27%)
  blocking collectives  20.4 us (14%)
  Pallas kernels  17.6 us (12%)
  local copies, waits for them, and re-layouts  12.2 us (8%)
    all_to_all x1, blocking collectives, local(): return lax.all_to_all(result, 'ch', 0, 0, tiled=True)  20.4 us
    all_to_all x1, waiting for transfers between devices, local(): mixed = lax.all_to_all(mixed, every, 0, 0, tiled=True)  20.1 us
    ppermute x6, starting transfers between devices, over_z(): return lax.ppermute(x, 'ch', [(n, (n + 2 * step) % 8) for n in range(8)])  17.8 us
    pallas_call x5, Pallas kernels, call(): pl.pallas_call(kernel, out_shape=jax.ShapeDtypeStruct(shape, dtype), in_s...  17.6 us
    unnamed x29, local copies, waits for them, and re-layouts  11.3 us
    ppermute x6, waiting for transfers between devices, over_plane(): return lax.ppermute(x, 'ctx', pairs)  8.89 us
    all_to_all x1, starting transfers between devices, local(): signal = lax.all_to_all(signal, every, 0, 0, tiled=True)  8.17 us
    all_to_all x1, starting transfers between devices, local(): shaped = lax.all_to_all(shaped, 'ctx', 0, 0, tiled=True)  8.01 us
  transfers between devices with their start and end apart: 18, of which 9 were waited for; matrix products, arithmetic and copies ran while one was open for 6% of the time, Pallas kernels for 11%

profile of v6, /device:TPU:2, one launch (start us, length us, event | category | flops | bytes accessed | tf_op | source)
XLA Modules:
  0.0 143.6 jit_solution(847178988721277204)
XLA Ops:
  0.0 0.9 copy-done
  1.2 3.3 %collective-permute-start = (bf16[32,1024]{1,0:T(8,128)(2,1)S(1)}, bf16[32,1024]{1,0:T(8,128)(2,1)S(1)}, u32[]{:S(2)}, u32[]{:S(2)}) collective-permute-start(bf16[32,1024]{1,0:T(8,128)(2,1)S(1)} %bitcast.20), channel_id=1, source_target_pairs={{0,2},{1,3},{2,4},{3,5},{4,6},{5,7},{6,0},{7,1},{8,10},{9,11},{10,... | collective-permute-start | bytes 196616 | tf_op jit(solution)/shard_map/ppermute | solution.py:213
  4.6 5.4 %collective-permute-start.1 = (bf16[32,1024]{1,0:T(8,128)(2,1)S(1)}, bf16[32,1024]{1,0:T(8,128)(2,1)S(1)}, u32[]{:S(2)}, u32[]{:S(2)}) collective-permute-start(bf16[32,1024]{1,0:T(8,128)(2,1)S(1)} %bitcast.21), channel_id=1, source_target_pairs={{0,4},{1,5},{2,6},{3,7},{4,0},{5,1},{6,2},{7,3},{8,12},{9,13},{10,... | collective-permute-start | bytes 196616 | tf_op jit(solution)/shard_map/ppermute | solution.py:213
  10.0 2.7 %collective-permute-start.2 = (bf16[32,1024]{1,0:T(8,128)(2,1)S(1)}, bf16[32,1024]{1,0:T(8,128)(2,1)S(1)}, u32[]{:S(2)}, u32[]{:S(2)}) collective-permute-start(bf16[32,1024]{1,0:T(8,128)(2,1)S(1)} %bitcast.22), channel_id=1, source_target_pairs={{0,6},{1,7},{2,0},{3,1},{4,2},{5,3},{6,4},{7,5},{8,14},{9,15},{10,... | collective-permute-start | bytes 196616 | tf_op jit(solution)/shard_map/ppermute | solution.py:213
  12.6 3.5 %all-to-all-start = ((bf16[8,256,128]{2,1,0:T(8,128)(2,1)}), bf16[8,256,128]{2,1,0:T(8,128)(2,1)S(1)}, u32[]{:S(2)}, u32[]{:S(2)}) async-start(bf16[8,256,128]{2,1,0:T(8,128)(2,1)} %bitcast.24), calls=%async_computation | async-start | bytes 1048576 | tf_op jit(solution)/shard_map/all_to_all | solution.py:247
  16.9 1.6 %collective-permute-start.3 = (bf16[128,1024]{1,0:T(8,128)(2,1)S(1)}, bf16[128,1024]{1,0:T(8,128)(2,1)S(1)}, u32[]{:S(2)}, u32[]{:S(2)}) collective-permute-start(bf16[128,1024]{1,0:T(8,128)(2,1)S(1)} %pad_maximum_fusion), channel_id=1, source_target_pairs={{0,16},{8,24},{16,32},{24,40},{32,48},{40,56},{48,0},{56,8},{64,80... | collective-permute-start | bytes 786440 | tf_op jit(solution)/shard_map/ppermute | solution.py:226
  18.5 1.6 %collective-permute-start.4 = (bf16[128,1024]{1,0:T(8,128)(2,1)S(1)}, bf16[128,1024]{1,0:T(8,128)(2,1)S(1)}, u32[]{:S(2)}, u32[]{:S(2)}) collective-permute-start(bf16[128,1024]{1,0:T(8,128)(2,1)S(1)} %pad_maximum_fusion), channel_id=1, source_target_pairs={{0,64},{8,72},{16,80},{24,88},{32,96},{40,104},{48,112},{56,120},{... | collective-permute-start | bytes 786440 | tf_op jit(solution)/shard_map/ppermute | solution.py:226
  22.5 3.0 %collective-permute-done.3 = bf16[128,1024]{1,0:T(8,128)(2,1)S(1)} collective-permute-done((bf16[128,1024]{1,0:T(8,128)(2,1)S(1)}, bf16[128,1024]{1,0:T(8,128)(2,1)S(1)}, u32[]{:S(2)}, u32[]{:S(2)}) %collective-permute-start.3) | collective-permute-done | bytes 262176 | tf_op jit(solution)/shard_map/ppermute | solution.py:226
  26.2 1.8 %collective-permute-done.4 = bf16[128,1024]{1,0:T(8,128)(2,1)S(1)} collective-permute-done((bf16[128,1024]{1,0:T(8,128)(2,1)S(1)}, bf16[128,1024]{1,0:T(8,128)(2,1)S(1)}, u32[]{:S(2)}, u32[]{:S(2)}) %collective-permute-start.4) | collective-permute-done | bytes 262176 | tf_op jit(solution)/shard_map/ppermute | solution.py:226
  29.8 2.0 %shard_map.101 = bf16[2048,128]{1,0:T(8,128)(2,1)} custom-call(f32[2048,24]{1,0:T(8,128)S(1)} %copy.12.filters_ref, f32[24,128]{1,0:T(8,128)S(1)} %copy-done.1), custom_call_target="tpu_custom_call" | custom-call | flops 33554432 | bytes 1257472 | tf_op jit(solution)/shard_map/pallas_call | solution.py:199
  31.8 2.4 %all-to-all-done = bf16[8,256,128]{2,1,0:T(8,128)(2,1)S(1)} async-done(((bf16[8,256,128]{2,1,0:T(8,128)(2,1)}), bf16[8,256,128]{2,1,0:T(8,128)(2,1)S(1)}, u32[]{:S(2)}, u32[]{:S(2)}) %all-to-all-start) | async-done | bytes 524320 | tf_op jit(solution)/shard_map/all_to_all | solution.py:247
  34.2 8.0 %all-to-all-start.2 = ((bf16[32,64,128]{2,1,0:T(8,128)(2,1)}), bf16[32,64,128]{2,1,0:T(8,128)(2,1)S(1)}, u32[]{:S(2)}, u32[]{:S(2)}) async-start(bf16[32,64,128]{2,1,0:T(8,128)(2,1)} %bitcast.8), calls=%async_computation.2 | async-start | bytes 1048576 | tf_op jit(solution)/shard_map/all_to_all | solution.py:249
  42.3 0.8 constant_dynamic-update-slice_fusion.13
  43.3 3.0 %collective-permute-start.8 = (bf16[32,1024]{1,0:T(8,128)(2,1)S(1)}, bf16[32,1024]{1,0:T(8,128)(2,1)}, u32[]{:S(2)}, u32[]{:S(2)}) collective-permute-start(bf16[32,1024]{1,0:T(8,128)(2,1)S(1)} %get-tuple-element.10), channel_id=1, source_target_pairs={{0,4},{1,5},{2,6},{3,7},{4,0},{5,1},{6,2},{7,3},{8,12},{9,13},{10,... | collective-permute-start | bytes 196616 | tf_op jit(solution)/shard_map/ppermute | solution.py:213
  46.3 3.3 %collective-permute-start.9 = (bf16[32,1024]{1,0:T(8,128)(2,1)S(1)}, bf16[32,1024]{1,0:T(8,128)(2,1)}, u32[]{:S(2)}, u32[]{:S(2)}) collective-permute-start(bf16[32,1024]{1,0:T(8,128)(2,1)S(1)} %get-tuple-element.10), channel_id=1, source_target_pairs={{0,6},{1,7},{2,0},{3,1},{4,2},{5,3},{6,4},{7,5},{8,14},{9,15},{10,... | collective-permute-start | bytes 196616 | tf_op jit(solution)/shard_map/ppermute | solution.py:213
  49.5 3.2 %shard_map.100 = bf16[2048,128]{1,0:T(8,128)(2,1)} custom-call(s32[3]{0:T(128)S(1)} %pad_add_fusion.place_ref, bf16[2048,128]{1,0:T(8,128)(2,1)S(1)} %bitcast.15, bf16[512,1024]{1,0:T(8,128)(2,1)} %constant_dynamic-update-slice_fusion.own_ref, bf16[512,1024]{1,0:T(8,128)(2,1)} %collective-permute-done.6.mate_ref), custom_call_target="tpu_custom_call" | custom-call | flops 536870912 | bytes 3670028 | tf_op jit(solution)/shard_map/pallas_call | solution.py:199
  52.7 4.2 %all-to-all-done.2 = bf16[32,64,128]{2,1,0:T(8,128)(2,1)S(1)} async-done(((bf16[32,64,128]{2,1,0:T(8,128)(2,1)}), bf16[32,64,128]{2,1,0:T(8,128)(2,1)S(1)}, u32[]{:S(2)}, u32[]{:S(2)}) %all-to-all-start.2) | async-done | bytes 524320 | tf_op jit(solution)/shard_map/all_to_all | solution.py:249
  56.9 8.2 %all-to-all-start.1 = ((bf16[256,8,128]{2,1,0:T(8,128)(2,1)}), bf16[256,8,128]{2,1,0:T(8,128)(2,1)}, u32[]{:S(2)}, u32[]{:S(2)}) async-start(bf16[256,8,128]{2,1,0:T(8,128)(2,1)} %bitcast.6), calls=%async_computation.1 | async-start | bytes 1048576 | tf_op jit(solution)/shard_map/all_to_all | solution.py:258
  65.1 0.9 pad_maximum_fusion.1
  66.0 1.6 %collective-permute-start.10 = (bf16[128,1024]{1,0:T(8,128)(2,1)S(1)}, bf16[128,1024]{1,0:T(8,128)(2,1)S(1)}, u32[]{:S(2)}, u32[]{:S(2)}) collective-permute-start(bf16[128,1024]{1,0:T(8,128)(2,1)S(1)} %pad_maximum_fusion.1), channel_id=1, source_target_pairs={{0,16},{8,24},{16,32},{24,40},{32,48},{40,56},{48,0},{56,8},{64,80... | collective-permute-start | bytes 786440 | tf_op jit(solution)/shard_map/ppermute | solution.py:226
  67.5 1.5 %collective-permute-start.11 = (bf16[128,1024]{1,0:T(8,128)(2,1)S(1)}, bf16[128,1024]{1,0:T(8,128)(2,1)S(1)}, u32[]{:S(2)}, u32[]{:S(2)}) collective-permute-start(bf16[128,1024]{1,0:T(8,128)(2,1)S(1)} %pad_maximum_fusion.1), channel_id=1, source_target_pairs={{0,64},{8,72},{16,80},{24,88},{32,96},{40,104},{48,112},{56,120},{... | collective-permute-start | bytes 786440 | tf_op jit(solution)/shard_map/ppermute | solution.py:226
  71.3 1.2 copy-done.2
  72.5 2.7 %shard_map.102.refs_4_ = f32[1024,512]{1,0:T(8,128)S(1)} custom-call(bf16[2048,128]{1,0:T(8,128)(2,1)S(1)} %bitcast.18, bf16[2,512,256]{2,1,0:T(8,128)(2,1)S(1)} %copy-done.4, bf16[2,512,512]{2,1,0:T(8,128)(2,1)S(1)} %copy-done.2, f32[2,256,256]{2,1,0:T(8,128)S(1)} %copy-done.3), custom_call_target="tpu_custom_call" | custom-call | flops 2147483648 | bytes 4718592 | tf_op jit(solution)/shard_map/pallas_call | solution.py:199
  75.2 1.3 copy-done.5
  76.6 1.6 %collective-permute-done.10 = bf16[128,1024]{1,0:T(8,128)(2,1)S(1)} collective-permute-done((bf16[128,1024]{1,0:T(8,128)(2,1)S(1)}, bf16[128,1024]{1,0:T(8,128)(2,1)S(1)}, u32[]{:S(2)}, u32[]{:S(2)}) %collective-permute-start.10) | collective-permute-done | bytes 262176 | tf_op jit(solution)/shard_map/ppermute | solution.py:226
  78.1 2.5 %collective-permute-done.11 = bf16[128,1024]{1,0:T(8,128)(2,1)S(1)} collective-permute-done((bf16[128,1024]{1,0:T(8,128)(2,1)S(1)}, bf16[128,1024]{1,0:T(8,128)(2,1)S(1)}, u32[]{:S(2)}, u32[]{:S(2)}) %collective-permute-start.11) | collective-permute-done | bytes 262176 | tf_op jit(solution)/shard_map/ppermute | solution.py:226
  80.8 3.6 %all-to-all-done.1 = bf16[256,8,128]{2,1,0:T(8,128)(2,1)} async-done(((bf16[256,8,128]{2,1,0:T(8,128)(2,1)}), bf16[256,8,128]{2,1,0:T(8,128)(2,1)}, u32[]{:S(2)}, u32[]{:S(2)}) %all-to-all-start.1) | async-done | bytes 524320 | tf_op jit(solution)/shard_map/all_to_all | solution.py:258
  84.4 8.4 %shard_map.103 = bf16[2048,128]{1,0:T(8,128)(2,1)} custom-call(bf16[2048,128]{1,0:T(8,128)(2,1)} %bitcast.7.refs_0_, bf16[2,512,256]{2,1,0:T(8,128)(2,1)} %constant.82.clone.refs_1_, f32[2,256,256]{2,1,0:T(8,128)} %constant.81.clone.turn_ref.refs_2_, bf16[2,512,512]{2,1,0:T(8,128)(2,1)} %constant.80.clone.inner_ref.refs_3_, f32[1024,512]{1,0:T(8,128)} %copy-done.5, ...), custom_call_target="tpu_custom_call" | custom-call | flops 4294967296 | bytes 6291456 | tf_op jit(solution)/shard_map/pallas_call | solution.py:199
  92.9 7.9 %all-to-all-start.3 = ((bf16[256,8,128]{2,1,0:T(8,128)(2,1)}), bf16[256,8,128]{2,1,0:T(8,128)(2,1)S(1)}, u32[]{:S(2)}, u32[]{:S(2)}) async-start(bf16[256,8,128]{2,1,0:T(8,128)(2,1)} %bitcast.25), calls=%async_computation.3 | async-start | bytes 1048576 | tf_op jit(solution)/shard_map/all_to_all | solution.py:264
  100.8 20.1 %all-to-all-done.3 = bf16[256,8,128]{2,1,0:T(8,128)(2,1)S(1)} async-done(((bf16[256,8,128]{2,1,0:T(8,128)(2,1)}), bf16[256,8,128]{2,1,0:T(8,128)(2,1)S(1)}, u32[]{:S(2)}, u32[]{:S(2)}) %all-to-all-start.3) | async-done | bytes 524320 | tf_op jit(solution)/shard_map/all_to_all | solution.py:264
  120.9 1.4 shard_map.104
  122.3 20.4 %all_to_all.57 = bf16[8,256,128]{2,1,0:T(8,128)(2,1)S(1)} all-to-all(bf16[8,256,128]{2,1,0:T(8,128)(2,1)S(1)} %bitcast.17), channel_id=1, replica_groups=mesh['ctx'=32,'ch'=8] {'ch'}, dimensions={0} | all-to-all | bytes 1048576 | tf_op jit(solution)/shard_map/all_to_all | solution.py:268
  (45 shorter events, 9.4 us)
Async XLA Ops:
  0.0 1.0 copy-start
  1.1 28.3 %copy-start.6 = (f32[2048,24]{0,1:T(8,128)S(1)}, f32[2048,24]{0,1:T(8,128)}, u32[]{:S(2)}) copy-start(f32[2048,24]{0,1:T(8,128)} %param.12) | copy-start | bytes 589828
  1.2 15.5 %collective-permute-start = (bf16[32,1024]{1,0:T(8,128)(2,1)S(1)}, bf16[32,1024]{1,0:T(8,128)(2,1)S(1)}, u32[]{:S(2)}, u32[]{:S(2)}) collective-permute-start(bf16[32,1024]{1,0:T(8,128)(2,1)S(1)} %bitcast.20), channel_id=1, source_target_pairs={{0,2},{1,3},{2,4},{3,5},{4,6},{5,7},{6,0},{7,1},{8,10},{9,11},{10,... | collective-permute-start | bytes 196616 | tf_op jit(solution)/shard_map/ppermute | solution.py:213
  4.6 12.2 %collective-permute-start.1 = (bf16[32,1024]{1,0:T(8,128)(2,1)S(1)}, bf16[32,1024]{1,0:T(8,128)(2,1)S(1)}, u32[]{:S(2)}, u32[]{:S(2)}) collective-permute-start(bf16[32,1024]{1,0:T(8,128)(2,1)S(1)} %bitcast.21), channel_id=1, source_target_pairs={{0,4},{1,5},{2,6},{3,7},{4,0},{5,1},{6,2},{7,3},{8,12},{9,13},{10,... | collective-permute-start | bytes 196616 | tf_op jit(solution)/shard_map/ppermute | solution.py:213
  10.0 6.9 %collective-permute-start.2 = (bf16[32,1024]{1,0:T(8,128)(2,1)S(1)}, bf16[32,1024]{1,0:T(8,128)(2,1)S(1)}, u32[]{:S(2)}, u32[]{:S(2)}) collective-permute-start(bf16[32,1024]{1,0:T(8,128)(2,1)S(1)} %bitcast.22), channel_id=1, source_target_pairs={{0,6},{1,7},{2,0},{3,1},{4,2},{5,3},{6,4},{7,5},{8,14},{9,15},{10,... | collective-permute-start | bytes 196616 | tf_op jit(solution)/shard_map/ppermute | solution.py:213
  12.6 21.5 %all-to-all-start = ((bf16[8,256,128]{2,1,0:T(8,128)(2,1)}), bf16[8,256,128]{2,1,0:T(8,128)(2,1)S(1)}, u32[]{:S(2)}, u32[]{:S(2)}) async-start(bf16[8,256,128]{2,1,0:T(8,128)(2,1)} %bitcast.24), calls=%async_computation | async-start | bytes 1048576 | tf_op jit(solution)/shard_map/all_to_all | solution.py:247
  16.1 13.6 %copy-start.1 = (f32[24,128]{1,0:T(8,128)S(1)}, f32[24,128]{1,0:T(8,128)}, u32[]{:S(2)}) copy-start(f32[24,128]{1,0:T(8,128)} %w_ref.1) | copy-start | bytes 36868
  16.9 8.6 %collective-permute-start.3 = (bf16[128,1024]{1,0:T(8,128)(2,1)S(1)}, bf16[128,1024]{1,0:T(8,128)(2,1)S(1)}, u32[]{:S(2)}, u32[]{:S(2)}) collective-permute-start(bf16[128,1024]{1,0:T(8,128)(2,1)S(1)} %pad_maximum_fusion), channel_id=1, source_target_pairs={{0,16},{8,24},{16,32},{24,40},{32,48},{40,56},{48,0},{56,8},{64,80... | collective-permute-start | bytes 786440 | tf_op jit(solution)/shard_map/ppermute | solution.py:226
  18.5 9.5 %collective-permute-start.4 = (bf16[128,1024]{1,0:T(8,128)(2,1)S(1)}, bf16[128,1024]{1,0:T(8,128)(2,1)S(1)}, u32[]{:S(2)}, u32[]{:S(2)}) collective-permute-start(bf16[128,1024]{1,0:T(8,128)(2,1)S(1)} %pad_maximum_fusion), channel_id=1, source_target_pairs={{0,64},{8,72},{16,80},{24,88},{32,96},{40,104},{48,112},{56,120},{... | collective-permute-start | bytes 786440 | tf_op jit(solution)/shard_map/ppermute | solution.py:226
  20.1 8.7 %collective-permute-start.5 = (bf16[128,1024]{1,0:T(8,128)(2,1)S(1)}, bf16[128,1024]{1,0:T(8,128)(2,1)S(1)}, u32[]{:S(2)}, u32[]{:S(2)}) collective-permute-start(bf16[128,1024]{1,0:T(8,128)(2,1)S(1)} %pad_maximum_fusion), channel_id=1, source_target_pairs={{0,48},{8,56},{16,0},{24,8},{32,16},{40,24},{48,32},{56,40},{64,11... | collective-permute-start | bytes 786440 | tf_op jit(solution)/shard_map/ppermute | solution.py:226
  29.4 20.1 %collective-permute-start.6 = (bf16[512,1024]{1,0:T(8,128)(2,1)}, bf16[512,1024]{1,0:T(8,128)(2,1)}, u32[]{:S(2)}, u32[]{:S(2)}) collective-permute-start(bf16[512,1024]{1,0:T(8,128)(2,1)} %constant_dynamic-update-slice_fusion.own_ref), channel_id=1, source_target_pairs={{0,1},{1,0},{2,3},{3,2},{4,5},{5,4},{6,7},{7,6},{8,9},{9,8},{10,11... | collective-permute-start | bytes 3145736 | tf_op jit(solution)/shard_map/ppermute | solution.py:217
  34.2 22.7 %all-to-all-start.2 = ((bf16[32,64,128]{2,1,0:T(8,128)(2,1)}), bf16[32,64,128]{2,1,0:T(8,128)(2,1)S(1)}, u32[]{:S(2)}, u32[]{:S(2)}) async-start(bf16[32,64,128]{2,1,0:T(8,128)(2,1)} %bitcast.8), calls=%async_computation.2 | async-start | bytes 1048576 | tf_op jit(solution)/shard_map/all_to_all | solution.py:249
  43.1 28.2 %copy-start.3 = (f32[2,256,256]{2,1,0:T(8,128)S(1)}, f32[2,256,256]{2,1,0:T(8,128)}, u32[]{:S(2)}) copy-start(f32[2,256,256]{2,1,0:T(8,128)} %constant.81.clone.turn_ref.refs_2_) | copy-start | bytes 1572868
  43.1 28.2 %copy-start.4 = (bf16[2,512,256]{2,1,0:T(8,128)(2,1)S(1)}, bf16[2,512,256]{2,1,0:T(8,128)(2,1)}, u32[]{:S(2)}) copy-start(bf16[2,512,256]{2,1,0:T(8,128)(2,1)} %constant.79.clone.outer_ref) | copy-start | bytes 1572868
  43.2 21.9 %collective-permute-start.7 = (bf16[32,1024]{1,0:T(8,128)(2,1)S(1)}, bf16[32,1024]{1,0:T(8,128)(2,1)S(1)}, u32[]{:S(2)}, u32[]{:S(2)}) collective-permute-start(bf16[32,1024]{1,0:T(8,128)(2,1)S(1)} %get-tuple-element.10), channel_id=1, source_target_pairs={{0,2},{1,3},{2,4},{3,5},{4,6},{5,7},{6,0},{7,1},{8,10},{9,11},{10,... | collective-permute-start | bytes 196616 | tf_op jit(solution)/shard_map/ppermute | solution.py:213
  43.3 21.8 %collective-permute-start.8 = (bf16[32,1024]{1,0:T(8,128)(2,1)S(1)}, bf16[32,1024]{1,0:T(8,128)(2,1)}, u32[]{:S(2)}, u32[]{:S(2)}) collective-permute-start(bf16[32,1024]{1,0:T(8,128)(2,1)S(1)} %get-tuple-element.10), channel_id=1, source_target_pairs={{0,4},{1,5},{2,6},{3,7},{4,0},{5,1},{6,2},{7,3},{8,12},{9,13},{10,... | collective-permute-start | bytes 196616 | tf_op jit(solution)/shard_map/ppermute | solution.py:213
  46.3 18.8 %collective-permute-start.9 = (bf16[32,1024]{1,0:T(8,128)(2,1)S(1)}, bf16[32,1024]{1,0:T(8,128)(2,1)}, u32[]{:S(2)}, u32[]{:S(2)}) collective-permute-start(bf16[32,1024]{1,0:T(8,128)(2,1)S(1)} %get-tuple-element.10), channel_id=1, source_target_pairs={{0,6},{1,7},{2,0},{3,1},{4,2},{5,3},{6,4},{7,5},{8,14},{9,15},{10,... | collective-permute-start | bytes 196616 | tf_op jit(solution)/shard_map/ppermute | solution.py:213
  56.9 27.6 %all-to-all-start.1 = ((bf16[256,8,128]{2,1,0:T(8,128)(2,1)}), bf16[256,8,128]{2,1,0:T(8,128)(2,1)}, u32[]{:S(2)}, u32[]{:S(2)}) async-start(bf16[256,8,128]{2,1,0:T(8,128)(2,1)} %bitcast.6), calls=%async_computation.1 | async-start | bytes 1048576 | tf_op jit(solution)/shard_map/all_to_all | solution.py:258
  66.0 12.1 %collective-permute-start.10 = (bf16[128,1024]{1,0:T(8,128)(2,1)S(1)}, bf16[128,1024]{1,0:T(8,128)(2,1)S(1)}, u32[]{:S(2)}, u32[]{:S(2)}) collective-permute-start(bf16[128,1024]{1,0:T(8,128)(2,1)S(1)} %pad_maximum_fusion.1), channel_id=1, source_target_pairs={{0,16},{8,24},{16,32},{24,40},{32,48},{40,56},{48,0},{56,8},{64,80... | collective-permute-start | bytes 786440 | tf_op jit(solution)/shard_map/ppermute | solution.py:226
  67.5 13.1 %collective-permute-start.11 = (bf16[128,1024]{1,0:T(8,128)(2,1)S(1)}, bf16[128,1024]{1,0:T(8,128)(2,1)S(1)}, u32[]{:S(2)}, u32[]{:S(2)}) collective-permute-start(bf16[128,1024]{1,0:T(8,128)(2,1)S(1)} %pad_maximum_fusion.1), channel_id=1, source_target_pairs={{0,64},{8,72},{16,80},{24,88},{32,96},{40,104},{48,112},{56,120},{... | collective-permute-start | bytes 786440 | tf_op jit(solution)/shard_map/ppermute | solution.py:226
  69.1 11.6 %collective-permute-start.12 = (bf16[128,1024]{1,0:T(8,128)(2,1)S(1)}, bf16[128,1024]{1,0:T(8,128)(2,1)S(1)}, u32[]{:S(2)}, u32[]{:S(2)}) collective-permute-start(bf16[128,1024]{1,0:T(8,128)(2,1)S(1)} %pad_maximum_fusion.1), channel_id=1, source_target_pairs={{0,48},{8,56},{16,0},{24,8},{32,16},{40,24},{48,32},{56,40},{64,11... | collective-permute-start | bytes 786440 | tf_op jit(solution)/shard_map/ppermute | solution.py:226
  71.3 1.2 copy-start.2
  75.2 1.3 copy-start.5
  80.7 20.0 %collective-permute-start.13 = (bf16[512,1024]{1,0:T(8,128)(2,1)S(1)}, bf16[512,1024]{1,0:T(8,128)(2,1)S(1)}, u32[]{:S(2)}, u32[]{:S(2)}) collective-permute-start(bf16[512,1024]{1,0:T(8,128)(2,1)S(1)} %constant_dynamic-update-slice_fusion.7.own_ref), channel_id=1, source_target_pairs={{0,1},{1,0},{2,3},{3,2},{4,5},{5,4},{6,7},{7,6},{8,9},{9,8},{10,11... | collective-permute-start | bytes 3145736 | tf_op jit(solution)/shard_map/ppermute | solution.py:217
  92.9 28.0 %all-to-all-start.3 = ((bf16[256,8,128]{2,1,0:T(8,128)(2,1)}), bf16[256,8,128]{2,1,0:T(8,128)(2,1)S(1)}, u32[]{:S(2)}, u32[]{:S(2)}) async-start(bf16[256,8,128]{2,1,0:T(8,128)(2,1)} %bitcast.25), calls=%async_computation.3 | async-start | bytes 1048576 | tf_op jit(solution)/shard_map/all_to_all | solution.py:264

commit v7 on v6

--- a/solution.py
+++ b/solution.py
@@ -54,11 +54,11 @@
     return high, (x - high.astype(F32)).astype(BF)
 
 
-def weight_rows(place_ref, part_ref, z):
+def weight_rows(place_ref, part_ref, z, group=4, first=0):
     z_back = (place_ref[1] - z + 4) % 4
     return jnp.concatenate(
         [
-            part_ref[pl.ds(pl.multiple_of(((place_ref[2] - q + 4) % 4 * 4 + z_back) * 32, 32), 32), :]
+            part_ref[pl.ds(pl.multiple_of(((place_ref[2] - q + 4) % 4 * group + first + z_back) * 32, 32), 32), :]
             for q in range(4)
         ],
         axis=0,
@@ -165,15 +165,15 @@
     out_ref[...] = wide_ref[...].astype(out_ref.dtype)
 
 
-def output_kernel(place_ref, mixed_ref, own_ref, mate_ref, out_ref, wide_ref):
+def output_kernel(place_ref, mixed_ref, w_ref, out_ref, wide_ref):
     count = out_ref.shape[0] // NB
     for j in range(count):
         wide_ref[j] = mixed_ref[pl.ds(NB * j, NB), :].astype(F32)
     rows, weights = [], []
-    for rel, part_ref in enumerate((own_ref, mate_ref)):
+    for rel in range(2):
         for z in range(count // 2):
             j = 2 * z + (place_ref[0] + rel) % 2
-            weights.append(weight_rows(place_ref, part_ref, z))
+            weights.append(weight_rows(place_ref, w_ref, z, count, rel * count // 2))
             for c in range(4):
                 rows.append(
                     jnp.concatenate(
@@ -226,12 +226,14 @@
     return lax.ppermute(x, "ctx", pairs)
 
 
-def gather_rows(rows):
-    rows = jnp.concatenate([rows, over_z(rows, 1), over_z(rows, 2), over_z(rows, -1)])
-    rows = jnp.concatenate(
+def gather_z(rows):
+    return jnp.concatenate([rows, over_z(rows, 1), over_z(rows, 2), over_z(rows, -1)])
+
+
+def gather_plane(rows):
+    return jnp.concatenate(
         [rows, over_plane(rows, 0, 1), over_plane(rows, 1, 0), over_plane(rows, 0, -1)]
     )
-    return rows, over_core(rows)
 
 
 def local(tokens, w_in, filters, w_filter, w_out):
@@ -243,27 +245,32 @@
     blocks = (ch_count, wide[0] // ch_count, wide[1])
     quarter = (ctx_place // 2 % 4 + 2 * (ctx_place // 8)) % 4
     place = jnp.stack([ch_place % 2, ch_place // 2, quarter]).astype(jnp.int32)
-    in_own, in_mate = gather_rows(lax.dynamic_slice_in_dim(w_in, 32 * quarter, 32, 1).T)
+    in_own = gather_plane(gather_z(lax.dynamic_slice_in_dim(w_in, 32 * quarter, 32, 1).T))
+    in_mate = over_core(in_own)
     tokens = lax.all_to_all(tokens, "ch", 0, 0, tiled=True)
     shaped = call(shape_kernel, wide, BF, wide, 2**25, filters, w_filter)
     shaped = lax.all_to_all(shaped, "ctx", 0, 0, tiled=True)
     spectrum = call(
         filter_kernel, (4 * NB, 2 * NB), F32, wide, 2**31, shaped, outer, inner, turn
     )
-    w_out, tokens = lax.optimization_barrier((w_out, tokens))
-    out_own, out_mate = gather_rows(lax.dynamic_slice_in_dim(w_out, 32 * quarter, 32, 0))
     signal = call(
         project_kernel, wide, BF, blocks, 2**29, place, tokens, in_own, in_mate, scalars=True
     )
+    w_out, signal = lax.optimization_barrier((w_out, signal))
+    out_rows = gather_z(lax.dynamic_slice_in_dim(w_out, 32 * quarter, 32, 0))
+    out_rows = jnp.concatenate([out_rows, over_core(out_rows)])
     signal = lax.all_to_all(signal, every, 0, 0, tiled=True)
     operands = [signal, outer_x, turn, inner, spectrum, back]
     fetched = [pltpu.VMEM(a.shape, a.dtype) for a in operands] + [pltpu.SemaphoreType.DMA((6,))]
     mixed = call(
         conv_kernel, wide, BF, wide, 2**32, *operands, fetched=fetched, limit=60 * 2**20
     )
+    out_rows, mixed = lax.optimization_barrier((out_rows, mixed))
+    w_out = gather_plane(out_rows)
     mixed = lax.all_to_all(mixed, every, 0, 0, tiled=True)
+    mixed, w_out = lax.optimization_barrier((mixed, w_out))
     result = call(
-        output_kernel, wide, BF, blocks, 2**29, place, mixed, out_own, out_mate, scalars=True
+        output_kernel, wide, BF, blocks, 2**29, place, mixed, w_out, scalars=True
     )
     return lax.all_to_all(result, "ch", 0, 0, tiled=True)
 

time: 144 us -> 152 us (1.056); the launches traced: 144 us -> 150 us
  local copies, waits for them, and re-layouts: 12.2 us -> 6.71 us
  waiting for transfers between devices: 39.4 us -> 44 us
  blocking collectives: 20.4 us -> 24.8 us
  starting transfers between devices: 52.8 us -> 55.1 us
    all_to_all x1, waiting for transfers between devices: 20.1 us -> 0.01 us  [local(): mixed = lax.all_to_all(mixed, every, 0, 0, tiled=True)]
    ppermute x6, waiting for transfers between devices: 8.89 us -> 23.1 us  [over_plane(): return lax.ppermute(x, 'ctx', pairs)]
    ppermute x6, waiting for transfers between devices: 0.14 us -> 7.31 us  [over_z(): return lax.ppermute(x, 'ch', [(n, (n + 2 * step) % 8) for n in range(8)])]
    unnamed x29 -> x31, local copies, waits for them, and re-layouts: 11.3 us -> 6.54 us
    all_to_all x1, blocking collectives: 20.4 us -> 24.8 us  [local(): return lax.all_to_all(result, 'ch', 0, 0, tiled=True)]
    all_to_all x1, waiting for transfers between devices: 4.18 us -> 7.93 us  [local(): shaped = lax.all_to_all(shaped, 'ctx', 0, 0, tiled=True)]
    all_to_all x1, waiting for transfers between devices: 3.6 us -> 0.01 us  [local(): signal = lax.all_to_all(signal, every, 0, 0, tiled=True)]
    ppermute x6, starting transfers between devices: 17.8 us -> 19.6 us  [over_z(): return lax.ppermute(x, 'ch', [(n, (n + 2 * step) % 8) for n in range(8)])]
  transfers between devices with their start and end apart: 18 -> 18, of which waited for: 9 -> 10; matrix products, arithmetic and copies ran while one was open for 6% -> 2% of each run, Pallas kernels for 11% -> 5%
where the time goes in v7:
time: 152 us; the launch traced here: 150 us
  starting transfers between devices  55.1 us (36%)
  waiting for transfers between devices  44 us (29%)
  blocking collectives  24.8 us (16%)
  Pallas kernels  17.4 us (11%)
  local copies, waits for them, and re-layouts  6.71 us (4%)
    all_to_all x1, blocking collectives, local(): return lax.all_to_all(result, 'ch', 0, 0, tiled=True)  24.8 us
    ppermute x6, waiting for transfers between devices, over_plane(): return lax.ppermute(x, 'ctx', pairs)  23.1 us
    ppermute x6, starting transfers between devices, over_z(): return lax.ppermute(x, 'ch', [(n, (n + 2 * step) % 8) for n in range(8)])  19.6 us
    pallas_call x5, Pallas kernels, call(): pl.pallas_call(kernel, out_shape=jax.ShapeDtypeStruct(shape, dtype), in_s...  17.4 us
    all_to_all x1, starting transfers between devices, local(): mixed = lax.all_to_all(mixed, every, 0, 0, tiled=True)  9.5 us
    all_to_all x1, starting transfers between devices, local(): shaped = lax.all_to_all(shaped, 'ctx', 0, 0, tiled=True)  7.99 us
    all_to_all x1, waiting for transfers between devices, local(): shaped = lax.all_to_all(shaped, 'ctx', 0, 0, tiled=True)  7.93 us
    ppermute x6, waiting for transfers between devices, over_z(): return lax.ppermute(x, 'ch', [(n, (n + 2 * step) % 8) for n in range(8)])  7.31 us
  transfers between devices with their start and end apart: 18, of which 10 were waited for; matrix products, arithmetic and copies ran while one was open for 2% of the time, Pallas kernels for 5%

profile of v7, /device:TPU:2, one launch (start us, length us, event | category | flops | bytes accessed | tf_op | source)
XLA Modules:
  0.0 149.5 jit_solution(16720304431502942485)
XLA Ops:
  1.2 6.4 %collective-permute-start.2 = (bf16[32,1024]{1,0:T(8,128)(2,1)S(1)}, bf16[32,1024]{1,0:T(8,128)(2,1)S(1)}, u32[]{:S(2)}, u32[]{:S(2)}) collective-permute-start(bf16[32,1024]{1,0:T(8,128)(2,1)S(1)} %bitcast.20), channel_id=1, source_target_pairs={{0,6},{1,7},{2,0},{3,1},{4,2},{5,3},{6,4},{7,5},{8,14},{9,15},{10,... | collective-permute-start | bytes 196616 | tf_op jit(solution)/shard_map/ppermute | solution.py:213
  7.6 1.0 collective-permute-start.1
  8.6 2.8 %collective-permute-start = (bf16[32,1024]{1,0:T(8,128)(2,1)S(1)}, bf16[32,1024]{1,0:T(8,128)(2,1)S(1)}, u32[]{:S(2)}, u32[]{:S(2)}) collective-permute-start(bf16[32,1024]{1,0:T(8,128)(2,1)S(1)} %bitcast.22), channel_id=1, source_target_pairs={{0,2},{1,3},{2,4},{3,5},{4,6},{5,7},{6,0},{7,1},{8,10},{9,11},{10,... | collective-permute-start | bytes 196616 | tf_op jit(solution)/shard_map/ppermute | solution.py:213
  11.4 4.0 %all-to-all-start = ((bf16[8,256,128]{2,1,0:T(8,128)(2,1)}), bf16[8,256,128]{2,1,0:T(8,128)(2,1)S(1)}, u32[]{:S(2)}, u32[]{:S(2)}) async-start(bf16[8,256,128]{2,1,0:T(8,128)(2,1)} %bitcast.24), calls=%async_computation | async-start | bytes 1048576 | tf_op jit(solution)/shard_map/all_to_all | solution.py:250
  15.4 1.4 collective-permute-done.1
  17.8 1.2 collective-permute-start.4
  19.1 1.5 collective-permute-start.3
  20.6 6.2 %collective-permute-done.3 = bf16[128,1024]{1,0:T(8,128)(2,1)S(1)} collective-permute-done((bf16[128,1024]{1,0:T(8,128)(2,1)S(1)}, bf16[128,1024]{1,0:T(8,128)(2,1)S(1)}, u32[]{:S(2)}, u32[]{:S(2)}) %collective-permute-start.3) | collective-permute-done | bytes 262176 | tf_op jit(solution)/shard_map/ppermute | solution.py:226
  27.4 2.0 %shard_map.101 = bf16[2048,128]{1,0:T(8,128)(2,1)} custom-call(f32[2048,24]{1,0:T(8,128)S(1)} %copy.12.filters_ref, f32[24,128]{1,0:T(8,128)S(1)} %copy-done.1), custom_call_target="tpu_custom_call" | custom-call | flops 33554432 | bytes 1257472 | tf_op jit(solution)/shard_map/pallas_call | solution.py:199
  29.3 4.1 %all-to-all-done = bf16[8,256,128]{2,1,0:T(8,128)(2,1)S(1)} async-done(((bf16[8,256,128]{2,1,0:T(8,128)(2,1)}), bf16[8,256,128]{2,1,0:T(8,128)(2,1)S(1)}, u32[]{:S(2)}, u32[]{:S(2)}) %all-to-all-start) | async-done | bytes 524320 | tf_op jit(solution)/shard_map/all_to_all | solution.py:250
  33.5 8.0 %all-to-all-start.2 = ((bf16[32,64,128]{2,1,0:T(8,128)(2,1)}), bf16[32,64,128]{2,1,0:T(8,128)(2,1)S(1)}, u32[]{:S(2)}, u32[]{:S(2)}) async-start(bf16[32,64,128]{2,1,0:T(8,128)(2,1)} %bitcast.8), calls=%async_computation.2 | async-start | bytes 1048576 | tf_op jit(solution)/shard_map/all_to_all | solution.py:252
  41.6 2.9 %shard_map.100 = bf16[2048,128]{1,0:T(8,128)(2,1)} custom-call(s32[3]{0:T(128)S(1)} %pad_add_fusion.place_ref, bf16[2048,128]{1,0:T(8,128)(2,1)S(1)} %bitcast.15, bf16[512,1024]{1,0:T(8,128)(2,1)S(1)} %constant_dynamic-update-slice_fusion.own_ref, bf16[512,1024]{1,0:T(8,128)(2,1)} %collective-permute-done.6.mate_ref), custom_call_target="tpu_custom_call" | custom-call | flops 536870912 | bytes 3670028 | tf_op jit(solution)/shard_map/pallas_call | solution.py:199
  44.5 7.9 %all-to-all-done.2 = bf16[32,64,128]{2,1,0:T(8,128)(2,1)S(1)} async-done(((bf16[32,64,128]{2,1,0:T(8,128)(2,1)}), bf16[32,64,128]{2,1,0:T(8,128)(2,1)S(1)}, u32[]{:S(2)}, u32[]{:S(2)}) %all-to-all-start.2) | async-done | bytes 524320 | tf_op jit(solution)/shard_map/all_to_all | solution.py:252
  52.4 6.5 %all-to-all-start.1 = ((bf16[256,8,128]{2,1,0:T(8,128)(2,1)}), bf16[256,8,128]{2,1,0:T(8,128)(2,1)S(1)}, u32[]{:S(2)}, u32[]{:S(2)}) async-start(bf16[256,8,128]{2,1,0:T(8,128)(2,1)} %bitcast.6), calls=%async_computation.1 | async-start | bytes 1048576 | tf_op jit(solution)/shard_map/all_to_all | solution.py:262
  59.9 5.3 %collective-permute-start.9 = (bf16[32,1024]{1,0:T(8,128)(2,1)S(1)}, bf16[32,1024]{1,0:T(8,128)(2,1)S(1)}, u32[]{:S(2)}, u32[]{:S(2)}) collective-permute-start(bf16[32,1024]{1,0:T(8,128)(2,1)S(1)} %get-tuple-element.18), channel_id=1, source_target_pairs={{0,6},{1,7},{2,0},{3,1},{4,2},{5,3},{6,4},{7,5},{8,14},{9,15},{10,... | collective-permute-start | bytes 196616 | tf_op jit(solution)/shard_map/ppermute | solution.py:213
  65.1 1.4 collective-permute-start.8
  66.5 2.8 %collective-permute-start.7 = (bf16[32,1024]{1,0:T(8,128)(2,1)S(1)}, bf16[32,1024]{1,0:T(8,128)(2,1)S(1)}, u32[]{:S(2)}, u32[]{:S(2)}) collective-permute-start(bf16[32,1024]{1,0:T(8,128)(2,1)S(1)} %get-tuple-element.18), channel_id=1, source_target_pairs={{0,2},{1,3},{2,4},{3,5},{4,6},{5,7},{6,0},{7,1},{8,10},{9,11},{10,... | collective-permute-start | bytes 196616 | tf_op jit(solution)/shard_map/ppermute | solution.py:213
  69.3 1.2 copy-done.2
  70.5 2.6 %shard_map.102.refs_4_ = f32[1024,512]{1,0:T(8,128)S(1)} custom-call(bf16[2048,128]{1,0:T(8,128)(2,1)S(1)} %bitcast.18, bf16[2,512,256]{2,1,0:T(8,128)(2,1)S(1)} %copy-done.4, bf16[2,512,512]{2,1,0:T(8,128)(2,1)S(1)} %copy-done.2, f32[2,256,256]{2,1,0:T(8,128)S(1)} %copy-done.3), custom_call_target="tpu_custom_call" | custom-call | flops 2147483648 | bytes 4718592 | tf_op jit(solution)/shard_map/pallas_call | solution.py:199
  73.2 1.3 copy-done.5
  74.5 1.2 collective-permute-done.9
  75.7 4.3 %collective-permute-done.8 = bf16[32,1024]{1,0:T(8,128)(2,1)S(1)} collective-permute-done((bf16[32,1024]{1,0:T(8,128)(2,1)S(1)}, bf16[32,1024]{1,0:T(8,128)(2,1)S(1)}, u32[]{:S(2)}, u32[]{:S(2)}) %collective-permute-start.8) | collective-permute-done | bytes 65568 | tf_op jit(solution)/shard_map/ppermute | solution.py:213
  80.5 1.5 collective-permute-done.10
  82.9 8.4 %shard_map.103 = bf16[2048,128]{1,0:T(8,128)(2,1)} custom-call(bf16[2048,128]{1,0:T(8,128)(2,1)} %bitcast.25, bf16[2,512,256]{2,1,0:T(8,128)(2,1)} %constant.82.clone.refs_1_, f32[2,256,256]{2,1,0:T(8,128)} %constant.81.clone.turn_ref.refs_2_, bf16[2,512,512]{2,1,0:T(8,128)(2,1)} %constant.80.clone.inner_ref.refs_3_, f32[1024,512]{1,0:T(8,128)} %copy-done.5, ...), custom_call_target="tpu_custom_call" | custom-call | flops 4294967296 | bytes 6291456 | tf_op jit(solution)/shard_map/pallas_call | solution.py:199
  91.3 9.5 %all-to-all-start.3 = ((bf16[256,8,128]{2,1,0:T(8,128)(2,1)}), bf16[256,8,128]{2,1,0:T(8,128)(2,1)S(1)}, u32[]{:S(2)}, u32[]{:S(2)}) async-start(bf16[256,8,128]{2,1,0:T(8,128)(2,1)} %bitcast.26), calls=%async_computation.3 | async-start | bytes 1048576 | tf_op jit(solution)/shard_map/all_to_all | solution.py:270
  100.8 2.2 %collective-permute-start.13 = (bf16[256,1024]{1,0:T(8,128)(2,1)S(1)}, bf16[256,1024]{1,0:T(8,128)(2,1)S(1)}, u32[]{:S(2)}, u32[]{:S(2)}) collective-permute-start(bf16[256,1024]{1,0:T(8,128)(2,1)S(1)} %constant_dynamic-update-slice_fusion.7), channel_id=1, source_target_pairs={{0,48},{8,56},{16,0},{24,8},{32,16},{40,24},{48,32},{56,40},{64,11... | collective-permute-start | bytes 1572872 | tf_op jit(solution)/shard_map/ppermute | solution.py:226
  103.1 1.3 collective-permute-start.11
  104.4 15.5 %collective-permute-done.13 = bf16[256,1024]{1,0:T(8,128)(2,1)S(1)} collective-permute-done((bf16[256,1024]{1,0:T(8,128)(2,1)S(1)}, bf16[256,1024]{1,0:T(8,128)(2,1)S(1)}, u32[]{:S(2)}, u32[]{:S(2)}) %collective-permute-start.13) | collective-permute-done | bytes 524320 | tf_op jit(solution)/shard_map/ppermute | solution.py:226
  119.9 1.4 collective-permute-done.12
  121.3 1.2 pad_maximum_fusion.w_ref
  122.5 1.4 shard_map.104
  123.9 24.8 %all_to_all.57 = bf16[8,256,128]{2,1,0:T(8,128)(2,1)S(1)} all-to-all(bf16[8,256,128]{2,1,0:T(8,128)(2,1)S(1)} %bitcast.17), channel_id=1, replica_groups=mesh['ctx'=32,'ch'=8] {'ch'}, dimensions={0} | all-to-all | bytes 1048576 | tf_op jit(solution)/shard_map/all_to_all | solution.py:275
  (48 shorter events, 5.7 us)
Async XLA Ops:
  0.0 1.0 copy-start
  1.1 25.9 %copy-start.8 = (f32[2048,24]{0,1:T(8,128)S(1)}, f32[2048,24]{0,1:T(8,128)}, u32[]{:S(2)}) copy-start(f32[2048,24]{0,1:T(8,128)} %param.12) | copy-start | bytes 589828
  1.2 14.2 %collective-permute-start.2 = (bf16[32,1024]{1,0:T(8,128)(2,1)S(1)}, bf16[32,1024]{1,0:T(8,128)(2,1)S(1)}, u32[]{:S(2)}, u32[]{:S(2)}) collective-permute-start(bf16[32,1024]{1,0:T(8,128)(2,1)S(1)} %bitcast.20), channel_id=1, source_target_pairs={{0,6},{1,7},{2,0},{3,1},{4,2},{5,3},{6,4},{7,5},{8,14},{9,15},{10,... | collective-permute-start | bytes 196616 | tf_op jit(solution)/shard_map/ppermute | solution.py:213
  7.6 9.3 %collective-permute-start.1 = (bf16[32,1024]{1,0:T(8,128)(2,1)S(1)}, bf16[32,1024]{1,0:T(8,128)(2,1)S(1)}, u32[]{:S(2)}, u32[]{:S(2)}) collective-permute-start(bf16[32,1024]{1,0:T(8,128)(2,1)S(1)} %bitcast.21), channel_id=1, source_target_pairs={{0,4},{1,5},{2,6},{3,7},{4,0},{5,1},{6,2},{7,3},{8,12},{9,13},{10,... | collective-permute-start | bytes 196616 | tf_op jit(solution)/shard_map/ppermute | solution.py:213
  8.6 8.3 %collective-permute-start = (bf16[32,1024]{1,0:T(8,128)(2,1)S(1)}, bf16[32,1024]{1,0:T(8,128)(2,1)S(1)}, u32[]{:S(2)}, u32[]{:S(2)}) collective-permute-start(bf16[32,1024]{1,0:T(8,128)(2,1)S(1)} %bitcast.22), channel_id=1, source_target_pairs={{0,2},{1,3},{2,4},{3,5},{4,6},{5,7},{6,0},{7,1},{8,10},{9,11},{10,... | collective-permute-start | bytes 196616 | tf_op jit(solution)/shard_map/ppermute | solution.py:213
  11.4 22.1 %all-to-all-start = ((bf16[8,256,128]{2,1,0:T(8,128)(2,1)}), bf16[8,256,128]{2,1,0:T(8,128)(2,1)S(1)}, u32[]{:S(2)}, u32[]{:S(2)}) async-start(bf16[8,256,128]{2,1,0:T(8,128)(2,1)} %bitcast.24), calls=%async_computation | async-start | bytes 1048576 | tf_op jit(solution)/shard_map/all_to_all | solution.py:250
  15.4 12.0 %copy-start.1 = (f32[24,128]{1,0:T(8,128)S(1)}, f32[24,128]{1,0:T(8,128)}, u32[]{:S(2)}) copy-start(f32[24,128]{1,0:T(8,128)} %w_ref.1) | copy-start | bytes 36868
  16.9 10.0 %collective-permute-start.5 = (bf16[128,1024]{1,0:T(8,128)(2,1)S(1)}, bf16[128,1024]{1,0:T(8,128)(2,1)S(1)}, u32[]{:S(2)}, u32[]{:S(2)}) collective-permute-start(bf16[128,1024]{1,0:T(8,128)(2,1)S(1)} %pad_maximum_fusion.1), channel_id=1, source_target_pairs={{0,48},{8,56},{16,0},{24,8},{32,16},{40,24},{48,32},{56,40},{64,11... | collective-permute-start | bytes 786440 | tf_op jit(solution)/shard_map/ppermute | solution.py:226
  17.8 9.0 %collective-permute-start.4 = (bf16[128,1024]{1,0:T(8,128)(2,1)S(1)}, bf16[128,1024]{1,0:T(8,128)(2,1)S(1)}, u32[]{:S(2)}, u32[]{:S(2)}) collective-permute-start(bf16[128,1024]{1,0:T(8,128)(2,1)S(1)} %pad_maximum_fusion.1), channel_id=1, source_target_pairs={{0,64},{8,72},{16,80},{24,88},{32,96},{40,104},{48,112},{56,120},{... | collective-permute-start | bytes 786440 | tf_op jit(solution)/shard_map/ppermute | solution.py:226
  19.1 7.7 %collective-permute-start.3 = (bf16[128,1024]{1,0:T(8,128)(2,1)S(1)}, bf16[128,1024]{1,0:T(8,128)(2,1)S(1)}, u32[]{:S(2)}, u32[]{:S(2)}) collective-permute-start(bf16[128,1024]{1,0:T(8,128)(2,1)S(1)} %pad_maximum_fusion.1), channel_id=1, source_target_pairs={{0,16},{8,24},{16,32},{24,40},{32,48},{40,56},{48,0},{56,8},{64,80... | collective-permute-start | bytes 786440 | tf_op jit(solution)/shard_map/ppermute | solution.py:226
  26.9 14.7 %collective-permute-start.6 = (bf16[512,1024]{1,0:T(8,128)(2,1)S(1)}, bf16[512,1024]{1,0:T(8,128)(2,1)}, u32[]{:S(2)}, u32[]{:S(2)}) collective-permute-start(bf16[512,1024]{1,0:T(8,128)(2,1)S(1)} %constant_dynamic-update-slice_fusion.own_ref), channel_id=1, source_target_pairs={{0,1},{1,0},{2,3},{3,2},{4,5},{5,4},{6,7},{7,6},{8,9},{9,8},{10,11... | collective-permute-start | bytes 3145736 | tf_op jit(solution)/shard_map/ppermute | solution.py:217
  33.5 19.0 %all-to-all-start.2 = ((bf16[32,64,128]{2,1,0:T(8,128)(2,1)}), bf16[32,64,128]{2,1,0:T(8,128)(2,1)S(1)}, u32[]{:S(2)}, u32[]{:S(2)}) async-start(bf16[32,64,128]{2,1,0:T(8,128)(2,1)} %bitcast.8), calls=%async_computation.2 | async-start | bytes 1048576 | tf_op jit(solution)/shard_map/all_to_all | solution.py:252
  41.6 27.7 %copy-start.3 = (f32[2,256,256]{2,1,0:T(8,128)S(1)}, f32[2,256,256]{2,1,0:T(8,128)}, u32[]{:S(2)}) copy-start(f32[2,256,256]{2,1,0:T(8,128)} %constant.81.clone.turn_ref.refs_2_) | copy-start | bytes 1572868
  41.6 27.7 %copy-start.4 = (bf16[2,512,256]{2,1,0:T(8,128)(2,1)S(1)}, bf16[2,512,256]{2,1,0:T(8,128)(2,1)}, u32[]{:S(2)}) copy-start(bf16[2,512,256]{2,1,0:T(8,128)(2,1)} %constant.79.clone.outer_ref) | copy-start | bytes 1572868
  52.4 29.6 %all-to-all-start.1 = ((bf16[256,8,128]{2,1,0:T(8,128)(2,1)}), bf16[256,8,128]{2,1,0:T(8,128)(2,1)S(1)}, u32[]{:S(2)}, u32[]{:S(2)}) async-start(bf16[256,8,128]{2,1,0:T(8,128)(2,1)} %bitcast.6), calls=%async_computation.1 | async-start | bytes 1048576 | tf_op jit(solution)/shard_map/all_to_all | solution.py:262
  59.9 15.9 %collective-permute-start.9 = (bf16[32,1024]{1,0:T(8,128)(2,1)S(1)}, bf16[32,1024]{1,0:T(8,128)(2,1)S(1)}, u32[]{:S(2)}, u32[]{:S(2)}) collective-permute-start(bf16[32,1024]{1,0:T(8,128)(2,1)S(1)} %get-tuple-element.18), channel_id=1, source_target_pairs={{0,6},{1,7},{2,0},{3,1},{4,2},{5,3},{6,4},{7,5},{8,14},{9,15},{10,... | collective-permute-start | bytes 196616 | tf_op jit(solution)/shard_map/ppermute | solution.py:213
  65.1 14.9 %collective-permute-start.8 = (bf16[32,1024]{1,0:T(8,128)(2,1)S(1)}, bf16[32,1024]{1,0:T(8,128)(2,1)S(1)}, u32[]{:S(2)}, u32[]{:S(2)}) collective-permute-start(bf16[32,1024]{1,0:T(8,128)(2,1)S(1)} %get-tuple-element.18), channel_id=1, source_target_pairs={{0,4},{1,5},{2,6},{3,7},{4,0},{5,1},{6,2},{7,3},{8,12},{9,13},{10,... | collective-permute-start | bytes 196616 | tf_op jit(solution)/shard_map/ppermute | solution.py:213
  66.5 13.9 %collective-permute-start.7 = (bf16[32,1024]{1,0:T(8,128)(2,1)S(1)}, bf16[32,1024]{1,0:T(8,128)(2,1)S(1)}, u32[]{:S(2)}, u32[]{:S(2)}) collective-permute-start(bf16[32,1024]{1,0:T(8,128)(2,1)S(1)} %get-tuple-element.18), channel_id=1, source_target_pairs={{0,2},{1,3},{2,4},{3,5},{4,6},{5,7},{6,0},{7,1},{8,10},{9,11},{10,... | collective-permute-start | bytes 196616 | tf_op jit(solution)/shard_map/ppermute | solution.py:213
  69.3 1.2 copy-start.2
  73.2 1.3 copy-start.5
  80.4 1.6 %collective-permute-start.10 = (bf16[128,1024]{1,0:T(8,128)(2,1)S(1)}, bf16[128,1024]{1,0:T(8,128)(2,1)S(1)}, u32[]{:S(2)}, u32[]{:S(2)}) collective-permute-start(bf16[128,1024]{1,0:T(8,128)(2,1)S(1)} %pad_maximum_fusion.2), channel_id=1, source_target_pairs={{0,1},{1,0},{2,3},{3,2},{4,5},{5,4},{6,7},{7,6},{8,9},{9,8},{10,11... | collective-permute-start | bytes 786440 | tf_op jit(solution)/shard_map/ppermute | solution.py:217
  82.0 21.0 %copy-start.6 = (bf16[256,1024]{1,0:T(8,128)(2,1)}, bf16[256,1024]{1,0:T(8,128)(2,1)S(1)}, u32[]{:S(2)}) copy-start(bf16[256,1024]{1,0:T(8,128)(2,1)S(1)} %constant_dynamic-update-slice_fusion.7) | copy-start | bytes 1572868
  82.0 0.8 copy-start.7
  91.3 31.2 %all-to-all-start.3 = ((bf16[256,8,128]{2,1,0:T(8,128)(2,1)}), bf16[256,8,128]{2,1,0:T(8,128)(2,1)S(1)}, u32[]{:S(2)}, u32[]{:S(2)}) async-start(bf16[256,8,128]{2,1,0:T(8,128)(2,1)} %bitcast.26), calls=%async_computation.3 | async-start | bytes 1048576 | tf_op jit(solution)/shard_map/all_to_all | solution.py:270
  100.8 19.1 %collective-permute-start.13 = (bf16[256,1024]{1,0:T(8,128)(2,1)S(1)}, bf16[256,1024]{1,0:T(8,128)(2,1)S(1)}, u32[]{:S(2)}, u32[]{:S(2)}) collective-permute-start(bf16[256,1024]{1,0:T(8,128)(2,1)S(1)} %constant_dynamic-update-slice_fusion.7), channel_id=1, source_target_pairs={{0,48},{8,56},{16,0},{24,8},{32,16},{40,24},{48,32},{56,40},{64,11... | collective-permute-start | bytes 1572872 | tf_op jit(solution)/shard_map/ppermute | solution.py:226
  103.1 18.2 %collective-permute-start.12 = (bf16[256,1024]{1,0:T(8,128)(2,1)S(1)}, bf16[256,1024]{1,0:T(8,128)(2,1)S(1)}, u32[]{:S(2)}, u32[]{:S(2)}) collective-permute-start(bf16[256,1024]{1,0:T(8,128)(2,1)S(1)} %constant_dynamic-update-slice_fusion.7), channel_id=1, source_target_pairs={{0,64},{8,72},{16,80},{24,88},{32,96},{40,104},{48,112},{56,120},{... | collective-permute-start | bytes 1572872 | tf_op jit(solution)/shard_map/ppermute | solution.py:226
  103.1 18.2 %collective-permute-start.11 = (bf16[256,1024]{1,0:T(8,128)(2,1)S(1)}, bf16[256,1024]{1,0:T(8,128)(2,1)S(1)}, u32[]{:S(2)}, u32[]{:S(2)}) collective-permute-start(bf16[256,1024]{1,0:T(8,128)(2,1)S(1)} %constant_dynamic-update-slice_fusion.7), channel_id=1, source_target_pairs={{0,16},{8,24},{16,32},{24,40},{32,48},{40,56},{48,0},{56,8},{64,80... | collective-permute-start | bytes 1572872 | tf_op jit(solution)/shard_map/ppermute | solution.py:226
